TPU v7x, 32 devices: a whole 2x2x4 slice. The times are simulated.
32 devices in a mesh: section: 2 (over core), dp: 16 (over z, y, x).
Axes of the slice: x: 2, y: 2, z: 4, core: 2. Of those that a mesh axis runs over, the one named last changes fastest.
Arguments:
- byte_codes: int32 [2, 32, 128], P('section', 'dp'), may hold values from 0 to 383
- encoder_segments: int32 [32, 128], P('dp'), may hold values from 0 to 2, never falling along the last dimension, each value on 1 to 64 neighbouring positions
- target_segments: int32 [32, 128], P('dp'), may hold values from 0 to 2, never falling along the last dimension, each value on 1 to 64 neighbouring positions
- embedding: bfloat16 [384, 1472], replicated, may hold values from -6 to 6
- attention_in: bfloat16 [2, 1472, 1152], P('section', None, 'dp'), may hold values from -0.15625 to 0.15625
- attention_out: bfloat16 [2, 384, 1472], P('section', 'dp'), may hold values from -0.875 to 0.875
- widen_weight: bfloat16 [2, 1472, 7168], P('section', None, 'dp'), may hold values from -0.15625 to 0.15625
- narrow_weight: bfloat16 [2, 3584, 1472], P('section', 'dp'), may hold values from -0.09375 to 0.09375
- cross_first: bfloat16 [2, 1472, 384], P('section', None, 'dp'), may hold values from -0.15625 to 0.15625
- cross_second: bfloat16 [2, 1472, 384], P('section', None, 'dp'), may hold values from -0.4375 to 0.4375
- norm_gains: bfloat16 [2, 3, 1472], P('section'), may hold values from 0.5 to 1.5
- cotangent: bfloat16 [2, 32, 128, 1472], P('section', 'dp'), may hold values from -6 to 6
Outputs:
- block_outputs: bfloat16 [2, 32, 128, 1472], P('section', 'dp')
- embedding_grad: float32 [384, 1472], replicated
- attention_in_grad: float32 [2, 1472, 1152], P('section', None, 'dp')
- attention_out_grad: float32 [2, 384, 1472], P('section', 'dp')
- widen_grad: float32 [2, 1472, 7168], P('section', None, 'dp')
- narrow_grad: float32 [2, 3584, 1472], P('section', 'dp')
- cross_first_grad: float32 [2, 1472, 384], P('section', None, 'dp')
- cross_second_grad: float32 [2, 1472, 384], P('section', None, 'dp')
- norm_gains_grad: float32 [2, 3, 1472], P('section')
Inputs may be any that keep to these rules, and one draw needn't show every extreme that they name: `encoder_segments`: non-decreasing along each row; every number from 0 to 2 occurs in each row, at most 128 // 2 times. `target_segments`: non-decreasing along each row; every number from 0 to 2 occurs in each row, at most 128 // 2 times.
All inputs are finite; a program needn't handle non-finite values.
Results may differ from a plain program's by a relative error of at most 0.023.
Values may be sent and summed in bfloat16 or wider, within the bound.
No kernel may reach another device: no remote copies, remote signals or barrier semaphores. Data moves between devices by JAX's collectives and lax.ppermute only.
A program may use at most 512 MiB of HBM per device.

v0:
```python
import jax
import jax.numpy as jnp
from jax import lax
from jax.sharding import PartitionSpec as P

HEADS = 6
HEAD_DIM = 64


epsilon = 1e-06
masked_value = -1000000000.0
precise = lax.Precision.HIGHEST


def as_sent(x):

    def short(part):
        return part.astype(jnp.bfloat16) if part.dtype == jnp.float32 else part

    return jax.tree.map(short, x)


def shifted(block, axis, distance):
    devices = range(lax.axis_size(axis))
    route = [(i - distance, i) for i in devices if i - distance in devices]
    return lax.ppermute(block, axis, route)


def rms_norm(inputs, gain_row):
    return inputs * lax.rsqrt(jnp.mean(inputs * inputs, -1, keepdims=True) + epsilon) * gain_row


def rms_back(inputs, gain_row, upstream):
    _, pull_back = jax.vjp(rms_norm, inputs, gain_row)
    return pull_back(upstream)


def gated_value(gate_part, up_part):
    return jax.nn.gelu(gate_part, approximate=True) * up_part


def product(first_factor, second_factor):
    return jnp.dot(first_factor, second_factor, preferred_element_type=jnp.float32)


def product_left(first_factor, second_factor):
    return lax.dot_general(
        first_factor, second_factor, (((0,), (0,)), ((), ())), preferred_element_type=jnp.float32
    )


def product_right(first_factor, second_factor):
    return lax.dot_general(
        first_factor, second_factor, (((1,), (1,)), ((), ())), preferred_element_type=jnp.float32
    )


def split_heads(matrix):
    return matrix.reshape(matrix.shape[0], HEADS, HEAD_DIM)


def one_hot_rows(byte_row, vocabulary):
    return (
        byte_row[:, None] == lax.broadcasted_iota(jnp.int32, (byte_row.shape[0], vocabulary), 1)
    ).astype(jnp.bfloat16)


def table_product(one_hot, stream):
    return lax.dot_general(
        one_hot.astype(jnp.float32),
        stream,
        (((0,), (0,)), ((), ())),
        precision=precise,
        preferred_element_type=jnp.float32,
    )


def score_table(queries, key_rows, allowed):
    raw_scores = jnp.einsum(
        "qhd,khd->hqk",
        split_heads(queries),
        split_heads(key_rows),
        preferred_element_type=jnp.float32,
    )
    return jnp.where(allowed[None], raw_scores * HEAD_DIM ** (-0.5), masked_value)


def attend(queries, key_rows, value_rows, allowed):
    scores = score_table(queries, key_rows, allowed)
    top_score = jnp.max(scores, -1, keepdims=True)
    exponent = jnp.exp(scores - top_score)
    totals = jnp.sum(exponent, -1, keepdims=True)
    attend_weights = (exponent / totals).astype(jnp.bfloat16)
    context = jnp.einsum(
        "hqk,khd->qhd", attend_weights, split_heads(value_rows), preferred_element_type=jnp.float32
    )
    context = context.reshape(queries.shape[0], queries.shape[1]).astype(jnp.bfloat16)
    return (context, (top_score + jnp.log(totals))[..., 0])


def attend_back(queries, key_rows, value_rows, allowed, log_total, context_grad):
    scores = score_table(queries, key_rows, allowed)
    chances = jnp.exp(scores - log_total[..., None])
    attend_weights = chances.astype(jnp.bfloat16)
    grad_heads = split_heads(context_grad)
    weight_grad = jnp.einsum(
        "qhd,khd->hqk", grad_heads, split_heads(value_rows), preferred_element_type=jnp.float32
    )
    value_grad = jnp.einsum(
        "hqk,qhd->khd", attend_weights, grad_heads, preferred_element_type=jnp.float32
    )
    score_grad = (
        chances * (weight_grad - jnp.sum(weight_grad * chances, -1, keepdims=True))
    ).astype(jnp.bfloat16)
    query_grad = jnp.einsum(
        "hqk,khd->qhd", score_grad, split_heads(key_rows), preferred_element_type=jnp.float32
    ) * HEAD_DIM ** (-0.5)
    key_grad = jnp.einsum(
        "hqk,qhd->khd", score_grad, split_heads(queries), preferred_element_type=jnp.float32
    ) * HEAD_DIM ** (-0.5)
    inner_width = queries.shape[1]
    return (
        query_grad.reshape(-1, inner_width),
        key_grad.reshape(-1, inner_width),
        value_grad.reshape(-1, inner_width),
    )


def self_forward(inputs, gain_row, in_weight, out_weight, allowed):
    normed = rms_norm(inputs, gain_row).astype(jnp.bfloat16)
    projected = product(normed, in_weight).astype(jnp.bfloat16)
    inner_width = out_weight.shape[0]
    context, log_total = attend(
        projected[:, :inner_width],
        projected[:, inner_width : 2 * inner_width],
        projected[:, 2 * inner_width :],
        allowed,
    )
    return (projected, log_total, context, inputs + product(context, out_weight))


def self_back(
    inputs, gain_row, in_weight, out_weight, allowed, projected, log_total, context, stream
):
    branch_grad = stream.astype(jnp.bfloat16)
    out_grad = product_left(context, branch_grad)
    context_grad = product_right(branch_grad, out_weight).astype(jnp.bfloat16)
    inner_width = out_weight.shape[0]
    query_grad, key_grad, value_grad = attend_back(
        projected[:, :inner_width],
        projected[:, inner_width : 2 * inner_width],
        projected[:, 2 * inner_width :],
        allowed,
        log_total,
        context_grad,
    )
    projected_grad = jnp.concatenate([query_grad, key_grad, value_grad], 1).astype(jnp.bfloat16)
    normed = rms_norm(inputs, gain_row).astype(jnp.bfloat16)
    in_grad = product_left(normed, projected_grad)
    input_grad, gain_grad = rms_back(inputs, gain_row, product_right(projected_grad, in_weight))
    return (in_grad, out_grad, stream + input_grad, gain_grad)


def feed_parts(normed, widen):
    gate_up = product(normed, widen)
    half_width = gate_up.shape[1] // 2
    return (
        gate_up,
        gated_value(gate_up[:, :half_width], gate_up[:, half_width:]).astype(jnp.bfloat16),
    )


def feed_back(normed, gate_up, hidden, widen, narrow, stream):
    output_grad = stream.astype(jnp.bfloat16)
    narrow_grad = product_left(hidden, output_grad)
    hidden_grad = product_right(output_grad, narrow)
    half_width = gate_up.shape[1] // 2
    _, pull_back = jax.vjp(gated_value, gate_up[:, :half_width], gate_up[:, half_width:])
    gate_grad, up_grad = pull_back(hidden_grad)
    parts_grad = jnp.concatenate([gate_grad, up_grad], 1).astype(jnp.bfloat16)
    widen_grad = product_left(normed, parts_grad)
    return (widen_grad, narrow_grad, product_right(parts_grad, widen))


def blank_state(length, model_width, inner_width):
    kept_state = (
        jnp.zeros((length, model_width), jnp.float32),
        jnp.zeros((length, model_width), jnp.float32),
        jnp.zeros((length, model_width), jnp.float32),
        jnp.zeros((length, 3 * inner_width), jnp.bfloat16),
        jnp.zeros((HEADS, length), jnp.float32),
        jnp.zeros((length, inner_width), jnp.bfloat16),
    )
    return kept_state


def zero_grads(weights, gain_rows, embedding):
    blanks = tuple((jnp.zeros(matrix.shape, jnp.float32) for matrix in weights))
    return blanks + (
        jnp.zeros(gain_rows.shape, jnp.float32),
        jnp.zeros(embedding.shape, jnp.float32),
    )


def encoder_forward(byte_row, segments, weights, gain_rows, embedding):
    in_weight, out_weight, widen, narrow, first_cross, second_cross = weights
    inputs = product(one_hot_rows(byte_row, embedding.shape[0]), embedding)
    allowed = segments[:, None] == segments[None, :]
    projected, log_total, context, first_sum = self_forward(
        inputs, gain_rows[0], in_weight, out_weight, allowed
    )
    gate_up, hidden = feed_parts(rms_norm(first_sum, gain_rows[1]).astype(jnp.bfloat16), widen)
    second_sum = first_sum + product(hidden, narrow)
    normed_final = rms_norm(second_sum, gain_rows[2]).astype(jnp.bfloat16)
    states = jnp.concatenate(
        [product(normed_final, first_cross), product(normed_final, second_cross)], 1
    ).astype(jnp.bfloat16)
    kept_state = (inputs, first_sum, second_sum, projected, log_total, context)
    return (states, second_sum.astype(jnp.bfloat16), kept_state)


def encoder_backward(
    byte_row, segments, weights, gain_rows, embedding, kept_state, state_grads, cotangent_rows
):
    in_weight, out_weight, widen, narrow, first_cross, second_cross = weights
    inputs, first_sum, second_sum, projected, log_total, context = kept_state[:6]
    inner_width = out_weight.shape[0]
    key_grads = state_grads[:, :inner_width]
    value_grads = state_grads[:, inner_width:]
    normed_final = rms_norm(second_sum, gain_rows[2]).astype(jnp.bfloat16)
    first_cross_grad = product_left(normed_final, key_grads)
    second_cross_grad = product_left(normed_final, value_grads)
    final_grad = product_right(key_grads, first_cross) + product_right(value_grads, second_cross)
    input_grad, gain_two = rms_back(second_sum, gain_rows[2], final_grad)
    stream = cotangent_rows + input_grad
    normed_middle = rms_norm(first_sum, gain_rows[1]).astype(jnp.bfloat16)
    gate_up, hidden = feed_parts(normed_middle, widen)
    widen_grad, narrow_grad, middle_grad = feed_back(
        normed_middle, gate_up, hidden, widen, narrow, stream
    )
    input_grad, gain_one = rms_back(first_sum, gain_rows[1], middle_grad)
    stream = stream + input_grad
    allowed = segments[:, None] == segments[None, :]
    in_grad, out_grad, stream, gain_zero = self_back(
        inputs, gain_rows[0], in_weight, out_weight, allowed, projected, log_total, context, stream
    )
    table_grad = table_product(one_hot_rows(byte_row, embedding.shape[0]), stream)
    return (
        in_grad,
        out_grad,
        widen_grad,
        narrow_grad,
        first_cross_grad,
        second_cross_grad,
        jnp.stack([gain_zero, gain_one, gain_two]),
        table_grad,
    )


def decoder_step(
    byte_row, segments, encoder_seg, weights, gain_rows, embedding, states, cotangent_rows
):
    in_weight, out_weight, widen, narrow, first_cross, second_cross = weights
    inner_width = out_weight.shape[0]
    one_hot = one_hot_rows(byte_row, embedding.shape[0])
    inputs = product(one_hot, embedding)
    length = segments.shape[0]
    positions = lax.broadcasted_iota(jnp.int32, (length, length), 0)
    earlier_keys = lax.broadcasted_iota(jnp.int32, (length, length), 1)
    allowed = (segments[:, None] == segments[None, :]) & (earlier_keys <= positions)
    projected, log_total, context, first_sum = self_forward(
        inputs, gain_rows[0], in_weight, out_weight, allowed
    )
    normed_cross = rms_norm(first_sum, gain_rows[1]).astype(jnp.bfloat16)
    cross_queries = product(normed_cross, first_cross).astype(jnp.bfloat16)
    cross_allowed = segments[:, None] == encoder_seg[None, :]
    cross_context, cross_total = attend(
        cross_queries, states[:, :inner_width], states[:, inner_width:], cross_allowed
    )
    second_sum = first_sum + product_right(cross_context, second_cross)
    normed_last = rms_norm(second_sum, gain_rows[2]).astype(jnp.bfloat16)
    gate_up, hidden = feed_parts(normed_last, widen)
    outputs = second_sum + product(hidden, narrow)
    stream = cotangent_rows
    widen_grad, narrow_grad, last_grad = feed_back(
        normed_last, gate_up, hidden, widen, narrow, stream
    )
    input_grad, gain_two = rms_back(second_sum, gain_rows[2], last_grad)
    stream = stream + input_grad
    cross_branch = stream.astype(jnp.bfloat16)
    second_cross_grad = product_left(cross_branch, cross_context)
    cross_context_grad = product(cross_branch, second_cross).astype(jnp.bfloat16)
    query_grad, key_grad, value_grad = attend_back(
        cross_queries,
        states[:, :inner_width],
        states[:, inner_width:],
        cross_allowed,
        cross_total,
        cross_context_grad,
    )
    state_grads = jnp.concatenate([key_grad, value_grad], 1).astype(jnp.bfloat16)
    query_rounded = query_grad.astype(jnp.bfloat16)
    first_cross_grad = product_left(normed_cross, query_rounded)
    input_grad, gain_one = rms_back(
        first_sum, gain_rows[1], product_right(query_rounded, first_cross)
    )
    stream = stream + input_grad
    in_grad, out_grad, stream, gain_zero = self_back(
        inputs, gain_rows[0], in_weight, out_weight, allowed, projected, log_total, context, stream
    )
    table_grad = table_product(one_hot, stream)
    gradients = (
        in_grad,
        out_grad,
        widen_grad,
        narrow_grad,
        first_cross_grad,
        second_cross_grad,
        jnp.stack([gain_zero, gain_one, gain_two]),
        table_grad,
    )
    return (state_grads, outputs.astype(jnp.bfloat16), gradients)


def send_states(states):
    return jax.tree.map(
        lambda part, own: part.astype(own.dtype), shifted(as_sent(states), "section", 1), states
    )


def send_back(state_grads):
    return jax.tree.map(
        lambda part, own: part.astype(own.dtype),
        shifted(as_sent(state_grads), "section", -1),
        state_grads,
    )


def add_tuples(first_tuple, second_tuple):
    return tuple(
        (left_part + right_part for left_part, right_part in zip(first_tuple, second_tuple))
    )


def pack_rows(matrix, split_dim, pieces):
    if split_dim == 0:
        return matrix.reshape(pieces, -1)
    row_count, column_count = matrix.shape
    return (
        matrix.reshape(row_count, pieces, column_count // pieces)
        .transpose(1, 0, 2)
        .reshape(pieces, -1)
    )


def unpack_rows(packed, split_dim, full_shape, pieces):
    if split_dim == 0:
        return packed.reshape(full_shape[0] // pieces, full_shape[1])
    return packed.reshape(full_shape[0], full_shape[1] // pieces)


def per_device(
    byte_codes,
    encoder_segments,
    target_segments,
    embedding,
    attention_in,
    attention_out,
    widen_weight,
    narrow_weight,
    cross_first,
    cross_second,
    norm_gains,
    cotangent,
):
    section_index = lax.axis_index("section")
    is_encoder = section_index == 0
    gathered = (
        lax.all_gather(attention_in, "dp", axis=2, tiled=True),
        lax.all_gather(attention_out, "dp", axis=1, tiled=True),
        lax.all_gather(widen_weight, "dp", axis=2, tiled=True),
        lax.all_gather(narrow_weight, "dp", axis=1, tiled=True),
        lax.all_gather(cross_first, "dp", axis=2, tiled=True),
        lax.all_gather(cross_second, "dp", axis=2, tiled=True),
    )
    weights = tuple((gathered_piece[0] for gathered_piece in gathered))
    gain_rows = norm_gains[0].astype(jnp.float32)
    byte_rows = byte_codes[0]
    micro_count = byte_rows.shape[0]
    length = byte_rows.shape[1]
    model_width = embedding.shape[1]
    inner_width = weights[1].shape[0]
    state_blank = jnp.zeros((length, 2 * inner_width), jnp.bfloat16)
    row_blank = jnp.zeros((length, model_width), jnp.bfloat16)
    received_states = []
    received_grads = []
    kept_states = []
    encoder_rows = []
    target_rows = []
    totals = zero_grads(weights, gain_rows, embedding)
    for tick_index in range(micro_count + 2):
        forward_now = tick_index < micro_count
        backward_now = tick_index >= 2
        target_now = 1 <= tick_index <= micro_count

        def encoder_work():
            packet = {}
            if forward_now:
                states, row_values, kept_state = encoder_forward(
                    byte_rows[tick_index],
                    encoder_segments[tick_index],
                    weights,
                    gain_rows,
                    embedding,
                )
                packet["states"] = states
                packet["encoder_rows"] = row_values
                packet["kept"] = kept_state
            if target_now:
                packet["state_grads"] = state_blank
                packet["target_rows"] = row_blank
            if backward_now:
                earlier = tick_index - 2
                packet["gradients"] = add_tuples(
                    totals,
                    encoder_backward(
                        byte_rows[earlier],
                        encoder_segments[earlier],
                        weights,
                        gain_rows,
                        embedding,
                        kept_states[earlier],
                        received_grads[earlier],
                        cotangent[0, earlier].astype(jnp.float32),
                    ),
                )
            elif target_now:
                packet["gradients"] = totals
            return packet

        def target_work():
            packet = {}
            if forward_now:
                packet["states"] = state_blank
                packet["encoder_rows"] = row_blank
                packet["kept"] = blank_state(length, model_width, inner_width)
            if target_now:
                earlier = tick_index - 1
                state_grads, row_values, gradients = decoder_step(
                    byte_rows[earlier],
                    target_segments[earlier],
                    encoder_segments[earlier],
                    weights,
                    gain_rows,
                    embedding,
                    received_states[earlier],
                    cotangent[0, earlier].astype(jnp.float32),
                )
                packet["state_grads"] = state_grads
                packet["target_rows"] = row_values
                packet["gradients"] = add_tuples(totals, gradients)
            elif backward_now:
                packet["gradients"] = totals
            return packet

        packet = lax.cond(is_encoder, encoder_work, target_work)
        if forward_now:
            kept_states.append(packet["kept"])
            encoder_rows.append(packet["encoder_rows"])
            received_states.append(send_states(packet["states"]))
        if target_now:
            target_rows.append(packet["target_rows"])
            received_grads.append(send_back(packet["state_grads"]))
        if "gradients" in packet:
            totals = packet["gradients"]
    stacked_rows = jnp.where(is_encoder, jnp.stack(encoder_rows), jnp.stack(target_rows))[None]
    pieces = lax.axis_size("dp")
    split_dims = (1, 0, 1, 0, 1, 1)
    packed = jnp.concatenate(
        [pack_rows(totals[number], split_dims[number], pieces) for number in range(6)], 1
    )
    summed = lax.psum_scatter(packed, "dp", scatter_dimension=0, tiled=True)
    shard_list = []
    offset = 0
    for number in range(6):
        width_here = totals[number].size // pieces
        shard_list.append(
            unpack_rows(
                summed[:, offset : offset + width_here],
                split_dims[number],
                totals[number].shape,
                pieces,
            )
        )
        offset = offset + width_here
    weight_shards = tuple(shard_list)
    small_terms = totals[6:]
    slot_index = lax.broadcasted_iota(jnp.int32, (lax.axis_size("section"), 1, 1), 0)
    gain_slots = jnp.where(slot_index == section_index, small_terms[0][None], 0.0)
    summed_gains, embedding_grad = lax.psum((gain_slots, small_terms[1]), ("section", "dp"))
    gains_grad = lax.dynamic_slice_in_dim(summed_gains, section_index, 1, 0)
    return (
        stacked_rows,
        embedding_grad,
        weight_shards[0][None],
        weight_shards[1][None],
        weight_shards[2][None],
        weight_shards[3][None],
        weight_shards[4][None],
        weight_shards[5][None],
        gains_grad,
    )


def solution(mesh):
    return jax.shard_map(
        per_device,
        mesh=mesh,
        in_specs=(
            P("section", "dp", None),
            P("dp", None),
            P("dp", None),
            P(),
            P("section", None, "dp"),
            P("section", "dp", None),
            P("section", None, "dp"),
            P("section", "dp", None),
            P("section", None, "dp"),
            P("section", None, "dp"),
            P("section", None, None),
            P("section", "dp", None, None),
        ),
        out_specs=(
            P("section", "dp", None, None),
            P(),
            P("section", None, "dp"),
            P("section", "dp", None),
            P("section", None, "dp"),
            P("section", "dp", None),
            P("section", None, "dp"),
            P("section", None, "dp"),
            P("section", None, None),
        ),
        check_vma=False,
    )
```

profile of v0, /device:TPU:0, one launch (start us, length us, event | category | flops | bytes accessed | tf_op | source)
XLA Modules:
  0.0 3585.5 jit_solution(6173447196450877106)
XLA Ops:
  11.9 57.9 %all-gather.9.cloned.1.call-done = bf16[1,384,1472]{2,1,0:T(8,128)(2,1)} async-done(((bf16[1,24,1472]{2,1,0:T(8,128)(2,1)}), bf16[1,384,1472]{2,1,0:T(8,128)(2,1)}) %all-gather.9.cloned.1.call-update) | async-done | bytes 1130512 | tf_op jit(solution)/shard_map/all_gather | solution.py:380
  69.7 57.8 %all-gather.15.cloned.1.call-done = bf16[1,1472,384]{1,2,0:T(8,128)(2,1)} async-done(((bf16[1,1472,24]{1,2,0:T(8,128)(2,1)}), bf16[1,1472,384]{1,2,0:T(8,128)(2,1)}) %all-gather.15.cloned.1.call-update) | async-done | bytes 1130512 | tf_op jit(solution)/shard_map/all_gather | solution.py:383
  127.5 57.8 %all-gather.17.cloned.1.call-done = bf16[1,1472,384]{1,2,0:T(8,128)(2,1)} async-done(((bf16[1,1472,24]{1,2,0:T(8,128)(2,1)}), bf16[1,1472,384]{1,2,0:T(8,128)(2,1)}) %all-gather.17.cloned.1.call-update) | async-done | bytes 1130512 | tf_op jit(solution)/shard_map/all_gather | solution.py:384
  185.4 72.8 %all-gather.7.cloned.1.call-done = bf16[1,1472,1152]{1,2,0:T(8,128)(2,1)} async-done(((bf16[1,1472,72]{1,2,0:T(8,128)(2,1)}), bf16[1,1472,1152]{1,2,0:T(8,128)(2,1)}) %all-gather.7.cloned.1.call-update) | async-done | bytes 3391504 | tf_op jit(solution)/shard_map/all_gather | solution.py:379
  258.2 138.4 %all-gather.13.cloned.1.call-done = bf16[1,3584,1472]{2,1,0:T(8,128)(2,1)} async-done(((bf16[1,224,1472]{2,1,0:T(8,128)(2,1)}), bf16[1,3584,1472]{2,1,0:T(8,128)(2,1)}) %all-gather.13.cloned.1.call-update) | async-done | bytes 10551312 | tf_op jit(solution)/shard_map/all_gather | solution.py:382
  396.6 242.3 %all-gather.11.cloned.1.call-done = bf16[1,1472,7168]{1,2,0:T(8,128)(2,1)} async-done(((bf16[1,1472,448]{1,2,0:T(8,128)(2,1)}), bf16[1,1472,7168]{1,2,0:T(8,128)(2,1)}) %all-gather.11.cloned.1.call-update) | async-done | bytes 21102608 | tf_op jit(solution)/shard_map/all_gather | solution.py:381
  638.8 40.6 %conditional.4 = (f32[128,1472]{0,1:T(8,128)}, f32[128,1472]{0,1:T(8,128)}, f32[128,1472]{0,1:T(8,128)}, bf16[128,1152]{1,0:T(8,128)(2,1)}, f32[6,128]{1,0:T(8,1...) conditional(s32[]{:T(128)} %convert_element_type.326, () %tuple.54, ...), branch_computations={%region_0.0_spmd, %region_1.7_spmd} | conditional | flops 5099872256 | bytes 72641712 | solution.py:466
  683.0 75.6 %conditional.5 = (f32[1472,1152]{1,0:T(8,128)}, f32[384,1472]{0,1:T(8,128)}, f32[1472,7168]{1,0:T(8,128)}, f32[3584,1472]{0,1:T(8,128)}, f32[1472,384]{1,0:T(8,1...) conditional(s32[]{:T(128)} %convert_element_type.326, ...), branch_computations={%region_7.23_spmd, %region_23.29_spmd} | conditional | flops 15962501120 | bytes 355972672 | solution.py:466
  759.7 65.4 %collective-permute-start.1 = (bf16[128,768]{0,1:T(8,128)(2,1)S(1)}, bf16[128,768]{0,1:T(8,128)(2,1)S(1)}, u32[]{:S(2)}, u32[]{:S(2)}) collective-permute-start(bf16[128,768]{0,1:T(8,128)(2,1)S(1)} %copy.261), channel_id=1, source_target_pairs={{0,16},{1,17},{2,18},{3,19},{4,20},{5,21},{6,22},{7,23},{8,24},{9,... | collective-permute-start | bytes 589832 | tf_op jit(solution)/shard_map/ppermute | solution.py:26
  829.7 143.8 %conditional.6 = (f32[1472,1152]{1,0:T(8,128)}, f32[384,1472]{0,1:T(8,128)}, f32[1472,7168]{1,0:T(8,128)}, f32[3584,1472]{0,1:T(8,128)}, f32[1472,384]{1,0:T(8,1...) conditional(s32[]{:T(128)} %convert_element_type.326, ...), branch_computations={%region_29.45_spmd, %region_45.56_spmd} | conditional | flops 15982288896 | bytes 391629312 | solution.py:466
  871.7 15.3 multiply_reduce_fusion.30
  906.3 30.7 convolution_add_fusion.17
  937.0 18.1 convolution_add_fusion.18
  975.8 22.0 collective-permute-done.3
  997.8 125.6 %conditional.7 = ((f32[1472,1152]{1,0:T(8,128)}, f32[1472,7168]{1,0:T(8,128)}, f32[1472,384]{1,0:T(8,128)}, f32[1472,384]{1,0:T(8,128)}, f32[3,1472]{1,0:T(4,128...) conditional(s32[]{:T(128)} %convert_element_type.326, (f32[1472,1152]{1,0:T(8,128)}, ...), branch_computations={%region_56.0_spmd, %region_57.68_spmd} | conditional | flops 13529720832 | bytes 342030624 | solution.py:466
  1006.7 14.3 fusion.274
  1031.6 15.5 multiply_reduce_fusion.40
  1059.6 31.1 convolution_add_fusion.24
  1141.7 20.0 reshape.936
  1172.1 42.4 %copy.287 = f32[1472,7168]{0,1:T(8,128)} copy(f32[1472,7168]{1,0:T(8,128)} %get-tuple-element.867) | data formatting | bytes 84410368 | tf_op jit(solution)/shard_map/cond | solution.py:466
  1214.5 46.1 %copy.288 = f32[16,1472,448]{2,1,0:T(8,128)} copy(f32[16,1472,448]{1,2,0:T(8,128)} %bitcast.341) | data formatting | bytes 84410368 | tf_op jit(solution)/shard_map/transpose | solution.py:351
  1260.7 52.5 %reshape.939 = f32[16,659456]{1,0:T(8,128)} reshape(f32[16,1472,448]{2,1,0:T(8,128)} %copy.288) | data formatting | bytes 84410368 | tf_op jit(solution)/shard_map/reshape | solution.py:352
  1313.1 21.5 copy.352
  1334.6 27.2 reshape.953
  1370.5 17.5 reshape.942
  1396.7 15.9 reshape.944
  1415.8 28.0 constant_dynamic-update-slice_fusion.3
  1465.1 42.8 %psum.15 = f32[2,3,1472]{2,0,1:T(2,128)S(1)} all-reduce(f32[2,3,1472]{2,0,1:T(2,128)S(1)} %broadcast_select_fusion), channel_id=1, replica_groups=mesh['section'=2,'dp'=16] {'section','dp'}, use_global_device_ids=true, to_apply=%region_70.0 | all-reduce | flops 8832 | bytes 70656 | tf_op jit(solution)/shard_map/psum | solution.py:500
  1508.6 1927.6 %all-reduce.6.cloned.1.call-done = f32[16,1201152]{1,0:T(8,128)} async-done(((f32[16,1201152]{1,0:T(8,128)}), f32[16,1201152]{1,0:T(8,128)}) %all-reduce.6.cloned.1.call-update) | async-done | bytes 76873744
  3446.2 31.7 dynamic-slice_reduce_fusion
  3483.2 16.7 dynamic-slice_reduce_fusion.1
  3504.1 71.2 %all-reduce.4.cloned.1.call-done = f32[384,1472]{0,1:T(8,128)} async-done(((f32[384,1472]{0,1:T(8,128)}), f32[384,1472]{0,1:T(8,128)}) %all-reduce.4.cloned.1.call-update) | async-done | bytes 2261008 | tf_op jit(solution)/shard_map/psum | solution.py:500
  (348 shorter events, 356.1 us)
Async XLA Ops:
  7.2 631.7 %copy-start.212 = (s32[1,2,128]{2,1,0:T(2,128)S(1)}, s32[1,2,128]{2,1,0:T(2,128)}, u32[]{:S(2)}) copy-start(s32[1,2,128]{2,1,0:T(2,128)} %param.20) | copy-start | bytes 3076
  7.2 631.6 %copy-start.44 = (bf16[384,1472]{0,1:T(8,128)(2,1)S(1)}, bf16[384,1472]{0,1:T(8,128)(2,1)}, u32[]{:S(2)}) copy-start(bf16[384,1472]{0,1:T(8,128)(2,1)} %param.23) | copy-start | bytes 3391492
  7.2 631.6 %copy-start.193 = (s32[2,128]{1,0:T(2,128)S(1)}, s32[2,128]{1,0:T(2,128)}, u32[]{:S(2)}) copy-start(s32[2,128]{1,0:T(2,128)} %param.21) | copy-start | bytes 3076
  7.2 62.5 %all-gather.9.cloned.1.call-start = ((), (), s32[]{:S(2)}) async-start(), calls=%async_computation.1 | async-start | bytes 1253376 | tf_op jit(solution)/shard_map/all_gather | solution.py:380
  8.0 119.6 %all-gather.15.cloned.1.call-start = ((), (), s32[]{:S(2)}) async-start(), calls=%async_computation.4 | async-start | bytes 1253376 | tf_op jit(solution)/shard_map/all_gather | solution.py:383
  8.7 176.7 %all-gather.17.cloned.1.call-start = ((), (), s32[]{:S(2)}) async-start(), calls=%async_computation.5 | async-start | bytes 1253376 | tf_op jit(solution)/shard_map/all_gather | solution.py:384
  9.4 248.7 %all-gather.7.cloned.1.call-start = ((), (), s32[]{:S(2)}) async-start(), calls=%async_computation | async-start | bytes 3760128 | tf_op jit(solution)/shard_map/all_gather | solution.py:379
  10.0 386.6 %all-gather.13.cloned.1.call-start = ((), (), s32[]{:S(2)}) async-start(), calls=%async_computation.3 | async-start | bytes 11698176 | tf_op jit(solution)/shard_map/all_gather | solution.py:382
  10.6 628.2 %all-gather.11.cloned.1.call-start = ((), (), s32[]{:S(2)}) async-start(), calls=%async_computation.2 | async-start | bytes 23396352 | tf_op jit(solution)/shard_map/all_gather | solution.py:381
  11.2 3425.1 %all-reduce.6.cloned.1.call-start = ((), (), s32[]{:S(2)}) async-start(), calls=%async_computation.7 | async-start | bytes 153747456
  662.8 11.9 copy-start.16
  680.5 2.5 collective-permute-start
  709.9 9.2 copy-start.140
  759.7 67.8 %collective-permute-start.1 = (bf16[128,768]{0,1:T(8,128)(2,1)S(1)}, bf16[128,768]{0,1:T(8,128)(2,1)S(1)}, u32[]{:S(2)}, u32[]{:S(2)}) collective-permute-start(bf16[128,768]{0,1:T(8,128)(2,1)S(1)} %copy.261), channel_id=1, source_target_pairs={{0,16},{1,17},{2,18},{3,19},{4,20},{5,21},{6,22},{7,23},{8,24},{9,... | collective-permute-start | bytes 589832 | tf_op jit(solution)/shard_map/ppermute | solution.py:26
  826.2 3.5 collective-permute-start.2
  849.4 37.5 %copy-start.177 = (f32[128]{0:T(128)}, f32[128]{0:T(128)S(1)}, u32[]{:S(2)}) copy-start(f32[128]{0:T(128)S(1)} %fusion.214) | copy-start | bytes 1540 | tf_op jit(solution)/shard_map/cond
  861.9 9.7 copy-start.78
  888.7 14.0 copy-start.50
  894.8 7.9 copy-start.96
  895.4 7.3 copy-start.110
  895.6 7.1 copy-start.112
  895.6 7.1 copy-start.133
  937.0 18.1 copy-start.204
  974.5 23.3 collective-permute-start.3
  997.8 92.9 %copy-start.134 = (bf16[128,768]{1,0:T(8,128)(2,1)}, bf16[128,768]{1,0:T(8,128)(2,1)S(1)}, u32[]{:S(2)}) copy-start(bf16[128,768]{1,0:T(8,128)(2,1)S(1)} %get-tuple-element.332) | copy-start | bytes 589828 | tf_op jit(solution)/shard_map/cond
  1000.6 52.2 %copy-start.208 = (f32[128]{0:T(128)}, f32[128]{0:T(128)S(1)}, u32[]{:S(2)}) copy-start(f32[128]{0:T(128)S(1)} %fusion.263) | copy-start | bytes 1540 | tf_op jit(solution)/shard_map/cond
  1002.1 88.6 %copy-start.37 = (f32[128,1472]{0,1:T(8,128)}, f32[128,1472]{0,1:T(8,128)S(1)}, u32[]{:S(2)}) copy-start(f32[128,1472]{0,1:T(8,128)S(1)} %copy.281) | copy-start | bytes 2260996 | tf_op jit(solution)/shard_map/cond
  1002.3 88.4 %copy-start.200 = (f32[128]{0:T(128)}, f32[128]{0:T(128)S(1)}, u32[]{:S(2)}) copy-start(f32[128]{0:T(128)S(1)} %fusion.264) | copy-start | bytes 1540 | tf_op jit(solution)/shard_map/cond
  1004.8 42.4 %copy-start.60 = (f32[128,1472]{0,1:T(8,128)}, f32[128,1472]{0,1:T(8,128)S(1)}, u32[]{:S(2)}) copy-start(f32[128,1472]{0,1:T(8,128)S(1)} %fusion.238) | copy-start | bytes 2260996 | tf_op jit(solution)/shard_map/cond
  1052.0 7.6 copy-start.94
  1443.8 13.8 copy-start.76
  1460.7 2114.6 %all-reduce.4.cloned.1.call-start = ((), (), s32[]{:S(2)}) async-start(), calls=%async_computation.6 | async-start | bytes 4521984 | tf_op jit(solution)/shard_map/psum | solution.py:500
  (55 other events, 174.3 us)
Sparse Core Ops, SparseCore 0:
  10.9 58.8 all-gather.8
  72.5 54.9 all-gather.14
  130.3 54.9 all-gather.16
  188.0 70.1 all-gather.6
  260.8 135.7 all-gather.12
  399.2 239.5 all-gather.10
  1460.9 1975.3 all-reduce.5
  3441.8 133.4 all-reduce.3
where the time goes:
time: 3600 us; the launch traced here: 3590 us
  waiting for transfers between devices  2650 us (74%)
  local copies, waits for them, and re-layouts  473 us (13%)
  matrix products  295 us (8%)
  starting transfers between devices  70.3 us (2%)
  blocking collectives  42.8 us (1%)
    unnamed x9, waiting for transfers between devices  1930 us
    all_gather x1, waiting for transfers between devices, per_device(): lax.all_gather(widen_weight, 'dp', axis=2, tiled=True)  242 us
    all_gather x1, waiting for transfers between devices, per_device(): lax.all_gather(narrow_weight, 'dp', axis=1, tiled=True)  138 us
    dot_general x12, matrix products, product_left(): lax.dot_general(first_factor, second_factor, (((0,), (0,)), ((), ())), pr...  130 us
    reshape x4, local copies, waits for them, and re-layouts, pack_rows(): return matrix.reshape(row_count, pieces, column_count // pieces).transpos...  106 us
    dot_general x16, matrix products, product(): jnp.dot(first_factor, second_factor, preferred_element_type=jnp.float32)  88.3 us
    all_gather x1, waiting for transfers between devices, per_device(): lax.all_gather(attention_in, 'dp', axis=2, tiled=True)  72.8 us
  transfers between devices with their start and end apart: 12, of which 11 were waited for; matrix products, arithmetic and copies ran while one was open for 2% of the time, Pallas kernels for 0%

commit v1 on v0

v1 whole, which is shorter than its diff:
```python
import jax
import jax.numpy as jnp
from jax import lax
from jax.sharding import Mesh, PartitionSpec as P

HEADS = 6
HEAD_DIM = 64
PLANE = 4

epsilon = 1e-06
masked_value = -1000000000.0
AXES = ("section", "line", "plane")
bf16 = jnp.bfloat16
f32 = jnp.float32


def nn(a, b):
    return lax.dot_general(a, b, (((1,), (0,)), ((), ())), preferred_element_type=f32)


def nt(a, b):
    return lax.dot_general(a, b, (((1,), (1,)), ((), ())), preferred_element_type=f32)


def tn(a, b):
    return lax.dot_general(a, b, (((0,), (0,)), ((), ())), preferred_element_type=f32)


def rms_norm(inputs, gain_row):
    return inputs * lax.rsqrt(jnp.mean(inputs * inputs, -1, keepdims=True) + epsilon) * gain_row


def rms_back(inputs, gain_row, upstream):
    scale = lax.rsqrt(jnp.mean(inputs * inputs, -1, keepdims=True) + epsilon)
    normed = inputs * scale
    weighted = upstream * gain_row
    grad = (weighted - normed * jnp.mean(weighted * normed, -1, keepdims=True)) * scale
    return grad, jnp.sum(upstream * normed, 0)


def gated_value(gate_part, up_part):
    return jax.nn.gelu(gate_part, approximate=True) * up_part


def heads_of(matrix, rows):
    return matrix.reshape(rows, -1, HEADS, HEAD_DIM)


def score_table(queries, keys, allowed):
    raw = jnp.einsum("rqhd,rkhd->rhqk", queries, keys, preferred_element_type=f32)
    return jnp.where(allowed[:, None], raw * HEAD_DIM ** (-0.5), masked_value)


def attend(queries, keys, values, allowed):
    rows = allowed.shape[0]
    scores = score_table(heads_of(queries, rows), heads_of(keys, rows), allowed)
    top = jnp.max(scores, -1, keepdims=True)
    exponent = jnp.exp(scores - top)
    totals = jnp.sum(exponent, -1, keepdims=True)
    weights = (exponent / totals).astype(bf16)
    context = jnp.einsum("rhqk,rkhd->rqhd", weights, heads_of(values, rows), preferred_element_type=f32)
    return context.reshape(queries.shape).astype(bf16), top + jnp.log(totals)


def attend_back(queries, keys, values, allowed, log_total, context_grad):
    rows = allowed.shape[0]
    q, k, v, g = (heads_of(m, rows) for m in (queries, keys, values, context_grad))
    chances = jnp.exp(score_table(q, k, allowed) - log_total)
    weight_grad = jnp.einsum("rqhd,rkhd->rhqk", g, v, preferred_element_type=f32)
    value_grad = jnp.einsum("rhqk,rqhd->rkhd", chances.astype(bf16), g, preferred_element_type=f32)
    score_grad = (
        chances * (weight_grad - jnp.sum(weight_grad * chances, -1, keepdims=True))
    ).astype(bf16)
    query_grad = jnp.einsum("rhqk,rkhd->rqhd", score_grad, k, preferred_element_type=f32)
    key_grad = jnp.einsum("rhqk,rqhd->rkhd", score_grad, q, preferred_element_type=f32)
    scale = HEAD_DIM ** (-0.5)
    shape = queries.shape
    return (
        (query_grad.reshape(shape) * scale).astype(bf16),
        (key_grad.reshape(shape) * scale).astype(bf16),
        value_grad.reshape(shape).astype(bf16),
    )


def build(lines):
    devices = lines * PLANE

    def place(section, line, plane):
        return section * devices + line * PLANE + plane

    def hop(block, offset, sections=(0, 1)):
        route = [
            (place(s, z, j), place(s, z, j ^ offset))
            for s in sections
            for z in range(lines)
            for j in range(PLANE)
        ]
        return lax.ppermute(block, AXES, route)

    def cross(block, sources):
        return lax.ppermute(block, "section", [(s, 1 - s) for s in sources])

    def along(block, step):
        route = [(z, z + step) for z in range(lines) if 0 <= z + step < lines]
        return lax.ppermute(block, "line", route)

    def narrow_route(section, half):
        route = []
        for block in range(devices):
            target = (block % 2, 2 * (block // 8) + half, (block % 8) // 2)
            route.append((section * devices + block, place(*target)))
        return route

    def gather_line(block):
        if lines > 8:
            return lax.all_gather(block, "line", axis=0)
        z = lax.axis_index("line")
        right, left = [block], [block]
        for _ in range(lines - 1):
            right.append(along(right[-1], 1))
            left.append(along(left[-1], -1))
        out = jnp.zeros((lines,) + block.shape, block.dtype)
        out = lax.dynamic_update_index_in_dim(out, block, z, 0)
        for step in range(1, lines):
            piece = jnp.where(z >= step, right[step], left[lines - step])
            out = lax.dynamic_update_index_in_dim(out, piece, lax.rem(z - step + lines, lines), 0)
        return out

    def scatter_line(partial):
        if lines > 8:
            return lax.psum_scatter(partial, "line", scatter_dimension=0).astype(f32)
        z = lax.axis_index("line")

        def own(index):
            return lax.dynamic_index_in_dim(partial, jnp.clip(index, 0, lines - 1), 0, False).astype(f32)

        right = left = None
        for step in range(1, lines):
            to_right, to_left = own(z + lines - step), own(z - lines + step)
            if right is not None:
                to_right, to_left = to_right + right.astype(f32), to_left + left.astype(f32)
            right, left = along(to_right.astype(bf16), 1), along(to_left.astype(bf16), -1)
        return own(z) + right.astype(f32) + left.astype(f32)

    def gather_plane(block):
        j = lax.axis_index("plane")
        out = jnp.zeros((PLANE,) + block.shape, block.dtype)
        out = lax.dynamic_update_index_in_dim(out, block, j, 0)
        for offset in range(1, PLANE):
            out = lax.dynamic_update_index_in_dim(out, hop(block, offset), j ^ offset, 0)
        return out

    def gather_all(block):
        column = gather_line(block)
        return gather_plane(column).swapaxes(0, 1).reshape((devices,) + block.shape)

    def scatter_all(partial):
        j = lax.axis_index("plane")
        parts = partial.reshape((lines, PLANE) + partial.shape[1:])
        total = lax.dynamic_index_in_dim(parts, j, 1, False).astype(f32)
        for offset in range(1, PLANE):
            sent = lax.dynamic_index_in_dim(parts, j ^ offset, 1, False)
            total = total + hop(sent, offset).astype(f32)
        return scatter_line(total.astype(bf16))

    def per_device(
        byte_codes,
        encoder_segments,
        target_segments,
        embedding,
        attention_in,
        attention_out,
        widen_weight,
        narrow_weight,
        cross_first,
        cross_second,
        norm_gains,
        cotangent,
    ):
        section = lax.axis_index("section")
        z = lax.axis_index("line")
        is_encoder = section == 0
        inner = cross_first.shape[2] * devices
        width = embedding.shape[1]
        rows, length = encoder_segments.shape
        tokens = rows * length
        gains = norm_gains[0].astype(f32)

        def spread(block, source):
            blocks = [block] + [hop(block, k, (source,)) for k in range(1, PLANE)]
            here = section == source
            return jnp.concatenate([jnp.where(here, b, cross(b, (source,))) for b in blocks], 0)

        def collect(partial, source):
            partial = partial.astype(bf16)
            total = (partial.astype(f32) + cross(partial, (1 - source,)).astype(f32)).reshape(
                PLANE, tokens, width
            )
            result = total[0]
            for k in range(1, PLANE):
                result = result + hop(total[k].astype(bf16), k, (source,)).astype(f32)
            return result

        in_cols = attention_in.shape[2]
        cross_cols = cross_first.shape[2]
        out_rows = attention_out.shape[1]
        attention_pack = jnp.concatenate(
            [attention_in[0].T, cross_first[0].T, cross_second[0].T, attention_out[0]], 0
        )
        cuts = (0, in_cols, in_cols + cross_cols, in_cols + 2 * cross_cols, attention_pack.shape[0])
        widen_half = widen_weight.shape[2] // 2
        halves = widen_weight[0].T.reshape(2, widen_half, width)
        kept = lax.dynamic_index_in_dim(halves, section, 0, False)
        got = cross(lax.dynamic_index_in_dim(halves, 1 - section, 0, False), (0, 1))
        narrow_half = narrow_weight.shape[1] // 2
        narrow_parts = narrow_weight[0].reshape(2, narrow_half, width)
        even_line = lax.rem(z, 2) == 0

        def feed_weights(own_section):
            widen_piece = jnp.where(section == own_section, kept, got)
            pieces = [
                lax.ppermute(narrow_parts[half], AXES, narrow_route(own_section, half))
                for half in range(2)
            ]
            narrow_piece = jnp.where(even_line, pieces[0], pieces[1])
            full = lax.all_gather(jnp.concatenate([widen_piece, narrow_piece], 0), "line", axis=0)
            return (
                full[: lines // 2, :widen_half].reshape(-1, width),
                full[lines // 2 :, :widen_half].reshape(-1, width),
                full[:, widen_half:].reshape(-1, width),
            )

        encoder_feed = feed_weights(0)
        decoder_feed = feed_weights(1)
        gathered = gather_all(attention_pack)
        in_t, first_t, second_t, out_w = (
            gathered[:, cuts[i] : cuts[i + 1]].reshape(-1, width) for i in range(4)
        )

        codes = byte_codes[0].reshape(tokens)
        one_hot = (
            codes[:, None] == lax.broadcasted_iota(jnp.int32, (tokens, embedding.shape[0]), 1)
        ).astype(bf16)
        inputs = nn(one_hot, embedding)
        own_segments = jnp.where(is_encoder, encoder_segments, target_segments)
        earlier = lax.broadcasted_iota(jnp.int32, (length, length), 1) <= lax.broadcasted_iota(
            jnp.int32, (length, length), 0
        )
        allowed = (own_segments[:, :, None] == own_segments[:, None, :]) & (earlier | is_encoder)[None]
        normed_self = rms_norm(inputs, gains[0]).astype(bf16)
        projected = nt(normed_self, in_t).astype(bf16)
        queries, keys, values = (projected[:, i * inner : (i + 1) * inner] for i in range(3))
        context, log_total = attend(queries, keys, values, allowed)
        first_sum = inputs + nn(context, out_w)
        normed_first = rms_norm(first_sum, gains[1]).astype(bf16)

        def feed_forward(stream, weights):
            gate, up = nt(stream, weights[0]), nt(stream, weights[1])
            hidden = gated_value(gate, up).astype(bf16)
            return gate, up, hidden, nn(hidden, weights[2])

        def feed_back(output_grad, gate, up, weights):
            hidden_grad = nt(output_grad, weights[2])
            _, pull_back = jax.vjp(gated_value, gate, up)
            gate_grad, up_grad = (part.astype(bf16) for part in pull_back(hidden_grad))
            return gate_grad, up_grad, nn(gate_grad, weights[0]) + nn(up_grad, weights[1])

        def feed_grads(stream, hidden, gate_grad, up_grad, output_grad):
            gate_part = tn(gate_grad, stream).astype(bf16).reshape(lines // 2, widen_half, width)
            up_part = tn(up_grad, stream).astype(bf16).reshape(lines // 2, widen_half, width)
            narrow_part = tn(hidden, output_grad).astype(bf16).reshape(lines, narrow_half, width)
            pack = jnp.concatenate([jnp.concatenate([gate_part, up_part], 0), narrow_part], 1)
            return lax.psum_scatter(pack, "line", scatter_dimension=0)

        stream_e = spread(normed_first, 0)
        gate_e, up_e, hidden_e, part_e = feed_forward(stream_e, encoder_feed)
        second_e = first_sum + collect(part_e, 0)
        normed_final = rms_norm(second_e, gains[2]).astype(bf16)
        first_product = nt(jnp.where(is_encoder, normed_final, normed_first), first_t).astype(bf16)
        second_product = nt(normed_final, second_t).astype(bf16)
        states = cross(jnp.concatenate([first_product, second_product], 1), (0,))

        cross_queries, state_keys, state_values = first_product, states[:, :inner], states[:, inner:]
        cross_allowed = target_segments[:, :, None] == encoder_segments[:, None, :]
        cross_context, cross_total = attend(cross_queries, state_keys, state_values, cross_allowed)
        second_t_sum = first_sum + nn(cross_context, second_t)
        normed_last = rms_norm(second_t_sum, gains[2]).astype(bf16)
        own_cotangent = cotangent[0].reshape(tokens, width)
        cotangent_d = spread(own_cotangent, 1)
        stream_d = spread(normed_last, 1)
        gate_d, up_d, hidden_d, part_d = feed_forward(stream_d, decoder_feed)
        gate_grad_d, up_grad_d, back_d = feed_back(cotangent_d, gate_d, up_d, decoder_feed)
        last_grad = collect(back_d, 1)
        outputs_d = second_t_sum + collect(part_d, 1)
        summed_d = feed_grads(stream_d, hidden_d, gate_grad_d, up_grad_d, cotangent_d)
        long_cotangent = own_cotangent.astype(f32)
        input_grad, gain_two_d = rms_back(second_t_sum, gains[2], last_grad)
        stream_two_d = long_cotangent + input_grad
        cross_branch = stream_two_d.astype(bf16)
        cross_context_grad = nt(cross_branch, second_t).astype(bf16)
        cross_query_grad, state_key_grad, state_value_grad = attend_back(
            cross_queries, state_keys, state_values, cross_allowed, cross_total, cross_context_grad
        )
        state_grads = cross(jnp.concatenate([state_key_grad, state_value_grad], 1), (1,))
        input_grad, gain_one_d = rms_back(first_sum, gains[1], nn(cross_query_grad, first_t))
        stream_one_d = stream_two_d + input_grad

        key_grads, value_grads = state_grads[:, :inner], state_grads[:, inner:]
        final_grad = nn(key_grads, first_t) + nn(value_grads, second_t)
        input_grad, gain_two_e = rms_back(second_e, gains[2], final_grad)
        stream_two_e = long_cotangent + input_grad
        output_grad_e = spread(stream_two_e.astype(bf16), 0)
        gate_grad_e, up_grad_e, back_e = feed_back(output_grad_e, gate_e, up_e, encoder_feed)
        middle_grad = collect(back_e, 0)
        summed_e = feed_grads(stream_e, hidden_e, gate_grad_e, up_grad_e, output_grad_e)
        input_grad, gain_one_e = rms_back(first_sum, gains[1], middle_grad)
        stream_one_e = stream_two_e + input_grad

        stream_one = jnp.where(is_encoder, stream_one_e, stream_one_d)
        branch_grad = stream_one.astype(bf16)
        context_grad = nt(branch_grad, out_w).astype(bf16)
        projected_grad = jnp.concatenate(
            attend_back(queries, keys, values, allowed, log_total, context_grad), 1
        )
        input_grad, gain_zero = rms_back(inputs, gains[0], nn(projected_grad, in_t))
        table_grad = tn(one_hot, (stream_one + input_grad).astype(bf16))

        first_left = jnp.where(is_encoder, key_grads, cross_query_grad)
        first_right = jnp.where(is_encoder, normed_final, normed_first)
        second_left = jnp.where(is_encoder, value_grads, cross_context)
        second_right = jnp.where(is_encoder, normed_final, cross_branch)
        products = (
            tn(projected_grad, normed_self),
            tn(first_left, first_right),
            tn(second_left, second_right),
            tn(context, branch_grad),
        )
        attention_sum = scatter_all(
            jnp.concatenate([m.astype(bf16).reshape(devices, -1, width) for m in products], 1)
        )

        gain_rows = jnp.stack(
            [
                gain_zero,
                jnp.where(is_encoder, gain_one_e, gain_one_d),
                jnp.where(is_encoder, gain_two_e, gain_two_d),
            ]
        )
        slot = lax.broadcasted_iota(jnp.int32, (2, 1, 1), 0)
        gain_slots = jnp.where(slot == section, gain_rows[None], 0.0)
        summed_gains, embedding_grad = lax.psum((gain_slots, table_grad), AXES)
        gains_grad = lax.dynamic_slice_in_dim(summed_gains, section, 1, 0)

        kept_half = jnp.where(is_encoder, summed_e[:widen_half], summed_d[:widen_half])
        sent_half = jnp.where(is_encoder, summed_d[:widen_half], summed_e[:widen_half])
        got_half = cross(sent_half, (0, 1))
        widen_t = jnp.where(
            is_encoder,
            jnp.concatenate([kept_half, got_half], 0),
            jnp.concatenate([got_half, kept_half], 0),
        )
        returned = []
        for own_section, summed in ((0, summed_e), (1, summed_d)):
            returned.append(
                jnp.concatenate(
                    [
                        lax.ppermute(
                            summed[widen_half:], AXES, [(b, a) for a, b in narrow_route(own_section, half)]
                        )
                        for half in range(2)
                    ],
                    0,
                )
            )
        narrow_grad = jnp.where(is_encoder, returned[0], returned[1]).astype(f32)

        block_output = jnp.where(is_encoder, second_e, outputs_d).astype(bf16)
        return (
            block_output.reshape(1, rows, length, width),
            embedding_grad,
            attention_sum[cuts[0] : cuts[1]].T[None],
            attention_sum[cuts[3] : cuts[4]][None],
            widen_t.astype(f32).T[None],
            narrow_grad[None],
            attention_sum[cuts[1] : cuts[2]].T[None],
            attention_sum[cuts[2] : cuts[3]].T[None],
            gains_grad,
        )

    return per_device


def solution(mesh):
    lines = mesh.shape["dp"] // PLANE
    inner_mesh = Mesh(mesh.devices.reshape(2, lines, PLANE), AXES)
    dp = ("line", "plane")
    return jax.shard_map(
        build(lines),
        mesh=inner_mesh,
        in_specs=(
            P("section", dp, None),
            P(dp, None),
            P(dp, None),
            P(),
            P("section", None, dp),
            P("section", dp, None),
            P("section", None, dp),
            P("section", dp, None),
            P("section", None, dp),
            P("section", None, dp),
            P("section", None, None),
            P("section", dp, None, None),
        ),
        out_specs=(
            P("section", dp, None, None),
            P(),
            P("section", None, dp),
            P("section", dp, None),
            P("section", None, dp),
            P("section", dp, None),
            P("section", None, dp),
            P("section", None, dp),
            P("section", None, None),
        ),
        check_vma=False,
    )
```

time: 3600 us -> 810 us (0.23)
  waiting for transfers between devices: 2650 us -> 339 us
  local copies, waits for them, and re-layouts: 473 us -> 79.3 us
  matrix products: 295 us -> 78 us
  starting transfers between devices: 70.3 us -> 153 us
  other arithmetic: 21.9 us -> 89.9 us
    unnamed x9 -> x5, waiting for transfers between devices: 1930 us -> 0.08 us
    all_gather x6 -> x2, waiting for transfers between devices: 627 us -> 30 us  [feed_weights(): lax.all_gather(jnp.concatenate([widen_piece, narrow_piece], 0), 'line', a...]
    dot_general x56 -> x47, matrix products: 295 us -> 78 us  [the longest x11 28 us: tn(): lax.dot_general(a, b, (((0,), (0,)), ((), ())), preferred_element_type=f32)]
    ppermute x4 -> x74, waiting for transfers between devices: 24.6 us -> 232 us  [the longest x30 172 us: hop(): return lax.ppermute(block, AXES, route)]
    reshape x12 -> x9, local copies, waits for them, and re-layouts: 135 us -> 2.39 us  [the longest x1 1.97 us: per_device(): block_output.reshape(1, rows, length, width)]
    ppermute x4 -> x74, starting transfers between devices: 70 us -> 153 us  [the longest x30 61.4 us: hop(): return lax.ppermute(block, AXES, route)]
    transpose x4 -> x0, local copies, waits for them, and re-layouts: 69.7 us -> none  [pack_rows(): return matrix.reshape(row_count, pieces, column_count // pieces).transpos...]
    cond x146 -> x0, local copies, waits for them, and re-layouts: 60 us -> none  [the longest x8 58.7 us: per_device(): packet = lax.cond(is_encoder, encoder_work, target_work)]
  transfers between devices with their start and end apart: 12 -> 79, of which waited for: 11 -> 27; matrix products, arithmetic and copies ran while one was open for 2% -> 24% of each run, Pallas kernels for 0% -> 0%
where the time goes in v1:
time: 810 us; the launch traced here: 800 us
  waiting for transfers between devices  339 us (42%)
  starting transfers between devices  153 us (19%)
  other arithmetic  89.9 us (11%)
  local copies, waits for them, and re-layouts  79.3 us (10%)
  matrix products  78 us (10%)
  blocking collectives  44.1 us (5%)
  between operations  17.1 us (2%)
    ppermute x30, waiting for transfers between devices, hop(): return lax.ppermute(block, AXES, route)  172 us
    psum x1, waiting for transfers between devices, per_device(): summed_gains, embedding_grad = lax.psum((gain_slots, table_grad), AXES)  76.6 us
    ppermute x30, starting transfers between devices, hop(): return lax.ppermute(block, AXES, route)  61.4 us
    psum x1, blocking collectives, per_device(): summed_gains, embedding_grad = lax.psum((gain_slots, table_grad), AXES)  44.1 us
    ppermute x24, starting transfers between devices, cross(): return lax.ppermute(block, 'section', [(s, 1 - s) for s in sources])  40.8 us
    ppermute x12, starting transfers between devices, along(): return lax.ppermute(block, 'line', route)  34.3 us
    ppermute x12, waiting for transfers between devices, along(): return lax.ppermute(block, 'line', route)  31.2 us
    all_gather x2, waiting for transfers between devices, feed_weights(): lax.all_gather(jnp.concatenate([widen_piece, narrow_piece], 0), 'line', a...  30 us
  transfers between devices with their start and end apart: 79, of which 27 were waited for; matrix products, arithmetic and copies ran while one was open for 24% of the time, Pallas kernels for 0%

profile of v1, /device:TPU:0, one launch (start us, length us, event | category | flops | bytes accessed | tf_op | source)
XLA Modules:
  0.0 800.0 jit_solution(16060514198796535330)
XLA Ops:
  9.3 5.7 collective-permute-start
  18.3 4.6 collective-permute-start.18
  22.9 4.3 collective-permute-start.17
  31.2 4.6 collective-permute-start.4
  35.8 9.6 %collective-permute-done.2 = bf16[144,1472]{1,0:T(8,128)(2,1)} collective-permute-done((bf16[144,1472]{1,0:T(8,128)(2,1)}, bf16[144,1472]{1,0:T(8,128)(2,1)}, u32[]{:S(2)}, u32[]{:S(2)}) %collective-permute-start.2) | collective-permute-done | bytes 423968 | tf_op jit(solution)/shard_map/ppermute | solution.py:105
  48.8 4.6 collective-permute-start.5
  53.4 4.8 collective-permute-done.3
  73.4 31.7 %collective-permute-done.6 = bf16[4,144,1472]{2,1,0:T(8,128)(2,1)} collective-permute-done((bf16[4,144,1472]{2,1,0:T(8,128)(2,1)}, bf16[4,144,1472]{2,1,0:T(8,128)(2,1)}, u32[]{:S(2)}, u32[]{:S(2)}) %collective-permute-start.6) | collective-permute-done | bytes 1695776 | tf_op jit(solution)/shard_map/ppermute | solution.py:98
  106.7 33.8 %collective-permute-done.7 = bf16[4,144,1472]{2,1,0:T(8,128)(2,1)} collective-permute-done((bf16[4,144,1472]{2,1,0:T(8,128)(2,1)}, bf16[4,144,1472]{2,1,0:T(8,128)(2,1)}, u32[]{:S(2)}, u32[]{:S(2)}) %collective-permute-start.7) | collective-permute-done | bytes 1695776 | tf_op jit(solution)/shard_map/ppermute | solution.py:98
  170.3 6.6 collective-permute-done.12
  198.0 6.3 copy.70
  233.0 5.5 collective-permute-done.20
  239.8 8.3 %collective-permute-done.22 = bf16[256,1472]{0,1:T(8,128)(2,1)} collective-permute-done((bf16[256,1472]{0,1:T(8,128)(2,1)}, bf16[256,1472]{0,1:T(8,128)(2,1)}, u32[]{:S(2)}, u32[]{:S(2)}) %collective-permute-start.22) | collective-permute-done | bytes 753696 | tf_op jit(solution)/shard_map/ppermute | solution.py:98
  248.1 7.5 collective-permute-done.21
  281.2 30.0 %all-gather.7.cloned.1.call-done = bf16[1344,1472]{1,0:T(8,128)(2,1)} async-done(((bf16[336,1472]{1,0:T(8,128)(2,1)}), bf16[1344,1472]{1,0:T(8,128)(2,1)}) %all-gather.7.cloned.1.call-update) | async-done | bytes 3956752 | tf_op jit(solution)/shard_map/all_gather | solution.py:226
  324.1 4.5 multiply_convert_fusion.1
  334.0 6.4 collective-permute-start.44
  344.2 4.3 convert_add_fusion.1
  366.1 20.5 %collective-permute-done.48 = bf16[256,768]{0,1:T(8,128)(2,1)S(1)} collective-permute-done((bf16[256,768]{0,1:T(8,128)(2,1)S(1)}, bf16[256,768]{0,1:T(8,128)(2,1)S(1)}, u32[]{:S(2)}, u32[]{:S(2)}) %collective-permute-start.48) | collective-permute-done | bytes 393248 | tf_op jit(solution)/shard_map/ppermute | solution.py:101
  458.8 6.9 convert_add_fusion
  482.9 6.3 collective-permute-done.59
  489.2 11.4 %collective-permute-done.58 = bf16[256,1472]{0,1:T(8,128)(2,1)} collective-permute-done((bf16[256,1472]{0,1:T(8,128)(2,1)}, bf16[256,1472]{0,1:T(8,128)(2,1)}, u32[]{:S(2)}, u32[]{:S(2)}) %collective-permute-start.58) | collective-permute-done | bytes 753696 | tf_op jit(solution)/shard_map/ppermute | solution.py:98
  522.1 5.8 copy.95
  551.1 30.5 %collective-permute-done.60 = bf16[4,144,1472]{2,1,0:T(8,128)(2,1)} collective-permute-done((bf16[4,144,1472]{2,1,0:T(8,128)(2,1)}, bf16[4,144,1472]{2,1,0:T(8,128)(2,1)}, u32[]{:S(2)}, u32[]{:S(2)}) %collective-permute-start.60) | collective-permute-done | bytes 1695776 | tf_op jit(solution)/shard_map/ppermute | solution.py:98
  581.6 24.1 %collective-permute-done.62 = bf16[4,144,1472]{2,1,0:T(8,128)(2,1)} collective-permute-done((bf16[4,144,1472]{2,1,0:T(8,128)(2,1)}, bf16[4,144,1472]{2,1,0:T(8,128)(2,1)}, u32[]{:S(2)}, u32[]{:S(2)}) %collective-permute-start.62) | collective-permute-done | bytes 1695776 | tf_op jit(solution)/shard_map/ppermute | solution.py:98
  616.1 6.7 collective-permute-done.63
  623.0 4.4 collective-permute-start.64
  627.4 5.7 collective-permute-done.64
  635.5 5.8 collective-permute-start.65
  649.0 44.1 %psum.15 = f32[2,3,1472]{2,0,1:T(2,128)S(1)} all-reduce(f32[2,3,1472]{2,0,1:T(2,128)S(1)} %broadcast_select_fusion.21), channel_id=1, replica_groups=mesh['section'=2,'line'=4,'plane'=4] {'section','line','plane'}, use_global_device_ids=true, to_apply=%region_23.24 | all-reduce | flops 8832 | bytes 70656 | tf_op jit(solution)/shard_map/psum | solution.py:351
  704.7 4.4 collective-permute-done.71
  713.4 76.6 %all-reduce.2.cloned.1.call-done = f32[384,1472]{0,1:T(8,128)} async-done(((f32[384,1472]{0,1:T(8,128)}), f32[384,1472]{0,1:T(8,128)}) %all-reduce.2.cloned.1.call-update) | async-done | bytes 2261008 | tf_op jit(solution)/shard_map/psum | solution.py:351
  (597 shorter events, 346.5 us)
Async XLA Ops:
  7.2 176.2 %all-gather.5.cloned.1.call-start = ((), (), s32[]{:S(2)}) async-start(), calls=%async_computation.5 | async-start | bytes 5160960 | tf_op jit(solution)/shard_map/all_gather | solution.py:226
  18.3 44.9 %collective-permute-start.18 = (bf16[112,1472]{1,0:T(8,128)(2,1)}, bf16[112,1472]{1,0:T(8,128)(2,1)S(1)}, u32[]{:S(2)}, u32[]{:S(2)}) collective-permute-start(bf16[112,1472]{1,0:T(8,128)(2,1)} %get-tuple-element.92), channel_id=1, source_target_pairs={{0,4},{1,20},{2,5},{3,21},{4,6},{5,22},{6,7},{7,23},{8,12},{9,28},... | collective-permute-start | bytes 989192 | tf_op jit(solution)/shard_map/ppermute | solution.py:222
  22.9 40.3 %collective-permute-start.17 = (bf16[112,1472]{1,0:T(8,128)(2,1)}, bf16[112,1472]{1,0:T(8,128)(2,1)}, u32[]{:S(2)}, u32[]{:S(2)}) collective-permute-start(bf16[112,1472]{1,0:T(8,128)(2,1)} %get-tuple-element.93), channel_id=1, source_target_pairs={{0,0},{1,16},{2,1},{3,17},{4,2},{5,18},{6,3},{7,19},{8,8},{9,24},{... | collective-permute-start | bytes 989192 | tf_op jit(solution)/shard_map/ppermute | solution.py:222
  28.1 36.2 %collective-permute-start.16 = (bf16[224,1472]{1,0:T(8,128)(2,1)}, bf16[224,1472]{1,0:T(8,128)(2,1)}, u32[]{:S(2)}, u32[]{:S(2)}) collective-permute-start(bf16[224,1472]{1,0:T(8,128)(2,1)} %dynamic-slice_bitcast_fusion.3), channel_id=1, source_target_pairs={{0,16},{16,0},{1,17},{17,1},{2,18},{18,2},{3,19},{19,3},{4,20},{20... | collective-permute-start | bytes 1978376 | tf_op jit(solution)/shard_map/ppermute | solution.py:101
  63.2 41.9 %collective-permute-start.6 = (bf16[4,144,1472]{2,1,0:T(8,128)(2,1)}, bf16[4,144,1472]{2,1,0:T(8,128)(2,1)}, u32[]{:S(2)}, u32[]{:S(2)}) collective-permute-start(bf16[4,144,1472]{2,1,0:T(8,128)(2,1)} %bitcast_dynamic-update-slice_fusion.4), channel_id=1, source_target_pairs={{0,1},{1,0},{2,3},{3,2},{4,5},{5,4},{6,7},{7,6},{8,9},{9,8},{10,11... | collective-permute-start | bytes 5087240 | tf_op jit(solution)/shard_map/ppermute | solution.py:98
  64.2 76.3 %collective-permute-start.7 = (bf16[4,144,1472]{2,1,0:T(8,128)(2,1)}, bf16[4,144,1472]{2,1,0:T(8,128)(2,1)}, u32[]{:S(2)}, u32[]{:S(2)}) collective-permute-start(bf16[4,144,1472]{2,1,0:T(8,128)(2,1)} %bitcast_dynamic-update-slice_fusion.4), channel_id=1, source_target_pairs={{0,2},{1,3},{2,0},{3,1},{4,6},{5,7},{6,4},{7,5},{8,10},{9,11},{10,... | collective-permute-start | bytes 5087240 | tf_op jit(solution)/shard_map/ppermute | solution.py:98
  67.4 243.8 %all-gather.7.cloned.1.call-start = ((), (), s32[]{:S(2)}) async-start(), calls=%async_computation.6 | async-start | bytes 5160960 | tf_op jit(solution)/shard_map/all_gather | solution.py:226
  67.5 74.7 %collective-permute-start.8 = (bf16[4,144,1472]{2,1,0:T(8,128)(2,1)}, bf16[4,144,1472]{2,1,0:T(8,128)(2,1)S(1)}, u32[]{:S(2)}, u32[]{:S(2)}) collective-permute-start(bf16[4,144,1472]{2,1,0:T(8,128)(2,1)} %bitcast_dynamic-update-slice_fusion.4), channel_id=1, source_target_pairs={{0,3},{1,2},{2,1},{3,0},{4,7},{5,6},{6,5},{7,4},{8,11},{9,10},{10,... | collective-permute-start | bytes 5087240 | tf_op jit(solution)/shard_map/ppermute | solution.py:98
  221.4 26.7 %collective-permute-start.22 = (bf16[256,1472]{0,1:T(8,128)(2,1)}, bf16[256,1472]{0,1:T(8,128)(2,1)}, u32[]{:S(2)}, u32[]{:S(2)}) collective-permute-start(bf16[256,1472]{0,1:T(8,128)(2,1)} %get-tuple-element.79), channel_id=1, source_target_pairs={{0,3},{1,2},{2,1},{3,0},{4,7},{5,6},{6,5},{7,4},{8,11},{9,10},{10,... | collective-permute-start | bytes 2261000 | tf_op jit(solution)/shard_map/ppermute | solution.py:98
  223.3 32.2 %collective-permute-start.21 = (bf16[256,1472]{0,1:T(8,128)(2,1)}, bf16[256,1472]{0,1:T(8,128)(2,1)}, u32[]{:S(2)}, u32[]{:S(2)}) collective-permute-start(bf16[256,1472]{0,1:T(8,128)(2,1)} %get-tuple-element.80), channel_id=1, source_target_pairs={{0,2},{1,3},{2,0},{3,1},{4,6},{5,7},{6,4},{7,5},{8,10},{9,11},{10,... | collective-permute-start | bytes 2261000 | tf_op jit(solution)/shard_map/ppermute | solution.py:98
  227.8 318.2 %reduce-scatter.5.cloned.1.call-start = ((), (), s32[]{:S(2)}) async-start(), calls=%async_computation.4 | async-start | bytes 5160960 | tf_op jit(solution)/shard_map/reduce_scatter | solution.py:273
  230.0 34.3 %collective-permute-start.39 = (bf16[256,1472]{0,1:T(8,128)(2,1)}, bf16[256,1472]{0,1:T(8,128)(2,1)S(1)}, u32[]{:S(2)}, u32[]{:S(2)}) collective-permute-start(bf16[256,1472]{0,1:T(8,128)(2,1)} %collective-permute-done.38), channel_id=1, source_target_pairs={{16,0},{17,1},{18,2},{19,3},{20,4},{21,5},{22,6},{23,7},{24,8},{25... | collective-permute-start | bytes 2261000 | tf_op jit(solution)/shard_map/ppermute | solution.py:101
  231.7 39.7 %collective-permute-start.43 = (bf16[256,1472]{0,1:T(8,128)(2,1)}, bf16[256,1472]{0,1:T(8,128)(2,1)}, u32[]{:S(2)}, u32[]{:S(2)}) collective-permute-start(bf16[256,1472]{0,1:T(8,128)(2,1)} %collective-permute-done.42), channel_id=1, source_target_pairs={{16,0},{17,1},{18,2},{19,3},{20,4},{21,5},{22,6},{23,7},{24,8},{25... | collective-permute-start | bytes 2261000 | tf_op jit(solution)/shard_map/ppermute | solution.py:101
  238.5 39.3 %collective-permute-start.41 = (bf16[256,1472]{0,1:T(8,128)(2,1)}, bf16[256,1472]{0,1:T(8,128)(2,1)}, u32[]{:S(2)}, u32[]{:S(2)}) collective-permute-start(bf16[256,1472]{0,1:T(8,128)(2,1)} %collective-permute-done.40), channel_id=1, source_target_pairs={{16,0},{17,1},{18,2},{19,3},{20,4},{21,5},{22,6},{23,7},{24,8},{25... | collective-permute-start | bytes 2261000 | tf_op jit(solution)/shard_map/ppermute | solution.py:101
  273.4 41.2 %collective-permute-start.25 = (bf16[256,1472]{0,1:T(8,128)(2,1)}, bf16[256,1472]{0,1:T(8,128)(2,1)}, u32[]{:S(2)}, u32[]{:S(2)}) collective-permute-start(bf16[256,1472]{0,1:T(8,128)(2,1)} %multiply_convert_fusion.4), channel_id=1, source_target_pairs={{16,17},{17,16},{18,19},{19,18},{20,21},{21,20},{22,23},{23,22},{2... | collective-permute-start | bytes 2261000 | tf_op jit(solution)/shard_map/ppermute | solution.py:98
  275.0 41.0 %collective-permute-start.29 = (bf16[256,1472]{0,1:T(8,128)(2,1)}, bf16[256,1472]{0,1:T(8,128)(2,1)}, u32[]{:S(2)}, u32[]{:S(2)}) collective-permute-start(bf16[256,1472]{0,1:T(8,128)(2,1)} %multiply_convert_fusion.4), channel_id=1, source_target_pairs={{16,19},{17,18},{18,17},{19,16},{20,23},{21,22},{22,21},{23,20},{2... | collective-permute-start | bytes 2261000 | tf_op jit(solution)/shard_map/ppermute | solution.py:98
  276.5 40.7 %collective-permute-start.24 = (bf16[256,1472]{0,1:T(8,128)(2,1)}, bf16[256,1472]{0,1:T(8,128)(2,1)}, u32[]{:S(2)}, u32[]{:S(2)}) collective-permute-start(bf16[256,1472]{0,1:T(8,128)(2,1)} %multiply_convert_fusion.4), channel_id=1, source_target_pairs={{16,0},{17,1},{18,2},{19,3},{20,4},{21,5},{22,6},{23,7},{24,8},{25... | collective-permute-start | bytes 2261000 | tf_op jit(solution)/shard_map/ppermute | solution.py:101
  279.9 38.9 %collective-permute-start.28 = (bf16[256,1472]{0,1:T(8,128)(2,1)}, bf16[256,1472]{0,1:T(8,128)(2,1)}, u32[]{:S(2)}, u32[]{:S(2)}) collective-permute-start(bf16[256,1472]{0,1:T(8,128)(2,1)} %collective-permute-done.27), channel_id=1, source_target_pairs={{16,0},{17,1},{18,2},{19,3},{20,4},{21,5},{22,6},{23,7},{24,8},{25... | collective-permute-start | bytes 2261000 | tf_op jit(solution)/shard_map/ppermute | solution.py:101
  406.0 289.9 %reduce-scatter.3.cloned.1.call-start = ((), (), s32[]{:S(2)}) async-start(), calls=%async_computation.3 | async-start | bytes 5160960 | tf_op jit(solution)/shard_map/reduce_scatter | solution.py:273
  430.8 28.0 %collective-permute-start.56 = (bf16[1024,1472]{0,1:T(8,128)(2,1)}, bf16[1024,1472]{0,1:T(8,128)(2,1)}, u32[]{:S(2)}, u32[]{:S(2)}) collective-permute-start(bf16[1024,1472]{0,1:T(8,128)(2,1)} %add_convert_fusion), channel_id=1, source_target_pairs={{16,0},{17,1},{18,2},{19,3},{20,4},{21,5},{22,6},{23,7},{24,8},{25... | collective-permute-start | bytes 9043976 | tf_op jit(solution)/shard_map/ppermute | solution.py:101
  437.7 101.4 %collective-permute-start.34 = (bf16[256,1472]{0,1:T(8,128)(2,1)}, bf16[256,1472]{0,1:T(8,128)(2,1)}, u32[]{:S(2)}, u32[]{:S(2)}) collective-permute-start(bf16[256,1472]{0,1:T(8,128)(2,1)} %get-tuple-element.75), channel_id=1, source_target_pairs={{16,17},{17,16},{18,19},{19,18},{20,21},{21,20},{22,23},{23,22},{2... | collective-permute-start | bytes 2261000 | tf_op jit(solution)/shard_map/ppermute | solution.py:98
  439.3 100.3 %collective-permute-start.36 = (bf16[256,1472]{0,1:T(8,128)(2,1)}, bf16[256,1472]{0,1:T(8,128)(2,1)}, u32[]{:S(2)}, u32[]{:S(2)}) collective-permute-start(bf16[256,1472]{0,1:T(8,128)(2,1)} %get-tuple-element.76), channel_id=1, source_target_pairs={{16,19},{17,18},{18,17},{19,16},{20,23},{21,22},{22,21},{23,20},{2... | collective-permute-start | bytes 2261000 | tf_op jit(solution)/shard_map/ppermute | solution.py:98
  473.0 27.6 %collective-permute-start.58 = (bf16[256,1472]{0,1:T(8,128)(2,1)}, bf16[256,1472]{0,1:T(8,128)(2,1)}, u32[]{:S(2)}, u32[]{:S(2)}) collective-permute-start(bf16[256,1472]{0,1:T(8,128)(2,1)} %get-tuple-element.71), channel_id=1, source_target_pairs={{0,2},{1,3},{2,0},{3,1},{4,6},{5,7},{6,4},{7,5},{8,10},{9,11},{10,... | collective-permute-start | bytes 2261000 | tf_op jit(solution)/shard_map/ppermute | solution.py:98
  481.1 308.9 %all-reduce.2.cloned.1.call-start = ((), (), s32[]{:S(2)}) async-start(), calls=%async_computation.2 | async-start | bytes 4521984 | tf_op jit(solution)/shard_map/psum | solution.py:351
  481.2 58.4 %collective-permute-start.35 = (bf16[256,1472]{0,1:T(8,128)(2,1)}, bf16[256,1472]{0,1:T(8,128)(2,1)}, u32[]{:S(2)}, u32[]{:S(2)}) collective-permute-start(bf16[256,1472]{0,1:T(8,128)(2,1)} %get-tuple-element.77), channel_id=1, source_target_pairs={{16,18},{17,19},{18,16},{19,17},{20,22},{21,23},{22,20},{23,21},{2... | collective-permute-start | bytes 2261000 | tf_op jit(solution)/shard_map/ppermute | solution.py:98
  536.1 45.5 %collective-permute-start.60 = (bf16[4,144,1472]{2,1,0:T(8,128)(2,1)}, bf16[4,144,1472]{2,1,0:T(8,128)(2,1)}, u32[]{:S(2)}, u32[]{:S(2)}) collective-permute-start(bf16[4,144,1472]{2,1,0:T(8,128)(2,1)} %get-tuple-element.46), channel_id=1, source_target_pairs={{0,1},{1,0},{2,3},{3,2},{4,5},{5,4},{6,7},{7,6},{8,9},{9,8},{10,11... | collective-permute-start | bytes 5087240 | tf_op jit(solution)/shard_map/ppermute | solution.py:98
  537.6 68.1 %collective-permute-start.62 = (bf16[4,144,1472]{2,1,0:T(8,128)(2,1)}, bf16[4,144,1472]{2,1,0:T(8,128)(2,1)}, u32[]{:S(2)}, u32[]{:S(2)}) collective-permute-start(bf16[4,144,1472]{2,1,0:T(8,128)(2,1)} %get-tuple-element.47), channel_id=1, source_target_pairs={{0,3},{1,2},{2,1},{3,0},{4,7},{5,6},{6,5},{7,4},{8,11},{9,10},{10,... | collective-permute-start | bytes 5087240 | tf_op jit(solution)/shard_map/ppermute | solution.py:98
  539.1 68.3 %collective-permute-start.61 = (bf16[4,144,1472]{2,1,0:T(8,128)(2,1)}, bf16[4,144,1472]{2,1,0:T(8,128)(2,1)}, u32[]{:S(2)}, u32[]{:S(2)}) collective-permute-start(bf16[4,144,1472]{2,1,0:T(8,128)(2,1)} %get-tuple-element.48), channel_id=1, source_target_pairs={{0,2},{1,3},{2,0},{3,1},{4,6},{5,7},{6,4},{7,5},{8,10},{9,11},{10,... | collective-permute-start | bytes 5087240 | tf_op jit(solution)/shard_map/ppermute | solution.py:98
  547.7 157.0 %collective-permute-start.73 = (bf16[112,1472]{1,0:T(8,128)(2,1)}, bf16[112,1472]{1,0:T(8,128)(2,1)}, u32[]{:S(2)}, u32[]{:S(2)}) collective-permute-start(bf16[112,1472]{1,0:T(8,128)(2,1)} %slice_bitcast_fusion.1), channel_id=1, source_target_pairs={{4,16},{20,17},{5,18},{21,19},{6,20},{22,21},{7,22},{23,23},{12,24... | collective-permute-start | bytes 989192 | tf_op jit(solution)/shard_map/ppermute | solution.py:367
  549.1 155.6 %collective-permute-start.72 = (bf16[112,1472]{1,0:T(8,128)(2,1)}, bf16[112,1472]{1,0:T(8,128)(2,1)}, u32[]{:S(2)}, u32[]{:S(2)}) collective-permute-start(bf16[112,1472]{1,0:T(8,128)(2,1)} %slice_bitcast_fusion.1), channel_id=1, source_target_pairs={{0,16},{16,17},{1,18},{17,19},{2,20},{18,21},{3,22},{19,23},{8,24}... | collective-permute-start | bytes 989192 | tf_op jit(solution)/shard_map/ppermute | solution.py:367
  635.5 58.3 %collective-permute-start.65 = (bf16[144,1472]{1,0:T(8,128)(2,1)}, bf16[144,1472]{1,0:T(8,128)(2,1)}, u32[]{:S(2)}, u32[]{:S(2)}) collective-permute-start(bf16[144,1472]{1,0:T(8,128)(2,1)} %get-tuple-element.85), channel_id=1, source_target_pairs={{0,4},{4,8},{8,12},{1,5},{5,9},{9,13},{2,6},{6,10},{10,14},{3,7},{... | collective-permute-start | bytes 1271816 | tf_op jit(solution)/shard_map/ppermute | solution.py:105
  645.6 48.1 %collective-permute-start.68 = (bf16[144,1472]{1,0:T(8,128)(2,1)}, bf16[144,1472]{1,0:T(8,128)(2,1)}, u32[]{:S(2)}, u32[]{:S(2)}) collective-permute-start(bf16[144,1472]{1,0:T(8,128)(2,1)} %fusion.44), channel_id=1, source_target_pairs={{4,0},{8,4},{12,8},{5,1},{9,5},{13,9},{6,2},{10,6},{14,10},{7,3},{... | collective-permute-start | bytes 1271816 | tf_op jit(solution)/shard_map/ppermute | solution.py:105
  (183 other events, 2168.5 us)
Sparse Core Ops, SparseCore 0:
  67.6 81.1 all-gather.4
  227.9 83.2 all-gather.6
  406.1 73.3 reduce-scatter.4
  481.7 83.1 reduce-scatter.2
  649.2 140.7 all-reduce.1

commit v2 on v1

v2 whole, which is shorter than its diff:
```python
import functools

import jax
import jax.numpy as jnp
from jax import lax
from jax.experimental import pallas as pl
from jax.experimental.pallas import tpu as pltpu
from jax.sharding import Mesh, PartitionSpec as P

HEADS = 6
HEAD_DIM = 64
PLANE = 4
SCALE = HEAD_DIM ** (-0.5)

epsilon = 1e-06
masked_value = -1000000000.0
AXES = ("section", "line", "plane")
bf16 = jnp.bfloat16
f32 = jnp.float32


def nn(a, b):
    return lax.dot_general(a, b, (((1,), (0,)), ((), ())), preferred_element_type=f32)


def nt(a, b):
    return lax.dot_general(a, b, (((1,), (1,)), ((), ())), preferred_element_type=f32)


def tn(a, b):
    return lax.dot_general(a, b, (((0,), (0,)), ((), ())), preferred_element_type=f32)


def permute(block, axes, route):
    shape = block.shape
    if block.ndim == 2 and shape[0] % 8 == 0:
        block = block.reshape(shape[0] // 8, 8, shape[1])
    return lax.ppermute(block, axes, route).reshape(shape)


def rounded(value):
    return lax.reduce_precision(value, 8, 7).astype(bf16)


def rms_norm(inputs, gain_row):
    return inputs * lax.rsqrt(jnp.mean(inputs * inputs, -1, keepdims=True) + epsilon) * gain_row


def rms_back(inputs, gain_row, upstream):
    scale = lax.rsqrt(jnp.mean(inputs * inputs, -1, keepdims=True) + epsilon)
    normed = inputs * scale
    weighted = upstream * gain_row
    grad = (weighted - normed * jnp.mean(weighted * normed, -1, keepdims=True)) * scale
    return grad, jnp.sum(upstream * normed, 0, keepdims=True)


def gelu_parts(gate):
    slope = (2.0 / jnp.pi) ** 0.5
    cube = 0.044715 * gate * gate
    bent = jnp.tanh(slope * gate * (1.0 + cube))
    half = 0.5 * (1.0 + bent)
    return half * gate, half + 0.5 * gate * (1.0 - bent * bent) * slope * (1.0 + 3.0 * cube)


def whole(shape):
    return pl.BlockSpec(shape, lambda step: (0,) * len(shape))


def call(kernel, outputs, *args, scratch=(), steps=1, specs=None, time_us=5, ties=()):
    specs = specs or {}
    in_specs = [
        specs.get(i)
        or (pl.BlockSpec(memory_space=pltpu.SMEM) if a.dtype == jnp.int32 else whole(a.shape))
        for i, a in enumerate(args)
    ]
    in_specs += [pl.BlockSpec(memory_space=pl.ANY)] * len(ties)
    first, after = len(args), len(args) + len(ties)
    out_shape = tuple(jax.ShapeDtypeStruct(output[0], output[1]) for output in outputs)
    return pl.pallas_call(
        lambda *refs: kernel(*refs[:first], *refs[after:]),
        grid=(steps,),
        out_shape=out_shape,
        in_specs=in_specs,
        out_specs=tuple(output[2] if len(output) > 2 else whole(output[0]) for output in outputs),
        scratch_shapes=list(scratch),
        compiler_params=pltpu.CompilerParams(vmem_limit_bytes=56 * 1024 * 1024),
        cost_estimate=pl.CostEstimate(
            flops=int(time_us * 8e8), bytes_accessed=int(time_us * 2.5e6), transcendentals=0
        ),
    )(*args, *ties)


def chances_of(queries, keys, allowed):
    scores = jnp.where(allowed > 0, tn(queries, keys) * SCALE, masked_value)
    exponent = jnp.exp(scores - jnp.max(scores, -1, keepdims=True))
    return exponent / jnp.sum(exponent, -1, keepdims=True)


def attend_into(context_ref, query_ref, key_ref, value_ref, allowed_ref, starts=(0, 0, 0)):
    rows, length, _ = allowed_ref.shape
    for row in range(rows):
        columns = slice(row * length, (row + 1) * length)
        for head in range(HEADS):
            q, k, v = (
                ref[start + head * HEAD_DIM : start + (head + 1) * HEAD_DIM, columns]
                for ref, start in zip((query_ref, key_ref, value_ref), starts)
            )
            weights = chances_of(q, k, allowed_ref[row]).astype(bf16)
            context_ref[head * HEAD_DIM : (head + 1) * HEAD_DIM, columns] = nt(v, weights).astype(bf16)


def attend_back_into(grads_ref, query_ref, key_ref, value_ref, allowed_ref, upstream, starts=(0, 0, 0)):
    rows, length, _ = allowed_ref.shape
    inner = HEADS * HEAD_DIM
    for row in range(rows):
        columns = slice(row * length, (row + 1) * length)
        for head in range(HEADS):
            first = head * HEAD_DIM
            q, k, v = (
                ref[start + first : start + first + HEAD_DIM, columns]
                for ref, start in zip((query_ref, key_ref, value_ref), starts)
            )
            g = upstream[first : first + HEAD_DIM, columns]
            chances = chances_of(q, k, allowed_ref[row])
            weight_grad = tn(g, v)
            score_grad = (
                chances * (weight_grad - jnp.sum(weight_grad * chances, -1, keepdims=True))
            ).astype(bf16)
            grads = (nt(k, score_grad) * SCALE, nn(q, score_grad) * SCALE, nn(g, chances.astype(bf16)))
            for number, grad in enumerate(grads):
                at = number * inner + first
                grads_ref[at : at + HEAD_DIM, columns] = grad.astype(bf16)


def added(refs):
    total = refs[0][...].astype(f32)
    for ref in refs[1:]:
        total = total + ref[...].astype(f32)
    return total


def split_rows(section, value, kept_ref, sent_ref):
    length = kept_ref.shape[0]
    mine, other = value[:length], value[length:]
    kept_ref[...] = jnp.where(section == 0, mine, other)
    sent_ref[...] = jnp.where(section == 0, other, mine)


def self_forward_kernel(section_ref, projected_ref, allowed_ref, inputs_ref, out_w_ref, context_ref, kept_ref, sent_ref):
    inner = context_ref.shape[0]
    attend_into(context_ref, projected_ref, projected_ref, projected_ref, allowed_ref, (0, inner, 2 * inner))
    first_sum = inputs_ref[...] + tn(context_ref[...], out_w_ref[...])
    split_rows(section_ref[0], first_sum, kept_ref, sent_ref)


def first_norm_kernel(section_ref, kept_ref, got_ref, gains_e_ref, gains_d_ref, first_e_ref, first_d_ref, normed_e_ref, normed_d_ref):
    is_encoder = section_ref[0] == 0
    first_e = jnp.where(is_encoder, kept_ref[...], got_ref[...])
    first_d = jnp.where(is_encoder, got_ref[...], kept_ref[...])
    first_e_ref[...] = first_e
    first_d_ref[...] = first_d
    normed_e_ref[...] = rms_norm(first_e, gains_e_ref[1:2]).astype(bf16)
    normed_d_ref[...] = rms_norm(first_d, gains_d_ref[1:2]).astype(bf16)


def joined(refs, scratch):
    length = refs[0].shape[0]
    for k, ref in enumerate(refs):
        scratch[k * length : (k + 1) * length] = ref[...]
    return scratch[...]


def feed_specs(lines, padded, width):
    half = lines // 2
    return [
        pl.BlockSpec((1, padded, width), lambda step: (step, 0, 0)),
        pl.BlockSpec((1, padded, width), lambda step: (half + step, 0, 0)),
        pl.BlockSpec((2, padded // 2, width), lambda step: (step, 2, 0)),
    ]


def stacked(weights):
    wide = jnp.concatenate([w[0] for pack in weights for w in pack[:2]], 0)
    narrow = jnp.concatenate([half for pack in weights for half in (pack[2][0], pack[2][1])], 0)
    return wide, narrow


def sum_over_steps(total, scratch, out_ref, prior_ref=None):
    step = pl.program_id(0)

    @pl.when(step == 0)
    def _():
        scratch[...] = total if prior_ref is None else total + prior_ref[...].astype(f32)

    @pl.when(step > 0)
    def _():
        scratch[...] += total

    @pl.when(step == pl.num_programs(0) - 1)
    def _():
        out_ref[...] = scratch[...].astype(bf16)


def join_once(refs, scratch):
    @pl.when(pl.program_id(0) == 0)
    def _():
        joined(refs, scratch)


def cut(array, count):
    rows = array.shape[0] // count
    return [array[i * rows : (i + 1) * rows] for i in range(count)]


def feed_forward_kernel(priors, *refs):
    streams, pack, refs = refs[:4], refs[4:7], refs[7:]
    prior_refs, (value_ref, slope_ref, hidden_ref, part_ref, x_ref, part_sum) = refs[:priors], refs[priors:]
    join_once(streams, x_ref)
    wide, narrow = stacked([pack])
    gate, up = cut(nt(wide, x_ref[...]), 2)
    value, slope = gelu_parts(gate)
    value_ref[0, 0] = value.astype(bf16)
    slope_ref[0, 0] = (slope * up).astype(bf16)
    hidden = (value * up).astype(bf16)
    hidden_ref[0, 0] = hidden
    sum_over_steps(tn(hidden, narrow), part_sum, part_ref, *prior_refs)


def feed_back_kernel(*refs):
    outputs, packs, saved = refs[:4], (refs[4:7], refs[7:10]), refs[10:14]
    grads_refs, (back_ref, output_ref, back_sum) = refs[14:16], refs[16:]
    join_once(outputs, output_ref)
    wide, narrow = stacked(packs)
    grads = []
    for core, hidden_grad in enumerate(cut(nt(narrow, output_ref[...]), 2)):
        value_ref, slope_ref = saved[2 * core : 2 * core + 2]
        grads.append((hidden_grad * slope_ref[0, 0].astype(f32)).astype(bf16))
        grads.append((hidden_grad * value_ref[0, 0].astype(f32)).astype(bf16))
        grads_refs[core][0, 0] = grads[-2]
        grads_refs[core][0, 1] = grads[-1]
    sum_over_steps(tn(jnp.concatenate(grads, 0), wide), back_sum, back_ref)


def feed_both_kernel(priors, *refs):
    streams, outputs, pack, refs = refs[:4], refs[4:8], refs[8:11], refs[11:]
    prior_refs, refs = refs[:priors], refs[priors:]
    hidden_ref, grads_ref, part_ref, back_ref, x_ref, output_ref, part_sum, back_sum = refs
    join_once(streams, x_ref)
    join_once(outputs, output_ref)
    wide, narrow = stacked([pack])
    gate, up = cut(nt(wide, x_ref[...]), 2)
    hidden_grad = nt(narrow, output_ref[...])
    value, slope = gelu_parts(gate)
    hidden = (value * up).astype(bf16)
    hidden_ref[0, 0] = hidden
    grads = [(hidden_grad * (slope * up)).astype(bf16), (hidden_grad * value).astype(bf16)]
    grads_ref[0, 0] = grads[0]
    grads_ref[0, 1] = grads[1]
    sum_over_steps(tn(jnp.concatenate(grads, 0), wide), back_sum, back_ref, *prior_refs[1:])
    sum_over_steps(tn(hidden, narrow), part_sum, part_ref, *prior_refs[:1])


def feed_grads_kernel(*refs):
    streams, outputs, grads_refs, hidden_refs = refs[:4], refs[4:8], refs[8:10], refs[10:12]
    own_ref, other_ref, x_ref, output_ref = refs[12:]
    step, steps = pl.program_id(0), pl.num_programs(0)
    padded, rows = grads_refs[0].shape[2:]
    join_once(streams, x_ref)
    join_once(outputs, output_ref)
    for grads_ref, hidden_ref, ref in zip(grads_refs, hidden_refs, (own_ref, other_ref)):
        wide = cut(nn(grads_ref[...].reshape(2 * padded, rows), x_ref[...]), 2)
        narrow = cut(nn(hidden_ref[0, 0], output_ref[...]), 2)
        ref[step, :padded] = wide[0].astype(bf16)
        ref[steps + step, :padded] = wide[1].astype(bf16)
        ref[2 * step, padded:] = narrow[0].astype(bf16)
        ref[2 * step + 1, padded:] = narrow[1].astype(bf16)


def middle_kernel(*refs):
    parts = refs[:4]
    first_e_ref, first_d_ref, normed_d_ref, gains_e_ref, gains_d_ref, cross_e_ref, cross_d_ref, allowed_ref = refs[4:12]
    second_e_ref, normed_e_ref, queries_ref, states_ref, context_ref, second_d_ref, normed_last_ref = refs[12:]
    inner = context_ref.shape[0]
    queries_ref[...] = nt(cross_d_ref[:inner], normed_d_ref[...]).astype(bf16)
    second_e = first_e_ref[...] + added(parts)
    second_e_ref[...] = second_e
    normed = rms_norm(second_e, gains_e_ref[2:3]).astype(bf16)
    normed_e_ref[...] = normed
    states_ref[...] = nt(cross_e_ref[...], normed).astype(bf16)
    attend_into(context_ref, queries_ref, states_ref, states_ref, allowed_ref, (0, 0, inner))
    second_d = first_d_ref[...] + tn(context_ref[...], cross_d_ref[inner:])
    second_d_ref[...] = second_d
    normed_last_ref[...] = rms_norm(second_d, gains_d_ref[2:3]).astype(bf16)


def middle_back_kernel(*refs):
    parts = refs[:4]
    second_d_ref, second_e_ref, cotangent_d_ref, cotangent_e_ref, gains_d_ref, gains_e_ref = refs[4:10]
    cross_d_ref, cross_e_ref, queries_ref, states_ref, allowed_ref = refs[10:15]
    stream_d_ref, branch_ref, grads_ref, stream_e_ref, sent_ref, gain_d_ref, gain_e_ref = refs[15:]
    inner = queries_ref.shape[0]
    input_grad, gain_d_ref[...] = rms_back(second_d_ref[...], gains_d_ref[2:3], added(parts))
    stream_d = cotangent_d_ref[...].astype(f32) + input_grad
    stream_d_ref[...] = stream_d
    branch = stream_d.astype(bf16)
    branch_ref[...] = branch
    context_grad = nt(cross_d_ref[inner:], branch).astype(bf16)
    attend_back_into(grads_ref, queries_ref, states_ref, states_ref, allowed_ref, context_grad, (0, 0, inner))
    final_grad = tn(grads_ref[inner:], cross_e_ref[...])
    input_grad, gain_e_ref[...] = rms_back(second_e_ref[...], gains_e_ref[2:3], final_grad)
    stream_e = cotangent_e_ref[...].astype(f32) + input_grad
    stream_e_ref[...] = stream_e
    sent_ref[...] = stream_e.astype(bf16)


def first_back_d_kernel(grads_ref, cross_d_ref, first_d_ref, gains_d_ref, stream_ref, out_ref, gain_ref):
    inner = cross_d_ref.shape[0] // 2
    upstream = tn(grads_ref[:inner], cross_d_ref[:inner])
    input_grad, gain_ref[...] = rms_back(first_d_ref[...], gains_d_ref[1:2], upstream)
    out_ref[...] = stream_ref[...] + input_grad


def first_back_e_kernel(*refs):
    parts = refs[:4]
    section_ref, first_e_ref, gains_e_ref, stream_ref, stream_d_ref, kept_ref, sent_ref, gain_ref = refs[4:]
    input_grad, gain_ref[...] = rms_back(first_e_ref[...], gains_e_ref[1:2], added(parts))
    stream_e = stream_ref[...] + input_grad
    is_encoder = section_ref[0] == 0
    kept_ref[...] = jnp.where(is_encoder, stream_e, stream_d_ref[...])
    sent_ref[...] = jnp.where(is_encoder, stream_d_ref[...], stream_e)


def self_back_kernel(section_ref, kept_ref, got_ref, out_w_ref, projected_ref, allowed_ref, stream_ref, branch_ref, grads_ref):
    is_encoder = section_ref[0] == 0
    inner, length = out_w_ref.shape[0], kept_ref.shape[0]
    stream_ref[:length] = jnp.where(is_encoder, kept_ref[...], got_ref[...])
    stream_ref[length:] = jnp.where(is_encoder, got_ref[...], kept_ref[...])
    branch = stream_ref[...].astype(bf16)
    branch_ref[...] = branch
    context_grad = nt(out_w_ref[...], branch).astype(bf16)
    attend_back_into(
        grads_ref, projected_ref, projected_ref, projected_ref, allowed_ref, context_grad, (0, inner, 2 * inner)
    )


def table_kernel(grads_ref, in_w_ref, inputs_ref, gain_ref, stream_ref, one_hot_ref, table_ref, gain_grad_ref):
    upstream = tn(grads_ref[...], in_w_ref[...])
    input_grad, gain_grad_ref[...] = rms_back(inputs_ref[...], gain_ref[...], upstream)
    table_ref[...] = tn(one_hot_ref[...], (stream_ref[...] + input_grad).astype(bf16)).astype(bf16)


def in_grad_kernel(*refs):
    grads, streams, out_ref = refs[:4], refs[4:8], refs[8]
    total = nn(grads[0][...], streams[0][...])
    for grad, stream in zip(grads[1:], streams[1:]):
        total = total + nn(grad[...], stream[...])
    out_ref[...] = total.astype(bf16)


def cross_grads_kernel(section_ref, grads_ref, normed_e_ref, normed_d_ref, context_ref, branch_ref, kept_ref, sent_ref):
    inner = context_ref.shape[0]
    is_encoder = section_ref[0] == 0
    grad_e = nn(grads_ref[inner:], normed_e_ref[...])
    grad_first = nn(grads_ref[:inner], normed_d_ref[...])
    grad_second = nn(context_ref[...], branch_ref[...])
    for start, grad_d in ((0, grad_first), (inner, grad_second)):
        part_e = grad_e[start : start + inner]
        kept_ref[start : start + inner] = jnp.where(is_encoder, part_e, grad_d).astype(bf16)
        sent_ref[start : start + inner] = jnp.where(is_encoder, grad_d, part_e).astype(bf16)


def build(lines):
    devices = lines * PLANE

    def place(section, line, plane):
        return section * devices + line * PLANE + plane

    def hop(block, offset):
        route = [
            (place(s, z, j), place(s, z, j ^ offset))
            for s in range(2)
            for z in range(lines)
            for j in range(PLANE)
        ]
        return permute(block, AXES, route)

    def swap(block):
        return permute(block, "section", [(0, 1), (1, 0)])

    narrow_route = []
    for core in range(2):
        for block in range(devices):
            target = (block % 2, 2 * (block // 8) + core, (block % 8) // 2)
            narrow_route.append((core * devices + block, place(*target)))

    def at(array, index, axis=0):
        return lax.dynamic_index_in_dim(array, index, axis, False)

    def ordered(own, others, index, axis=0):
        count = len(others) + 1
        shape = own.shape[:axis] + (count,) + own.shape[axis:]
        out = jnp.zeros(shape, own.dtype)
        for where_to, piece in [(index, own)] + others:
            out = lax.dynamic_update_index_in_dim(out, piece, where_to, axis)
        return out

    def sum_line(block):
        if lines & (lines - 1):
            return rounded(lax.psum(block.astype(f32), "line"))
        distance = 1
        while distance < lines:
            route = [(z, z ^ distance) for z in range(lines)]
            block = rounded(block.astype(f32) + permute(block, "line", route).astype(f32))
            distance *= 2
        return block

    def in_plane(blocks, axis=0):
        j = lax.axis_index("plane")
        return ordered(blocks[0], [(j ^ k, blocks[k]) for k in range(1, PLANE)], j, axis)

    def gather_plane(block, axis=0):
        return in_plane(spread(block), axis)

    def scatter_line(partial):
        if lines > 8:
            return lax.psum_scatter(partial, "line", scatter_dimension=0).astype(f32)
        z = lax.axis_index("line")
        total = at(partial, z).astype(f32)
        for step in range(1, lines):
            for distance in (step, -step):
                route = [(a, a + distance) for a in range(lines) if 0 <= a + distance < lines]
                sent = at(partial, jnp.clip(z + distance, 0, lines - 1))
                total = total + permute(sent, "line", route).astype(f32)
        return total

    def scatter_plane(parts):
        j = lax.axis_index("plane")
        total = at(parts, j).astype(f32)
        for k in range(1, PLANE):
            total = total + hop(at(parts, j ^ k), k).astype(f32)
        return total

    def spread(block):
        return [block] + [hop(block, k) for k in range(1, PLANE)]

    def collected(partial):
        parts = partial.reshape((PLANE, -1) + partial.shape[1:])
        return [parts[0]] + [hop(parts[k], k) for k in range(1, PLANE)]

    def per_device(
        byte_codes,
        encoder_segments,
        target_segments,
        embedding,
        attention_in,
        attention_out,
        widen_weight,
        narrow_weight,
        cross_first,
        cross_second,
        norm_gains,
        cotangent,
    ):
        section = lax.axis_index("section")
        j = lax.axis_index("plane")
        is_encoder = section == 0
        section_scalar = section.astype(jnp.int32).reshape(1)
        inner = cross_first.shape[2] * devices
        vocabulary, width = embedding.shape
        rows, length = encoder_segments.shape
        tokens = rows * length

        def together(*values):
            return lax.optimization_barrier(values)

        def by_section(mine, other):
            return jnp.where(is_encoder, mine, other), jnp.where(is_encoder, other, mine)

        def in_order(mine, other):
            return jnp.concatenate(by_section(mine, other), 0)

        in_cols = attention_in.shape[2]
        cross_cols = cross_first.shape[2]
        column, codes = together(
            jnp.concatenate([attention_in[0].T, attention_out[0], cross_first[0].T, cross_second[0].T], 0),
            byte_codes[0].reshape(tokens),
        )
        column = lax.all_gather(column, "line", axis=0)
        in_column = column[:, :in_cols].reshape(-1, width)

        widen_half = widen_weight.shape[2] // 2
        narrow_half = narrow_weight.shape[1] // 2
        padded_narrow = -(-narrow_half // 16) * 16
        padded_widen = 2 * padded_narrow

        def widened(block):
            return jnp.pad(block, ((0, 0),) * (block.ndim - 2) + ((0, padded_narrow - narrow_half), (0, 0)))

        narrow_parts = widened(narrow_weight[0].reshape(2, narrow_half, width))
        narrow_e, narrow_d = by_section(at(narrow_parts, section), swap(at(narrow_parts, 1 - section)))
        moved = permute(jnp.concatenate([narrow_e, narrow_d], 0), AXES, narrow_route)
        widen_parts = widened(widen_weight[0].T.reshape(2, 2, narrow_half, width)).reshape(
            2, padded_widen, width
        )
        widen_e, widen_d = by_section(at(widen_parts, section), swap(at(widen_parts, 1 - section)))

        one_hot = (
            codes[:, None] == lax.broadcasted_iota(jnp.int32, (tokens, vocabulary), 1)
        ).astype(bf16)
        inputs = nn(one_hot, embedding)
        own_segments = jnp.where(is_encoder, encoder_segments, target_segments)
        earlier = lax.broadcasted_iota(jnp.int32, (length, length), 1) <= lax.broadcasted_iota(
            jnp.int32, (length, length), 0
        )
        allowed = (
            (own_segments[:, :, None] == own_segments[:, None, :]) & (earlier | is_encoder)[None]
        ).astype(f32)
        encoder_row, target_row = at(encoder_segments, section), at(target_segments, section)
        cross_allowed = (target_row[:, None] == encoder_row[None, :]).astype(f32)[None]

        own_gains = norm_gains[0]
        received = swap(jnp.concatenate([at(cotangent[0], 1 - section), own_gains], 0))
        cotangent_e, cotangent_d = by_section(at(cotangent[0], section), received[:length])
        gains_e, gains_d = (g.astype(f32) for g in by_section(own_gains, received[length:]))
        gain_self = own_gains[:1].astype(f32)

        normed_plane = spread(rms_norm(inputs, gain_self).astype(bf16))
        moved, *normed_plane = together(moved, *normed_plane)
        pack_e, pack_d = lax.optimization_barrier(
            (
                jnp.concatenate([widen_e, moved[:padded_narrow]], 0),
                jnp.concatenate([widen_d, moved[padded_narrow:]], 0),
            )
        )
        own_e = lax.all_gather(pack_e, "line", axis=0)
        own_d = lax.all_gather(pack_d, "line", axis=0)

        projected_parts = [
            nt(in_column, block).astype(bf16).reshape(lines, in_cols, tokens) for block in normed_plane
        ]
        projected = ordered(
            projected_parts[0],
            [(j ^ k, hop(projected_parts[k], k)) for k in range(1, PLANE)],
            j,
            1,
        ).reshape(3 * inner, tokens)
        out_w = gather_plane(column[:, in_cols : in_cols + cross_cols], 1).reshape(-1, width)
        row_f32, row_bf16 = ((length, width), f32), ((length, width), bf16)
        context, first_kept, first_sent = call(
            self_forward_kernel,
            (((inner, tokens), bf16), row_f32, row_f32),
            section_scalar,
            projected,
            allowed,
            inputs,
            out_w,
        )

        first_e, first_d, normed_first, normed_cross = call(
            first_norm_kernel,
            (row_f32, row_f32, row_bf16, row_bf16),
            section_scalar,
            first_kept,
            swap(first_sent),
            gains_e,
            gains_d,
        )
        stream_e = spread(normed_first)
        cross_rows, *stream_e = together(column[:, in_cols + cross_cols :], *stream_e)
        cross_pieces = spread(cross_rows)
        group = PLANE * length
        group_bf16 = ((group, width), bf16)
        steps = lines // 2
        pack_shape = (lines, padded_widen + padded_narrow, width)
        pack_specs = feed_specs(lines, padded_widen, width)
        joined_scratch = pltpu.VMEM((group, width), bf16)
        sum_scratch = pltpu.VMEM((group, width), f32)

        def unit(*middle):
            block = (1,) + middle + (padded_widen, group)
            return (
                (steps,) + block[1:],
                bf16,
                pl.BlockSpec(block, lambda step: (step,) + (0,) * (len(block) - 1)),
            )

        def with_packs(first, *packs):
            specs = {first + 3 * i + k: pack_specs[k] for i in range(len(packs)) for k in range(3)}
            return [pack for pack in packs for _ in range(3)], specs

        def feed_forward(stream, pack, *priors):
            packs, specs = with_packs(4, pack)
            return call(
                functools.partial(feed_forward_kernel, len(priors)),
                (unit(1), unit(1), unit(1), group_bf16),
                *stream,
                *packs,
                *priors,
                scratch=(joined_scratch, sum_scratch),
                steps=steps,
                specs=specs,
            )

        def feed_back(output_grad, packs, saved, ties):
            packs, specs = with_packs(4, *packs)
            specs.update({10 + i: unit(1)[2] for i in range(4)})
            return call(
                feed_back_kernel,
                (unit(2), unit(2), group_bf16),
                *output_grad,
                *packs,
                *saved,
                scratch=(joined_scratch, sum_scratch),
                steps=steps,
                specs=specs,
                time_us=8,
                ties=ties,
            )

        def feed_both(stream, output_grad, pack, *priors, ties=()):
            packs, specs = with_packs(8, pack)
            return call(
                functools.partial(feed_both_kernel, len(priors)),
                (unit(1), unit(2), group_bf16, group_bf16),
                *stream,
                *output_grad,
                *packs,
                *priors,
                scratch=(joined_scratch, joined_scratch, sum_scratch, sum_scratch),
                steps=steps,
                specs=specs,
                time_us=8,
                ties=ties,
            )

        def feed_grads(stream, output_grad, grads, hidden):
            specs = {8 + i: unit(2)[2] for i in range(2)}
            specs.update({10 + i: unit(1)[2] for i in range(2)})
            own, other = call(
                feed_grads_kernel,
                ((pack_shape, bf16), (pack_shape, bf16)),
                *stream,
                *output_grad,
                *grads,
                *hidden,
                scratch=(joined_scratch, joined_scratch),
                steps=steps,
                specs=specs,
                time_us=9,
            )
            return (own.astype(f32) + swap(other).astype(f32)).astype(bf16)

        own_e, *stream_e = together(own_e, *stream_e)
        other_e = swap(own_e)
        value_own, slope_own, hidden_own, part_own = feed_forward(stream_e, own_e)
        value_other, slope_other, hidden_other, part_e = feed_forward(stream_e, other_e, part_own)

        part_e, *cross_pieces = together(part_e, *cross_pieces)
        cross_w = in_plane(cross_pieces, 1).reshape(devices, 2, cross_cols, width).swapaxes(0, 1)
        cross_w = cross_w.reshape(-1, width)
        cross_e, cross_d = by_section(cross_w, swap(cross_w))
        cotangent_d, cross_w = together(cotangent_d, cross_w)
        output_grad_d = spread(cotangent_d)

        second_e, normed_final, cross_queries, states, cross_context, second_d, normed_last = call(
            middle_kernel,
            (
                row_f32,
                row_bf16,
                ((inner, length), bf16),
                ((2 * inner, length), bf16),
                ((inner, length), bf16),
                row_f32,
                row_bf16,
            ),
            *collected(part_e),
            first_e,
            first_d,
            normed_cross,
            gains_e,
            gains_d,
            cross_e,
            cross_d,
            cross_allowed,
        )

        stream_d = spread(normed_last)
        own_d, in_rows, *stream_d = together(own_d, column[:, :in_cols], *stream_d)
        in_pieces = [in_rows, hop(in_rows, 1), hop(in_rows, 2)]
        other_d = swap(own_d)
        hidden_own_d, grads_own_d, part_d, back_d = feed_both(stream_d, output_grad_d, own_d)
        hidden_other_d, grads_other_d, part_d, back_d = feed_both(
            stream_d, output_grad_d, other_d, part_d, back_d, ties=in_pieces[1:]
        )
        gain_shape = ((1, width), f32)
        stream_two_d, cross_branch, cross_grads, stream_two_e, sent_e, gain_two_d, gain_two_e = call(
            middle_back_kernel,
            (row_f32, row_bf16, ((3 * inner, length), bf16), row_f32, row_bf16, gain_shape, gain_shape),
            *collected(back_d),
            second_d,
            second_e,
            cotangent_d,
            cotangent_e,
            gains_d,
            gains_e,
            cross_d,
            cross_e,
            cross_queries,
            states,
            cross_allowed,
        )

        output_grad_e = spread(sent_e)
        feed_sum_d = feed_grads(
            stream_d, output_grad_d, (grads_own_d, grads_other_d), (hidden_own_d, hidden_other_d)
        )
        grads_own_e, grads_other_e, back_e = feed_back(
            output_grad_e,
            (own_e, other_e),
            (value_own, slope_own, value_other, slope_other),
            (feed_sum_d,),
        )

        stream_one_d, gain_one_d = call(
            first_back_d_kernel,
            (row_f32, gain_shape),
            cross_grads,
            cross_d,
            first_d,
            gains_d,
            stream_two_d,
        )
        feed_sum_e = feed_grads(
            stream_e, output_grad_e, (grads_own_e, grads_other_e), (hidden_own, hidden_other)
        )
        summed_d = lax.psum_scatter(feed_sum_d, "line", scatter_dimension=0)
        feed_sum_e, summed_d = together(feed_sum_e, summed_d)
        summed_e = lax.psum_scatter(feed_sum_e, "line", scatter_dimension=0)

        cross_kept, cross_sent = call(
            cross_grads_kernel,
            (((2 * inner, width), bf16), ((2 * inner, width), bf16)),
            section_scalar,
            cross_grads,
            normed_final,
            normed_cross,
            cross_context,
            cross_branch,
            ties=(back_e,),
        )

        stream_kept, stream_sent, gain_one_e = call(
            first_back_e_kernel,
            (row_f32, row_f32, gain_shape),
            *collected(back_e),
            section_scalar,
            first_e,
            gains_e,
            stream_two_e,
            stream_one_d,
        )
        in_rows, part_d, stream_kept = together(in_rows, part_d, stream_kept)
        in_pieces.append(hop(in_rows, 3))
        in_w = in_plane(in_pieces, 1).reshape(-1, width)
        stream_got, cross_sent = together(swap(stream_sent), cross_sent)
        stream_one, branch_grad, projected_grad = call(
            self_back_kernel,
            (((tokens, width), f32), ((tokens, width), bf16), ((3 * inner, tokens), bf16)),
            section_scalar,
            stream_kept,
            stream_got,
            out_w,
            projected,
            allowed,
            ties=(feed_sum_e,),
        )
        def scatter_parts(*products):
            parts = [m.astype(bf16).reshape(lines, PLANE, -1, width).swapaxes(0, 1) for m in products]
            return scatter_plane(jnp.concatenate(parts, 2)).astype(bf16)

        cross_grad = (cross_kept.astype(f32) + swap(cross_sent).astype(f32)).astype(bf16)
        cross_part = scatter_parts(cross_grad[:inner], cross_grad[inner:])
        second_out_d = second_d + sum(
            part.astype(f32) for part in collected(part_d)
        )
        out_part = scatter_parts(nn(context, branch_grad))
        parts = projected_grad.reshape(lines, PLANE, in_cols, tokens)
        grad_parts = [at(parts, j, 1)] + [hop(at(parts, j ^ k, 1), k) for k in range(1, PLANE)]
        (in_part,) = call(
            in_grad_kernel,
            (((lines * in_cols, width), bf16),),
            *[part.reshape(lines * in_cols, tokens) for part in grad_parts],
            *normed_plane,
            ties=(cross_part, out_part),
        )
        rest_sum = scatter_line(
            jnp.concatenate([in_part.reshape(lines, in_cols, width), cross_part, out_part], 1)
        )
        table_grad, gain_zero = call(
            table_kernel,
            (((vocabulary, width), bf16), gain_shape),
            projected_grad,
            in_w,
            inputs,
            gain_self,
            stream_one,
            one_hot,
            ties=(in_part,),
        )

        zero_row = jnp.zeros_like(gain_zero)
        gain_rows = jnp.concatenate(
            [
                jnp.where(is_encoder, gain_zero, zero_row),
                gain_one_e,
                gain_two_e,
                jnp.where(is_encoder, zero_row, gain_zero),
                gain_one_d,
                gain_two_d,
            ],
            0,
        ).astype(bf16)
        padded = -(-(vocabulary + 6) // 64) * 64
        padding = jnp.zeros((padded - vocabulary - 6, width), bf16)
        small = jnp.concatenate([table_grad, gain_rows, padding], 0).reshape(2, padded // 2, width)
        chip_sum = at(small, section).astype(f32) + swap(at(small, 1 - section)).astype(f32)
        plane_sum = rounded(scatter_plane(chip_sum.astype(bf16).reshape(PLANE, -1, width)))
        plane_sum, summed_e = together(plane_sum, summed_e)
        rest_sum, summed_e = together(rest_sum, summed_e)
        half_sum = gather_plane(sum_line(plane_sum)).reshape(padded // 2, width)
        small_sum = in_order(half_sum, swap(half_sum)).astype(f32)
        embedding_grad = small_sum[:vocabulary]
        gains_grad = at(small_sum[vocabulary : vocabulary + 6].reshape(2, 3, width), section)[None]

        back = permute(
            jnp.concatenate([summed_e[padded_widen:], summed_d[padded_widen:]], 0),
            AXES,
            [(b, a) for a, b in narrow_route],
        )
        halves_e = jnp.concatenate([summed_e[:padded_widen], back[:padded_narrow]], 0)
        halves_d = jnp.concatenate([summed_d[:padded_widen], back[padded_narrow:]], 0)
        half_kept, half_sent = by_section(halves_e, halves_d)
        both = in_order(half_kept[None], swap(half_sent)[None])
        both = both.reshape(2, 3, padded_narrow, width)[:, :, :narrow_half]
        widen_t = both[:, :2].reshape(2 * widen_half, width)
        narrow_grad = both[:, 2].reshape(2 * narrow_half, width).astype(f32)

        output_kept, output_sent = by_section(second_e.astype(bf16), second_out_d.astype(bf16))
        block_output = in_order(output_kept, swap(output_sent)).reshape(rows, length, width)
        cuts = [0, in_cols, in_cols + cross_cols, in_cols + 2 * cross_cols, in_cols + 3 * cross_cols]
        in_sum, first_cross_sum, second_cross_sum, out_sum = (
            rest_sum[a:b] for a, b in zip(cuts[:-1], cuts[1:])
        )
        return (
            block_output[None],
            embedding_grad,
            in_sum.T[None],
            out_sum[None],
            widen_t.astype(f32).T[None],
            narrow_grad[None],
            first_cross_sum.T[None],
            second_cross_sum.T[None],
            gains_grad,
        )

    return per_device


def solution(mesh):
    lines = mesh.shape["dp"] // PLANE
    inner_mesh = Mesh(mesh.devices.reshape(2, lines, PLANE), AXES)
    dp = ("line", "plane")
    return jax.shard_map(
        build(lines),
        mesh=inner_mesh,
        in_specs=(
            P("section", dp, None),
            P(dp, None),
            P(dp, None),
            P(),
            P("section", None, dp),
            P("section", dp, None),
            P("section", None, dp),
            P("section", dp, None),
            P("section", None, dp),
            P("section", None, dp),
            P("section", None, None),
            P("section", dp, None, None),
        ),
        out_specs=(
            P("section", dp, None, None),
            P(),
            P("section", None, dp),
            P("section", dp, None),
            P("section", None, dp),
            P("section", dp, None),
            P("section", None, dp),
            P("section", None, dp),
            P("section", None, None),
        ),
        check_vma=False,
    )
```

time: 810 us -> 615 us (0.76)
  Pallas kernels: 0 us -> 130 us
  waiting for transfers between devices: 339 us -> 257 us
  matrix products: 78 us -> 9.49 us
  starting transfers between devices: 153 us -> 101 us
  blocking collectives: 44.1 us -> 0 us
  other arithmetic: 89.9 us -> 49.2 us
  local copies, waits for them, and re-layouts: 79.3 us -> 45.2 us
    pallas_call x0 -> x17, Pallas kernels: none -> 130 us  [call(): pl.pallas_call(lambda *refs: kernel(*refs[:first], *refs[after:]), grid=(...]
    psum x1 -> x0, waiting for transfers between devices: 76.6 us -> none  [per_device(): summed_gains, embedding_grad = lax.psum((gain_slots, table_grad), AXES)]
    ppermute x74 -> x79, starting transfers between devices: 153 us -> 100 us  [permute(): return lax.ppermute(block, axes, route).reshape(shape)]
    psum x1 -> x0, blocking collectives: 44.1 us -> none  [per_device(): summed_gains, embedding_grad = lax.psum((gain_slots, table_grad), AXES)]
    dot_general x23 -> x0, matrix products: 34.2 us -> none  [the longest x11 28 us: tn(): lax.dot_general(a, b, (((0,), (0,)), ((), ())), preferred_element_type=f32)]
    dot_general x13 -> x2, matrix products: 23.4 us -> 4.22 us  [nn(): lax.dot_general(a, b, (((1,), (0,)), ((), ())), preferred_element_type=f32)]
    add x7 -> x1, other arithmetic: 17.1 us -> 0.38 us  [scatter_line(): total = total + permute(sent, 'line', route).astype(f32)]
    dot_general x11 -> x4, matrix products: 20.4 us -> 5.28 us  [nt(): lax.dot_general(a, b, (((1,), (1,)), ((), ())), preferred_element_type=f32)]
  transfers between devices with their start and end apart: 79 -> 84, of which waited for: 27 -> 46; matrix products, arithmetic and copies ran while one was open for 24% -> 13% of each run, Pallas kernels for 0% -> 18%
where the time goes in v2:
time: 615 us; the launch traced here: 608 us
  waiting for transfers between devices  257 us (42%)
  Pallas kernels  130 us (21%)
  starting transfers between devices  101 us (16%)
  other arithmetic  49.2 us (8%)
  local copies, waits for them, and re-layouts  45.2 us (7%)
  between operations  15.6 us (3%)
  matrix products  9.49 us (2%)
    ppermute x79, waiting for transfers between devices, permute(): return lax.ppermute(block, axes, route).reshape(shape)  229 us
    pallas_call x17, Pallas kernels, call(): pl.pallas_call(lambda *refs: kernel(*refs[:first], *refs[after:]), grid=(...  130 us
    ppermute x79, starting transfers between devices, permute(): return lax.ppermute(block, axes, route).reshape(shape)  100 us
    unnamed x127, local copies, waits for them, and re-layouts  16 us
    all_gather x1, waiting for transfers between devices, per_device(): own_e = lax.all_gather(pack_e, 'line', axis=0)  14.7 us
    all_gather x1, waiting for transfers between devices, per_device(): own_d = lax.all_gather(pack_d, 'line', axis=0)  13.8 us
    convert_element_type x2, other arithmetic, feed_grads(): return (own.astype(f32) + swap(other).astype(f32)).astype(bf16)  13.2 us
  transfers between devices with their start and end apart: 84, of which 46 were waited for; matrix products, arithmetic and copies ran while one was open for 13% of the time, Pallas kernels for 18%

profile of v2, /device:TPU:0, one launch (start us, length us, event | category | flops | bytes accessed | tf_op | source)
XLA Modules:
  0.0 607.6 jit_solution(18385116612116171365)
XLA Ops:
  29.7 10.2 %collective-permute-done.3 = bf16[32,8,1472]{2,1,0:T(8,128)(2,1)} collective-permute-done((bf16[32,8,1472]{2,1,0:T(8,128)(2,1)}, bf16[32,8,1472]{2,1,0:T(8,128)(2,1)}, u32[]{:S(2)}, u32[]{:S(2)}) %collective-permute-start.3) | collective-permute-done | bytes 753696 | tf_op jit(solution)/shard_map/ppermute | solution.py:38
  40.0 27.6 %collective-permute-done.4 = bf16[32,8,1472]{2,1,0:T(8,128)(2,1)} collective-permute-done((bf16[32,8,1472]{2,1,0:T(8,128)(2,1)}, bf16[32,8,1472]{2,1,0:T(8,128)(2,1)}, u32[]{:S(2)}, u32[]{:S(2)}) %collective-permute-start.4) | collective-permute-done | bytes 753696 | tf_op jit(solution)/shard_map/ppermute | solution.py:38
  83.9 7.5 %collective-permute-done.6 = bf16[4,72,256]{2,1,0:T(8,128)(2,1)S(1)} collective-permute-done((bf16[4,72,256]{2,1,0:T(8,128)(2,1)S(1)}, bf16[4,72,256]{2,1,0:T(8,128)(2,1)S(1)}, u32[]{:S(2)}, u32[]{:S(2)}) %collective-permute-start.6) | collective-permute-done | bytes 147488 | tf_op jit(solution)/shard_map/ppermute | solution.py:38
  91.4 6.6 %collective-permute-done.7 = bf16[4,72,256]{2,1,0:T(8,128)(2,1)S(1)} collective-permute-done((bf16[4,72,256]{2,1,0:T(8,128)(2,1)S(1)}, bf16[4,72,256]{2,1,0:T(8,128)(2,1)S(1)}, u32[]{:S(2)}, u32[]{:S(2)}) %collective-permute-start.7) | collective-permute-done | bytes 147488 | tf_op jit(solution)/shard_map/ppermute | solution.py:38
  121.9 8.6 %collective-permute-done.14 = bf16[16,8,1472]{2,1,0:T(8,128)(2,1)S(1)} collective-permute-done((bf16[16,8,1472]{2,1,0:T(8,128)(2,1)}, bf16[16,8,1472]{2,1,0:T(8,128)(2,1)S(1)}, u32[]{:S(2)}, u32[]{:S(2)}) %collective-permute-start.14) | collective-permute-done | bytes 376864 | tf_op jit(solution)/shard_map/ppermute | solution.py:38
  130.5 7.9 %collective-permute-done.15 = bf16[16,8,1472]{2,1,0:T(8,128)(2,1)S(1)} collective-permute-done((bf16[16,8,1472]{2,1,0:T(8,128)(2,1)}, bf16[16,8,1472]{2,1,0:T(8,128)(2,1)S(1)}, u32[]{:S(2)}, u32[]{:S(2)}) %collective-permute-start.15) | collective-permute-done | bytes 376864 | tf_op jit(solution)/shard_map/ppermute | solution.py:38
  138.5 14.7 %all-gather.7.cloned.1.call-done = bf16[1344,1472]{1,0:T(8,128)(2,1)} async-done(((bf16[336,1472]{1,0:T(8,128)(2,1)}), bf16[1344,1472]{1,0:T(8,128)(2,1)}) %all-gather.7.cloned.1.call-update) | async-done | bytes 3956752 | tf_op jit(solution)/shard_map/all_gather | solution.py:535
  157.0 7.7 %shard_map.189 = (bf16[2,1,224,512]{3,2,1,0:T(8,128)(2,1)}, bf16[2,1,224,512]{3,2,1,0:T(8,128)(2,1)}, bf16[2,1,224,512]{3,2,1,0:T(8,128)(2,1)}, bf16[512,1472]{1,0:T(8,128)(2,1)}) custom-call(bf16[128,1472]{1,0:T(8,128)(2,1)} %get-tuple-element.122.refs_0_, bf16[128,1472]{1,0:T(8,128)(2,1)} %bitcast.470, bf16[128,1472]{1,0:T(8,128)(2,1)} %bitcast.473, ...), custom_call_target="tpu_custom_call" | custom-call | flops 4000000000 | bytes 12500000 | tf_op jit(solution)/shard_map/pallas_call | solution.py:79
  164.7 8.3 %shard_map.190 = (bf16[2,1,224,512]{3,2,1,0:T(8,128)(2,1)}, bf16[2,1,224,512]{3,2,1,0:T(8,128)(2,1)}, bf16[2,1,224,512]{3,2,1,0:T(8,128)(2,1)}, bf16[512,1472]{1,0:T(8,128)(2,1)}) custom-call(bf16[128,1472]{1,0:T(8,128)(2,1)} %get-tuple-element.122.refs_0_, bf16[128,1472]{1,0:T(8,128)(2,1)} %bitcast.471, bf16[128,1472]{1,0:T(8,128)(2,1)} %bitcast.474, ...), custom_call_target="tpu_custom_call" | custom-call | flops 4000000000 | bytes 12500000 | tf_op jit(solution)/shard_map/pallas_call | solution.py:79
  173.0 10.2 %collective-permute-done.19 = bf16[4,48,1472]{2,1,0:T(8,128)(2,1)S(1)} collective-permute-done((bf16[4,48,1472]{2,1,0:T(8,128)(2,1)S(1)}, bf16[4,48,1472]{2,1,0:T(8,128)(2,1)S(1)}, u32[]{:S(2)}, u32[]{:S(2)}) %collective-permute-start.19) | collective-permute-done | bytes 565280 | tf_op jit(solution)/shard_map/ppermute | solution.py:38
  197.9 6.8 %collective-permute-done.22 = bf16[16,8,1472]{2,1,0:T(8,128)(2,1)S(1)} collective-permute-done((bf16[16,8,1472]{2,1,0:T(8,128)(2,1)S(1)}, bf16[16,8,1472]{2,1,0:T(8,128)(2,1)S(1)}, u32[]{:S(2)}, u32[]{:S(2)}) %collective-permute-start.22) | collective-permute-done | bytes 376864 | tf_op jit(solution)/shard_map/ppermute | solution.py:38
  207.0 8.7 %shard_map.191 = (f32[128,1472]{1,0:T(8,128)}, bf16[128,1472]{1,0:T(8,128)(2,1)}, bf16[384,128]{1,0:T(8,128)(2,1)}, bf16[768,128]{1,0:T(8,128)(2,1)}, bf16[384,1...) custom-call(bf16[128,1472]{1,0:T(8,128)(2,1)} %get-tuple-element.267.refs_0_, ...), custom_call_target="tpu_custom_call" | custom-call | flops 4000000000 | bytes 12500000 | tf_op jit(solution)/shard_map/pallas_call | solution.py:79
  219.2 13.8 %all-gather.11.cloned.1.call-done = bf16[1344,1472]{1,0:T(8,128)(2,1)} async-done(((bf16[336,1472]{1,0:T(8,128)(2,1)}), bf16[1344,1472]{1,0:T(8,128)(2,1)}) %all-gather.11.cloned.1.call-update) | async-done | bytes 3956752 | tf_op jit(solution)/shard_map/all_gather | solution.py:536
  242.0 7.0 %collective-permute-done.28 = bf16[16,8,1472]{2,1,0:T(8,128)(2,1)S(1)} collective-permute-done((bf16[16,8,1472]{2,1,0:T(8,128)(2,1)S(1)}, bf16[16,8,1472]{2,1,0:T(8,128)(2,1)S(1)}, u32[]{:S(2)}, u32[]{:S(2)}) %collective-permute-start.28) | collective-permute-done | bytes 376864 | tf_op jit(solution)/shard_map/ppermute | solution.py:38
  250.1 8.4 %collective-permute-done.29 = bf16[16,8,1472]{2,1,0:T(8,128)(2,1)S(1)} collective-permute-done((bf16[16,8,1472]{2,1,0:T(8,128)(2,1)S(1)}, bf16[16,8,1472]{2,1,0:T(8,128)(2,1)S(1)}, u32[]{:S(2)}, u32[]{:S(2)}) %collective-permute-start.29) | collective-permute-done | bytes 376864 | tf_op jit(solution)/shard_map/ppermute | solution.py:38
  259.4 12.4 %shard_map.192 = (bf16[2,1,224,512]{3,2,1,0:T(8,128)(2,1)}, bf16[2,2,224,512]{3,2,1,0:T(8,128)(2,1)}, bf16[512,1472]{1,0:T(8,128)(2,1)}, bf16[512,1472]{1,0:T(8,128)(2,1)}) custom-call(bf16[128,1472]{1,0:T(8,128)(2,1)} %get-tuple-element.143.refs_0_, bf16[128,1472]{1,0:T(8,128)(2,1)} %bitcast.499, bf16[128,1472]{1,0:T(8,128)(2,1)} %bitcast.502, ...), custom_call_target="tpu_custom_call" | custom-call | flops 6400000000 | bytes 20000000 | tf_op jit(solution)/shard_map/pallas_call | solution.py:79
  278.0 12.9 %shard_map.193 = (bf16[2,1,224,512]{3,2,1,0:T(8,128)(2,1)}, bf16[2,2,224,512]{3,2,1,0:T(8,128)(2,1)}, bf16[512,1472]{1,0:T(8,128)(2,1)}, bf16[512,1472]{1,0:T(8,128)(2,1)}) custom-call(bf16[128,1472]{1,0:T(8,128)(2,1)} %get-tuple-element.143.refs_0_, bf16[128,1472]{1,0:T(8,128)(2,1)} %bitcast.500, bf16[128,1472]{1,0:T(8,128)(2,1)} %bitcast.503, ...), custom_call_target="tpu_custom_call" | custom-call | flops 6400000000 | bytes 20000000 | tf_op jit(solution)/shard_map/pallas_call | solution.py:79
  291.0 9.8 %shard_map.195 = (bf16[4,336,1472]{2,1,0:T(8,128)(2,1)}, bf16[4,336,1472]{2,1,0:T(8,128)(2,1)}) custom-call(bf16[128,1472]{1,0:T(8,128)(2,1)} %get-tuple-element.143.refs_0_, bf16[128,1472]{1,0:T(8,128)(2,1)} %bitcast.501, bf16[128,1472]{1,0:T(8,128)(2,1)} %bitcast.504, bf16[128,1472]{1,0:T(8,128)(2,1)} %bitcast.507, bf16[128,1472]{1,0:T(8,128)(2,1)} %copy-done.30, ...), custom_call_target="tpu_custom_call" | custom-call | flops 7200000000 | bytes 22500000 | tf_op jit(solution)/shard_map/pallas_call | solution.py:79
  308.1 6.6 %add_convert_fusion.1.refs_14_ = bf16[4,336,1472]{2,1,0:T(8,128)(2,1)} fusion(bf16[4,336,1472]{2,1,0:T(8,128)(2,1)} %collective-permute-done.40, bf16[4,336,1472]{2,1,0:T(8,128)(2,1)} %get-tuple-element.164), kind=kLoop, calls=%fused_computation.1 | loop fusion | flops 7913472 | bytes 11870208 | tf_op jit(solution)/shard_map/convert_element_type | solution.py:651
  315.5 8.0 %collective-permute-done.36 = bf16[16,8,1472]{2,1,0:T(8,128)(2,1)S(1)} collective-permute-done((bf16[16,8,1472]{2,1,0:T(8,128)(2,1)S(1)}, bf16[16,8,1472]{2,1,0:T(8,128)(2,1)S(1)}, u32[]{:S(2)}, u32[]{:S(2)}) %collective-permute-start.36) | collective-permute-done | bytes 376864 | tf_op jit(solution)/shard_map/ppermute | solution.py:38
  324.2 9.2 %shard_map.194 = (f32[128,1472]{1,0:T(8,128)}, bf16[128,1472]{1,0:T(8,128)(2,1)}, bf16[1152,128]{1,0:T(8,128)(2,1)}, f32[128,1472]{1,0:T(8,128)}, bf16[128,1472]...) custom-call(bf16[128,1472]{1,0:T(8,128)(2,1)} %get-tuple-element.263.refs_0_, bf16[128,1472]{1,0:T(8,128)(2,1)} %bitcast.511, ...), custom_call_target="tpu_custom_call" | custom-call | flops 4000000000 | bytes 12500000 | tf_op jit(solution)/shard_map/pallas_call | solution.py:79
  346.4 7.2 %collective-permute-done.39 = bf16[16,8,1472]{2,1,0:T(8,128)(2,1)S(1)} collective-permute-done((bf16[16,8,1472]{2,1,0:T(8,128)(2,1)}, bf16[16,8,1472]{2,1,0:T(8,128)(2,1)S(1)}, u32[]{:S(2)}, u32[]{:S(2)}) %collective-permute-start.39) | collective-permute-done | bytes 376864 | tf_op jit(solution)/shard_map/ppermute | solution.py:38
  354.4 10.7 %shard_map.196 = (bf16[2,2,224,512]{3,2,1,0:T(8,128)(2,1)}, bf16[2,2,224,512]{3,2,1,0:T(8,128)(2,1)}, bf16[512,1472]{1,0:T(8,128)(2,1)}) custom-call(bf16[128,1472]{1,0:T(8,128)(2,1)} %get-tuple-element.155.refs_0_.refs_4_, bf16[128,1472]{1,0:T(8,128)(2,1)} %bitcast.458, bf16[128,1472]{1,0:T(8,128)(2,1)} %bitcast.460, bf16[128,1472]{1,0:T(8,128)(2,1)} %bitcast.462, ...), custom_call_target="tpu_custom_call" | custom-call | flops 6400000000 | bytes 20000000 | tf_op jit(solution)/shard_map/pallas_call | solution.py:79
  370.8 9.8 %shard_map.200 = (bf16[4,336,1472]{2,1,0:T(8,128)(2,1)}, bf16[4,336,1472]{2,1,0:T(8,128)(2,1)}) custom-call(bf16[128,1472]{1,0:T(8,128)(2,1)} %get-tuple-element.122.refs_0_, bf16[128,1472]{1,0:T(8,128)(2,1)} %bitcast.472, bf16[128,1472]{1,0:T(8,128)(2,1)} %bitcast.475, bf16[128,1472]{1,0:T(8,128)(2,1)} %bitcast.478, ...), custom_call_target="tpu_custom_call" | custom-call | flops 7200000000 | bytes 22500000 | tf_op jit(solution)/shard_map/pallas_call | solution.py:79
  418.4 10.6 %collective-permute-done.50 = bf16[4,72,1472]{2,1,0:T(8,128)(2,1)S(1)} collective-permute-done((bf16[4,72,1472]{2,1,0:T(8,128)(2,1)S(1)}, bf16[4,72,1472]{2,1,0:T(8,128)(2,1)S(1)}, u32[]{:S(2)}, u32[]{:S(2)}) %collective-permute-start.50) | collective-permute-done | bytes 847904 | tf_op jit(solution)/shard_map/ppermute | solution.py:38
  430.0 6.6 %add_convert_fusion.refs_6_ = bf16[4,336,1472]{2,1,0:T(8,128)(2,1)} fusion(bf16[4,336,1472]{2,1,0:T(8,128)(2,1)} %collective-permute-done.49, bf16[4,336,1472]{2,1,0:T(8,128)(2,1)} %get-tuple-element.184), kind=kLoop, calls=%fused_computation | loop fusion | flops 7913472 | bytes 11870208 | tf_op jit(solution)/shard_map/convert_element_type | solution.py:651
  445.7 8.6 %shard_map.201 = (f32[256,1472]{1,0:T(8,128)}, bf16[256,1472]{1,0:T(8,128)(2,1)}, bf16[1152,256]{1,0:T(8,128)(2,1)}) custom-call(s32[1]{0:T(128)} %bitcast.28.refs_0_.refs_4_, f32[128,1472]{1,0:T(8,128)} %get-tuple-element.173.refs_1_, f32[128,1472]{1,0:T(8,128)} %bitcast.114.refs_2_, bf16[384,1472]{1,0:T(8,128)(2,1)} %bitcast.441, ...), custom_call_target="tpu_custom_call" | custom-call | flops 4000000000 | bytes 12500000 | tf_op jit(solution)/shard_map/pallas_call | solution.py:79
  463.2 8.5 %collective-permute-done.56 = bf16[4,48,1472]{2,1,0:T(8,128)(2,1)} collective-permute-done((bf16[4,48,1472]{2,1,0:T(8,128)(2,1)}, bf16[4,48,1472]{2,1,0:T(8,128)(2,1)}, u32[]{:S(2)}, u32[]{:S(2)}) %collective-permute-start.56) | collective-permute-done | bytes 565280 | tf_op jit(solution)/shard_map/ppermute | solution.py:38
  507.3 6.4 %collective-permute-start.75 = (bf16[18,8,1472]{2,1,0:T(8,128)(2,1)S(1)}, bf16[18,8,1472]{2,1,0:T(8,128)(2,1)S(1)}, u32[]{:S(2)}, u32[]{:S(2)}) collective-permute-start(bf16[18,8,1472]{2,1,0:T(8,128)(2,1)S(1)} %get-tuple-element.247), channel_id=1, source_target_pairs={{0,12},{1,13},{2,14},{3,15},{16,28},{17,29},{18,30},{19,31}} | collective-permute-start | bytes 1271816 | tf_op jit(solution)/shard_map/ppermute | solution.py:38
  529.5 10.5 %collective-permute-done.74 = bf16[18,8,1472]{2,1,0:T(8,128)(2,1)S(1)} collective-permute-done((bf16[18,8,1472]{2,1,0:T(8,128)(2,1)S(1)}, bf16[18,8,1472]{2,1,0:T(8,128)(2,1)S(1)}, u32[]{:S(2)}, u32[]{:S(2)}) %collective-permute-start.74) | collective-permute-done | bytes 423968 | tf_op jit(solution)/shard_map/ppermute | solution.py:38
  561.9 6.7 %collective-permute-done.66 = bf16[7,8,1472]{2,1,0:T(8,128)(2,1)S(1)} collective-permute-done((bf16[7,8,1472]{2,1,0:T(8,128)(2,1)S(1)}, bf16[7,8,1472]{2,1,0:T(8,128)(2,1)S(1)}, u32[]{:S(2)}, u32[]{:S(2)}) %collective-permute-start.66) | collective-permute-done | bytes 164896 | tf_op jit(solution)/shard_map/ppermute | solution.py:38
  572.4 15.7 %collective-permute-done.67 = bf16[7,8,1472]{2,1,0:T(8,128)(2,1)S(1)} collective-permute-done((bf16[7,8,1472]{2,1,0:T(8,128)(2,1)S(1)}, bf16[7,8,1472]{2,1,0:T(8,128)(2,1)S(1)}, u32[]{:S(2)}, u32[]{:S(2)}) %collective-permute-start.67) | collective-permute-done | bytes 164896 | tf_op jit(solution)/shard_map/ppermute | solution.py:38
  (403 shorter events, 277.9 us)
Async XLA Ops:
  7.2 62.8 %all-gather.9.cloned.1.call-start = ((), (), s32[]{:S(2)}) async-start(), calls=%async_computation.5 | async-start | bytes 2211840 | tf_op jit(solution)/shard_map/all_gather | solution.py:488
  14.7 25.3 %collective-permute-start.3 = (bf16[32,8,1472]{2,1,0:T(8,128)(2,1)}, bf16[32,8,1472]{2,1,0:T(8,128)(2,1)}, u32[]{:S(2)}, u32[]{:S(2)}) collective-permute-start(bf16[32,8,1472]{2,1,0:T(8,128)(2,1)} %fusion.52), channel_id=1, source_target_pairs={{0,1},{1,0},{2,3},{3,2},{4,5},{5,4},{6,7},{7,6},{8,9},{9,8},{10,11... | collective-permute-start | bytes 2261000 | tf_op jit(solution)/shard_map/ppermute | solution.py:38
  17.6 50.0 %collective-permute-start.4 = (bf16[32,8,1472]{2,1,0:T(8,128)(2,1)}, bf16[32,8,1472]{2,1,0:T(8,128)(2,1)}, u32[]{:S(2)}, u32[]{:S(2)}) collective-permute-start(bf16[32,8,1472]{2,1,0:T(8,128)(2,1)} %fusion.52), channel_id=1, source_target_pairs={{0,2},{1,3},{2,0},{3,1},{4,6},{5,7},{6,4},{7,5},{8,10},{9,11},{10,... | collective-permute-start | bytes 2261000 | tf_op jit(solution)/shard_map/ppermute | solution.py:38
  19.1 48.4 %collective-permute-start.5 = (bf16[32,8,1472]{2,1,0:T(8,128)(2,1)}, bf16[32,8,1472]{2,1,0:T(8,128)(2,1)}, u32[]{:S(2)}, u32[]{:S(2)}) collective-permute-start(bf16[32,8,1472]{2,1,0:T(8,128)(2,1)} %fusion.52), channel_id=1, source_target_pairs={{0,3},{1,2},{2,1},{3,0},{4,7},{5,6},{6,5},{7,4},{8,11},{9,10},{10,... | collective-permute-start | bytes 2261000 | tf_op jit(solution)/shard_map/ppermute | solution.py:38
  22.5 130.7 %all-gather.7.cloned.1.call-start = ((), (), s32[]{:S(2)}) async-start(), calls=%async_computation.4 | async-start | bytes 5160960 | tf_op jit(solution)/shard_map/all_gather | solution.py:535
  24.3 43.2 %collective-permute-start.2 = (bf16[28,8,1472]{2,1,0:T(8,128)(2,1)S(1)}, bf16[28,8,1472]{2,1,0:T(8,128)(2,1)S(1)}, u32[]{:S(2)}, u32[]{:S(2)}) collective-permute-start(bf16[28,8,1472]{2,1,0:T(8,128)(2,1)S(1)} %maximum_bitcast_fusion), channel_id=1, source_target_pairs={{0,0},{1,16},{2,1},{3,17},{4,2},{5,18},{6,3},{7,19},{8,8},{9,24},{... | collective-permute-start | bytes 1978376 | tf_op jit(solution)/shard_map/ppermute | solution.py:38
  25.1 87.0 %collective-permute-start.13 = (bf16[131,1472]{1,0:T(8,128)(2,1)S(1)}, bf16[131,1472]{1,0:T(8,128)(2,1)}, u32[]{:S(2)}, u32[]{:S(2)}) collective-permute-start(bf16[131,1472]{1,0:T(8,128)(2,1)S(1)} %pad_maximum_fusion.6), channel_id=1, source_target_pairs={{0,16},{16,0},{1,17},{17,1},{2,18},{18,2},{3,19},{19,3},{4,20},{20... | collective-permute-start | bytes 1157000 | tf_op jit(solution)/shard_map/ppermute | solution.py:38
  69.1 163.9 %all-gather.11.cloned.1.call-start = ((), (), s32[]{:S(2)}) async-start(), calls=%async_computation.6 | async-start | bytes 5160960 | tf_op jit(solution)/shard_map/all_gather | solution.py:536
  71.7 33.3 %collective-permute-start.9 = (bf16[4,24,1472]{2,1,0:T(8,128)(2,1)S(1)}, bf16[4,24,1472]{2,1,0:T(8,128)(2,1)S(1)}, u32[]{:S(2)}, u32[]{:S(2)}) collective-permute-start(bf16[4,24,1472]{2,1,0:T(8,128)(2,1)S(1)} %slice.188), channel_id=1, source_target_pairs={{0,1},{1,0},{2,3},{3,2},{4,5},{5,4},{6,7},{7,6},{8,9},{9,8},{10,11... | collective-permute-start | bytes 847880 | tf_op jit(solution)/shard_map/ppermute | solution.py:38
  74.8 30.2 %collective-permute-start.10 = (bf16[4,24,1472]{2,1,0:T(8,128)(2,1)S(1)}, bf16[4,24,1472]{2,1,0:T(8,128)(2,1)S(1)}, u32[]{:S(2)}, u32[]{:S(2)}) collective-permute-start(bf16[4,24,1472]{2,1,0:T(8,128)(2,1)S(1)} %slice.188), channel_id=1, source_target_pairs={{0,2},{1,3},{2,0},{3,1},{4,6},{5,7},{6,4},{7,5},{8,10},{9,11},{10,... | collective-permute-start | bytes 847880 | tf_op jit(solution)/shard_map/ppermute | solution.py:38
  74.8 30.2 %collective-permute-start.11 = (bf16[4,24,1472]{2,1,0:T(8,128)(2,1)S(1)}, bf16[4,24,1472]{2,1,0:T(8,128)(2,1)S(1)}, u32[]{:S(2)}, u32[]{:S(2)}) collective-permute-start(bf16[4,24,1472]{2,1,0:T(8,128)(2,1)S(1)} %slice.188), channel_id=1, source_target_pairs={{0,3},{1,2},{2,1},{3,0},{4,7},{5,6},{6,5},{7,4},{8,11},{9,10},{10,... | collective-permute-start | bytes 847880 | tf_op jit(solution)/shard_map/ppermute | solution.py:38
  153.2 283.4 %reduce-scatter.3.cloned.1.call-start = ((), (), s32[]{:S(2)}) async-start(), calls=%async_computation.2 | async-start | bytes 5160960 | tf_op jit(solution)/shard_map/reduce_scatter | solution.py:736
  155.0 28.1 %collective-permute-start.19 = (bf16[4,48,1472]{2,1,0:T(8,128)(2,1)S(1)}, bf16[4,48,1472]{2,1,0:T(8,128)(2,1)S(1)}, u32[]{:S(2)}, u32[]{:S(2)}) collective-permute-start(bf16[4,48,1472]{2,1,0:T(8,128)(2,1)S(1)} %slice.186), channel_id=1, source_target_pairs={{0,2},{1,3},{2,0},{3,1},{4,6},{5,7},{6,4},{7,5},{8,10},{9,11},{10,... | collective-permute-start | bytes 1695752 | tf_op jit(solution)/shard_map/ppermute | solution.py:38
  156.5 26.6 %collective-permute-start.20 = (bf16[4,48,1472]{2,1,0:T(8,128)(2,1)S(1)}, bf16[4,48,1472]{2,1,0:T(8,128)(2,1)S(1)}, u32[]{:S(2)}, u32[]{:S(2)}) collective-permute-start(bf16[4,48,1472]{2,1,0:T(8,128)(2,1)S(1)} %slice.186), channel_id=1, source_target_pairs={{0,3},{1,2},{2,1},{3,0},{4,7},{5,6},{6,5},{7,4},{8,11},{9,10},{10,... | collective-permute-start | bytes 1695752 | tf_op jit(solution)/shard_map/ppermute | solution.py:38
  235.0 42.1 %collective-permute-start.31 = (bf16[4,336,1472]{2,1,0:T(8,128)(2,1)}, bf16[4,336,1472]{2,1,0:T(8,128)(2,1)}, u32[]{:S(2)}, u32[]{:S(2)}) collective-permute-start(bf16[4,336,1472]{2,1,0:T(8,128)(2,1)} %bitcast.490), channel_id=1, source_target_pairs={{0,16},{16,0},{1,17},{17,1},{2,18},{18,2},{3,19},{19,3},{4,20},{20... | collective-permute-start | bytes 11870216 | tf_op jit(solution)/shard_map/ppermute | solution.py:38
  238.5 20.0 %collective-permute-start.29 = (bf16[16,8,1472]{2,1,0:T(8,128)(2,1)S(1)}, bf16[16,8,1472]{2,1,0:T(8,128)(2,1)S(1)}, u32[]{:S(2)}, u32[]{:S(2)}) collective-permute-start(bf16[16,8,1472]{2,1,0:T(8,128)(2,1)S(1)} %bitcast.465), channel_id=1, source_target_pairs={{0,2},{1,3},{2,0},{3,1},{4,6},{5,7},{6,4},{7,5},{8,10},{9,11},{10,... | collective-permute-start | bytes 1130504 | tf_op jit(solution)/shard_map/ppermute | solution.py:38
  240.6 35.5 %collective-permute-start.32 = (bf16[4,72,1472]{2,1,0:T(8,128)(2,1)S(1)}, bf16[4,72,1472]{2,1,0:T(8,128)(2,1)S(1)}, u32[]{:S(2)}, u32[]{:S(2)}) collective-permute-start(bf16[4,72,1472]{2,1,0:T(8,128)(2,1)S(1)} %slice.187), channel_id=1, source_target_pairs={{0,1},{1,0},{2,3},{3,2},{4,5},{5,4},{6,7},{7,6},{8,9},{9,8},{10,11... | collective-permute-start | bytes 2543624 | tf_op jit(solution)/shard_map/ppermute | solution.py:38
  249.0 28.1 %collective-permute-start.33 = (bf16[4,72,1472]{2,1,0:T(8,128)(2,1)S(1)}, bf16[4,72,1472]{2,1,0:T(8,128)(2,1)S(1)}, u32[]{:S(2)}, u32[]{:S(2)}) collective-permute-start(bf16[4,72,1472]{2,1,0:T(8,128)(2,1)S(1)} %slice.187), channel_id=1, source_target_pairs={{0,2},{1,3},{2,0},{3,1},{4,6},{5,7},{6,4},{7,5},{8,10},{9,11},{10,... | collective-permute-start | bytes 2543624 | tf_op jit(solution)/shard_map/ppermute | solution.py:38
  314.8 233.0 %reduce-scatter.5.cloned.1.call-start = ((), (), s32[]{:S(2)}) async-start(), calls=%async_computation.3 | async-start | bytes 5160960 | tf_op jit(solution)/shard_map/reduce_scatter | solution.py:738
  380.6 49.4 %collective-permute-start.49 = (bf16[4,336,1472]{2,1,0:T(8,128)(2,1)}, bf16[4,336,1472]{2,1,0:T(8,128)(2,1)}, u32[]{:S(2)}, u32[]{:S(2)}) collective-permute-start(bf16[4,336,1472]{2,1,0:T(8,128)(2,1)} %get-tuple-element.185), channel_id=1, source_target_pairs={{0,16},{16,0},{1,17},{17,1},{2,18},{18,2},{3,19},{19,3},{4,20},{20... | collective-permute-start | bytes 11870216 | tf_op jit(solution)/shard_map/ppermute | solution.py:38
  404.7 24.3 %collective-permute-start.50 = (bf16[4,72,1472]{2,1,0:T(8,128)(2,1)S(1)}, bf16[4,72,1472]{2,1,0:T(8,128)(2,1)S(1)}, u32[]{:S(2)}, u32[]{:S(2)}) collective-permute-start(bf16[4,72,1472]{2,1,0:T(8,128)(2,1)S(1)} %slice.187), channel_id=1, source_target_pairs={{0,3},{1,2},{2,1},{3,0},{4,7},{5,6},{6,5},{7,4},{8,11},{9,10},{10,... | collective-permute-start | bytes 2543624 | tf_op jit(solution)/shard_map/ppermute | solution.py:38
  414.8 21.8 %collective-permute-start.54 = (bf16[96,8,1472]{2,1,0:T(8,128)(2,1)}, bf16[96,8,1472]{2,1,0:T(8,128)(2,1)}, u32[]{:S(2)}, u32[]{:S(2)}) collective-permute-start(bf16[96,8,1472]{2,1,0:T(8,128)(2,1)} %bitcast.134), channel_id=1, source_target_pairs={{0,16},{16,0},{1,17},{17,1},{2,18},{18,2},{3,19},{19,3},{4,20},{20... | collective-permute-start | bytes 6782984 | tf_op jit(solution)/shard_map/ppermute | solution.py:38
  442.9 28.8 %collective-permute-start.56 = (bf16[4,48,1472]{2,1,0:T(8,128)(2,1)}, bf16[4,48,1472]{2,1,0:T(8,128)(2,1)}, u32[]{:S(2)}, u32[]{:S(2)}) collective-permute-start(bf16[4,48,1472]{2,1,0:T(8,128)(2,1)} %get-tuple-element.237), channel_id=1, source_target_pairs={{0,2},{1,3},{2,0},{3,1},{4,6},{5,7},{6,4},{7,5},{8,10},{9,11},{10,... | collective-permute-start | bytes 1695752 | tf_op jit(solution)/shard_map/ppermute | solution.py:38
  444.0 28.4 %collective-permute-start.55 = (bf16[4,48,1472]{2,1,0:T(8,128)(2,1)}, bf16[4,48,1472]{2,1,0:T(8,128)(2,1)}, u32[]{:S(2)}, u32[]{:S(2)}) collective-permute-start(bf16[4,48,1472]{2,1,0:T(8,128)(2,1)} %get-tuple-element.236), channel_id=1, source_target_pairs={{0,1},{1,0},{2,3},{3,2},{4,5},{5,4},{6,7},{7,6},{8,9},{9,8},{10,11... | collective-permute-start | bytes 1695752 | tf_op jit(solution)/shard_map/ppermute | solution.py:38
  460.6 21.4 %collective-permute-start.59 = (bf16[4,24,1472]{2,1,0:T(8,128)(2,1)S(1)}, bf16[4,24,1472]{2,1,0:T(8,128)(2,1)S(1)}, u32[]{:S(2)}, u32[]{:S(2)}) collective-permute-start(bf16[4,24,1472]{2,1,0:T(8,128)(2,1)S(1)} %get-tuple-element.274), channel_id=1, source_target_pairs={{0,2},{1,3},{2,0},{3,1},{4,6},{5,7},{6,4},{7,5},{8,10},{9,11},{10,... | collective-permute-start | bytes 847880 | tf_op jit(solution)/shard_map/ppermute | solution.py:38
  461.4 22.9 %collective-permute-start.58 = (bf16[4,24,1472]{2,1,0:T(8,128)(2,1)S(1)}, bf16[4,24,1472]{2,1,0:T(8,128)(2,1)S(1)}, u32[]{:S(2)}, u32[]{:S(2)}) collective-permute-start(bf16[4,24,1472]{2,1,0:T(8,128)(2,1)S(1)} %get-tuple-element.272), channel_id=1, source_target_pairs={{0,1},{1,0},{2,3},{3,2},{4,5},{5,4},{6,7},{7,6},{8,9},{9,8},{10,11... | collective-permute-start | bytes 847880 | tf_op jit(solution)/shard_map/ppermute | solution.py:38
  504.0 20.0 %collective-permute-start.61 = (bf16[28,8,1472]{2,1,0:T(8,128)(2,1)S(1)}, bf16[28,8,1472]{2,1,0:T(8,128)(2,1)S(1)}, u32[]{:S(2)}, u32[]{:S(2)}) collective-permute-start(bf16[28,8,1472]{2,1,0:T(8,128)(2,1)S(1)} %get-tuple-element.270), channel_id=1, source_target_pairs={{0,16},{16,0},{1,17},{17,1},{2,18},{18,2},{3,19},{19,3},{4,20},{20... | collective-permute-start | bytes 1978376 | tf_op jit(solution)/shard_map/ppermute | solution.py:38
  507.3 21.6 %collective-permute-start.75 = (bf16[18,8,1472]{2,1,0:T(8,128)(2,1)S(1)}, bf16[18,8,1472]{2,1,0:T(8,128)(2,1)S(1)}, u32[]{:S(2)}, u32[]{:S(2)}) collective-permute-start(bf16[18,8,1472]{2,1,0:T(8,128)(2,1)S(1)} %get-tuple-element.247), channel_id=1, source_target_pairs={{0,12},{1,13},{2,14},{3,15},{16,28},{17,29},{18,30},{19,31}} | collective-permute-start | bytes 1271816 | tf_op jit(solution)/shard_map/ppermute | solution.py:38
  513.7 26.3 %collective-permute-start.74 = (bf16[18,8,1472]{2,1,0:T(8,128)(2,1)S(1)}, bf16[18,8,1472]{2,1,0:T(8,128)(2,1)S(1)}, u32[]{:S(2)}, u32[]{:S(2)}) collective-permute-start(bf16[18,8,1472]{2,1,0:T(8,128)(2,1)S(1)} %get-tuple-element.248), channel_id=1, source_target_pairs={{8,0},{12,4},{9,1},{13,5},{10,2},{14,6},{11,3},{15,7},{24,16},{28,... | collective-permute-start | bytes 1271816 | tf_op jit(solution)/shard_map/ppermute | solution.py:38
  515.0 26.7 %collective-permute-start.73 = (bf16[18,8,1472]{2,1,0:T(8,128)(2,1)S(1)}, bf16[18,8,1472]{2,1,0:T(8,128)(2,1)S(1)}, u32[]{:S(2)}, u32[]{:S(2)}) collective-permute-start(bf16[18,8,1472]{2,1,0:T(8,128)(2,1)S(1)} %get-tuple-element.249), channel_id=1, source_target_pairs={{0,8},{4,12},{1,9},{5,13},{2,10},{6,14},{3,11},{7,15},{16,24},{20,... | collective-permute-start | bytes 1271816 | tf_op jit(solution)/shard_map/ppermute | solution.py:38
  522.8 19.8 %collective-permute-start.72 = (bf16[18,8,1472]{2,1,0:T(8,128)(2,1)S(1)}, bf16[18,8,1472]{2,1,0:T(8,128)(2,1)S(1)}, u32[]{:S(2)}, u32[]{:S(2)}) collective-permute-start(bf16[18,8,1472]{2,1,0:T(8,128)(2,1)S(1)} %get-tuple-element.250), channel_id=1, source_target_pairs={{4,0},{8,4},{12,8},{5,1},{9,5},{13,9},{6,2},{10,6},{14,10},{7,3},{... | collective-permute-start | bytes 1271816 | tf_op jit(solution)/shard_map/ppermute | solution.py:38
  561.2 27.0 %collective-permute-start.77 = (bf16[28,8,1472]{2,1,0:T(8,128)(2,1)S(1)}, bf16[28,8,1472]{2,1,0:T(8,128)(2,1)S(1)}, u32[]{:S(2)}, u32[]{:S(2)}) collective-permute-start(bf16[28,8,1472]{2,1,0:T(8,128)(2,1)S(1)} %maximum_bitcast_fusion.1), channel_id=1, source_target_pairs={{0,0},{16,1},{1,2},{17,3},{2,4},{18,5},{3,6},{19,7},{8,8},{24,9},{... | collective-permute-start | bytes 1978376 | tf_op jit(solution)/shard_map/ppermute | solution.py:38
  (114 other events, 1101.5 us)
Sparse Core Ops, SparseCore 0:
  22.6 45.9 all-gather.8
  70.7 82.4 all-gather.6
  154.7 78.2 all-gather.10
  314.9 73.0 reduce-scatter.2
  436.7 73.0 reduce-scatter.4

commit v3 on v2

--- a/solution.py
+++ b/solution.py
@@ -56,17 +56,17 @@
 
 def gelu_parts(gate):
     slope = (2.0 / jnp.pi) ** 0.5
-    cube = 0.044715 * gate * gate
-    bent = jnp.tanh(slope * gate * (1.0 + cube))
-    half = 0.5 * (1.0 + bent)
-    return half * gate, half + 0.5 * gate * (1.0 - bent * bent) * slope * (1.0 + 3.0 * cube)
+    square = gate * gate
+    half = 0.5 + 0.5 * jnp.tanh(gate * (slope + (slope * 0.044715) * square))
+    bend = gate * (slope + (slope * 0.134145) * square)
+    return gate * half, half + (2.0 * half) * ((1.0 - half) * bend)
 
 
 def whole(shape):
     return pl.BlockSpec(shape, lambda step: (0,) * len(shape))
 
 
-def call(kernel, outputs, *args, scratch=(), steps=1, specs=None, time_us=5, ties=()):
+def call(kernel, outputs, *args, scratch=(), specs=None, time_us=0.3, ties=(), vmem=56):
     specs = specs or {}
     in_specs = [
         specs.get(i)
@@ -78,12 +78,12 @@
     out_shape = tuple(jax.ShapeDtypeStruct(output[0], output[1]) for output in outputs)
     return pl.pallas_call(
         lambda *refs: kernel(*refs[:first], *refs[after:]),
-        grid=(steps,),
+        grid=(1,),
         out_shape=out_shape,
         in_specs=in_specs,
         out_specs=tuple(output[2] if len(output) > 2 else whole(output[0]) for output in outputs),
         scratch_shapes=list(scratch),
-        compiler_params=pltpu.CompilerParams(vmem_limit_bytes=56 * 1024 * 1024),
+        compiler_params=pltpu.CompilerParams(vmem_limit_bytes=vmem * 1024 * 1024),
         cost_estimate=pl.CostEstimate(
             flops=int(time_us * 8e8), bytes_accessed=int(time_us * 2.5e6), transcendentals=0
         ),
@@ -163,117 +163,114 @@
     normed_d_ref[...] = rms_norm(first_d, gains_d_ref[1:2]).astype(bf16)
 
 
-def joined(refs, scratch):
+def joined(refs, out_ref):
     length = refs[0].shape[0]
     for k, ref in enumerate(refs):
-        scratch[k * length : (k + 1) * length] = ref[...]
-    return scratch[...]
-
-
-def feed_specs(lines, padded, width):
-    half = lines // 2
+        out_ref[k * length : (k + 1) * length] = ref[...]
+    return out_ref[...]
+
+
+def apart(value, refs):
+    length = refs[0].shape[0]
+    for k, ref in enumerate(refs):
+        ref[...] = value[k * length : (k + 1) * length].astype(bf16)
+
+
+def pack_specs(lines, padded, width):
     return [
-        pl.BlockSpec((1, padded, width), lambda step: (step, 0, 0)),
-        pl.BlockSpec((1, padded, width), lambda step: (half + step, 0, 0)),
-        pl.BlockSpec((2, padded // 2, width), lambda step: (step, 2, 0)),
+        pl.BlockSpec((lines, padded, width), lambda step: (0, 0, 0)),
+        pl.BlockSpec((lines, padded // 2, width), lambda step: (0, 2, 0)),
     ]
 
 
-def stacked(weights):
-    wide = jnp.concatenate([w[0] for pack in weights for w in pack[:2]], 0)
-    narrow = jnp.concatenate([half for pack in weights for half in (pack[2][0], pack[2][1])], 0)
-    return wide, narrow
-
-
-def sum_over_steps(total, scratch, out_ref, prior_ref=None):
-    step = pl.program_id(0)
-
-    @pl.when(step == 0)
-    def _():
-        scratch[...] = total if prior_ref is None else total + prior_ref[...].astype(f32)
-
-    @pl.when(step > 0)
-    def _():
-        scratch[...] += total
-
-    @pl.when(step == pl.num_programs(0) - 1)
-    def _():
-        out_ref[...] = scratch[...].astype(bf16)
-
-
-def join_once(refs, scratch):
-    @pl.when(pl.program_id(0) == 0)
-    def _():
-        joined(refs, scratch)
-
-
-def cut(array, count):
-    rows = array.shape[0] // count
-    return [array[i * rows : (i + 1) * rows] for i in range(count)]
-
-
-def feed_forward_kernel(priors, *refs):
-    streams, pack, refs = refs[:4], refs[4:7], refs[7:]
-    prior_refs, (value_ref, slope_ref, hidden_ref, part_ref, x_ref, part_sum) = refs[:priors], refs[priors:]
-    join_once(streams, x_ref)
-    wide, narrow = stacked([pack])
-    gate, up = cut(nt(wide, x_ref[...]), 2)
-    value, slope = gelu_parts(gate)
-    value_ref[0, 0] = value.astype(bf16)
-    slope_ref[0, 0] = (slope * up).astype(bf16)
-    hidden = (value * up).astype(bf16)
-    hidden_ref[0, 0] = hidden
-    sum_over_steps(tn(hidden, narrow), part_sum, part_ref, *prior_refs)
+def rows_of(ref):
+    return ref[...].reshape(ref.shape[0] * ref.shape[1], ref.shape[2])
+
+
+def feed_forward(x, wide, narrow, value_ref, slope_ref, hidden_ref):
+    both = nt(wide, x)
+    units = both.shape[0] // 2
+    value, slope = gelu_parts(both[:units])
+    value_ref[...] = value.astype(bf16)
+    slope_ref[...] = (slope * both[units:]).astype(bf16)
+    hidden_ref[...] = (value * both[units:]).astype(bf16)
+    return tn(hidden_ref[...], narrow)
+
+
+def feed_forward_own_kernel(*refs):
+    streams, wide_ref, narrow_ref, value_ref, slope_ref, hidden_ref, part_ref, x_ref = refs[:4], *refs[4:]
+    x = joined(streams, x_ref)
+    part = feed_forward(x, rows_of(wide_ref), rows_of(narrow_ref), value_ref, slope_ref, hidden_ref)
+    part_ref[...] = part.astype(bf16)
+
+
+def feed_forward_other_kernel(x_ref, prior_ref, wide_ref, narrow_ref, value_ref, slope_ref, hidden_ref, *part_refs):
+    part = feed_forward(
+        x_ref[...], rows_of(wide_ref), rows_of(narrow_ref), value_ref, slope_ref, hidden_ref
+    )
+    apart(part + prior_ref[...].astype(f32), part_refs)
 
 
 def feed_back_kernel(*refs):
-    outputs, packs, saved = refs[:4], (refs[4:7], refs[7:10]), refs[10:14]
-    grads_refs, (back_ref, output_ref, back_sum) = refs[14:16], refs[16:]
-    join_once(outputs, output_ref)
-    wide, narrow = stacked(packs)
-    grads = []
-    for core, hidden_grad in enumerate(cut(nt(narrow, output_ref[...]), 2)):
+    outputs, packs, saved = refs[:4], (refs[4:6], refs[6:8]), refs[8:12]
+    grads_refs, output_ref, back_refs = refs[12:14], refs[14], refs[15:]
+    output_grad = joined(outputs, output_ref)
+    back = None
+    for core, (wide_ref, narrow_ref) in enumerate(packs):
+        hidden_grad = nt(rows_of(narrow_ref), output_grad)
+        units = hidden_grad.shape[0]
         value_ref, slope_ref = saved[2 * core : 2 * core + 2]
-        grads.append((hidden_grad * slope_ref[0, 0].astype(f32)).astype(bf16))
-        grads.append((hidden_grad * value_ref[0, 0].astype(f32)).astype(bf16))
-        grads_refs[core][0, 0] = grads[-2]
-        grads_refs[core][0, 1] = grads[-1]
-    sum_over_steps(tn(jnp.concatenate(grads, 0), wide), back_sum, back_ref)
-
-
-def feed_both_kernel(priors, *refs):
-    streams, outputs, pack, refs = refs[:4], refs[4:8], refs[8:11], refs[11:]
-    prior_refs, refs = refs[:priors], refs[priors:]
-    hidden_ref, grads_ref, part_ref, back_ref, x_ref, output_ref, part_sum, back_sum = refs
-    join_once(streams, x_ref)
-    join_once(outputs, output_ref)
-    wide, narrow = stacked([pack])
-    gate, up = cut(nt(wide, x_ref[...]), 2)
-    hidden_grad = nt(narrow, output_ref[...])
-    value, slope = gelu_parts(gate)
-    hidden = (value * up).astype(bf16)
-    hidden_ref[0, 0] = hidden
-    grads = [(hidden_grad * (slope * up)).astype(bf16), (hidden_grad * value).astype(bf16)]
-    grads_ref[0, 0] = grads[0]
-    grads_ref[0, 1] = grads[1]
-    sum_over_steps(tn(jnp.concatenate(grads, 0), wide), back_sum, back_ref, *prior_refs[1:])
-    sum_over_steps(tn(hidden, narrow), part_sum, part_ref, *prior_refs[:1])
+        grads_refs[core][:units] = (hidden_grad * slope_ref[...].astype(f32)).astype(bf16)
+        grads_refs[core][units:] = (hidden_grad * value_ref[...].astype(f32)).astype(bf16)
+        term = tn(grads_refs[core][...], rows_of(wide_ref))
+        back = term if back is None else back + term
+    apart(back, back_refs)
+
+
+def feed_both(x, output_grad, wide, narrow, grads_ref):
+    both = nt(wide, x)
+    hidden_grad = nt(narrow, output_grad)
+    units = hidden_grad.shape[0]
+    value, slope = gelu_parts(both[:units])
+    grads_ref[:units] = (hidden_grad * (slope * both[units:])).astype(bf16)
+    grads_ref[units : 2 * units] = (hidden_grad * value).astype(bf16)
+    grads_ref[2 * units :] = (value * both[units:]).astype(bf16)
+    return tn(grads_ref[2 * units :], narrow), tn(grads_ref[: 2 * units], wide)
+
+
+def feed_both_own_kernel(*refs):
+    streams, outputs, wide_ref, narrow_ref, grads_ref, part_ref, back_ref, x_ref, output_ref = (
+        refs[:4],
+        refs[4:8],
+        *refs[8:],
+    )
+    x, output_grad = joined(streams, x_ref), joined(outputs, output_ref)
+    part, back = feed_both(x, output_grad, rows_of(wide_ref), rows_of(narrow_ref), grads_ref)
+    part_ref[...] = part.astype(bf16)
+    back_ref[...] = back.astype(bf16)
+
+
+def feed_both_other_kernel(x_ref, output_ref, part_prior, back_prior, wide_ref, narrow_ref, grads_ref, *refs):
+    part, back = feed_both(x_ref[...], output_ref[...], rows_of(wide_ref), rows_of(narrow_ref), grads_ref)
+    apart(back + back_prior[...].astype(f32), refs[:4])
+    apart(part + part_prior[...].astype(f32), refs[4:])
 
 
 def feed_grads_kernel(*refs):
-    streams, outputs, grads_refs, hidden_refs = refs[:4], refs[4:8], refs[8:10], refs[10:12]
-    own_ref, other_ref, x_ref, output_ref = refs[12:]
-    step, steps = pl.program_id(0), pl.num_programs(0)
-    padded, rows = grads_refs[0].shape[2:]
-    join_once(streams, x_ref)
-    join_once(outputs, output_ref)
-    for grads_ref, hidden_ref, ref in zip(grads_refs, hidden_refs, (own_ref, other_ref)):
-        wide = cut(nn(grads_ref[...].reshape(2 * padded, rows), x_ref[...]), 2)
-        narrow = cut(nn(hidden_ref[0, 0], output_ref[...]), 2)
-        ref[step, :padded] = wide[0].astype(bf16)
-        ref[steps + step, :padded] = wide[1].astype(bf16)
-        ref[2 * step, padded:] = narrow[0].astype(bf16)
-        ref[2 * step + 1, padded:] = narrow[1].astype(bf16)
+    cores, pack_ref = (refs[: len(refs) // 2], refs[len(refs) // 2 : -1]), refs[-1]
+    lines = pack_ref.shape[0]
+    wide = narrow = 0.0
+    for x_ref, output_ref, *factors in cores:
+        if len(factors) == 1:
+            units = factors[0].shape[0] // 3
+            grads, hidden = factors[0][: 2 * units], factors[0][2 * units :]
+        else:
+            grads, hidden = factors[0][...], factors[1][...]
+        wide = wide + nn(grads, x_ref[...])
+        narrow = narrow + nn(hidden, output_ref[...])
+    padded = wide.shape[0] // lines
+    pack_ref[:, :padded] = wide.astype(bf16).reshape(lines, padded, wide.shape[1])
+    pack_ref[:, padded:] = narrow.astype(bf16).reshape(lines, padded // 2, wide.shape[1])
 
 
 def middle_kernel(*refs):
@@ -343,10 +340,41 @@
     )
 
 
-def table_kernel(grads_ref, in_w_ref, inputs_ref, gain_ref, stream_ref, one_hot_ref, table_ref, gain_grad_ref):
-    upstream = tn(grads_ref[...], in_w_ref[...])
-    input_grad, gain_grad_ref[...] = rms_back(inputs_ref[...], gain_ref[...], upstream)
-    table_ref[...] = tn(one_hot_ref[...], (stream_ref[...] + input_grad).astype(bf16)).astype(bf16)
+def table_kernel(*refs):
+    grads, codes, gain_refs, (section_ref, in_ref, embedding_ref, gain_ref, stream_ref, out_ref) = (
+        refs[:4],
+        refs[4:8],
+        refs[8:12],
+        refs[12:],
+    )
+    table = gain_grad = 0.0
+    for k, (grad, code_ref) in enumerate(zip(grads, codes)):
+        shape = (embedding_ref.shape[0], code_ref.shape[1])
+        one_hot = (lax.broadcasted_iota(jnp.int32, shape, 0) == code_ref[...]).astype(bf16)
+        inputs = tn(one_hot, embedding_ref[...])
+        input_grad, gain_part = rms_back(inputs, gain_ref[...], tn(grad[...], in_ref[...]))
+        if k == 0:
+            input_grad = input_grad + stream_ref[...]
+        gain_grad = gain_grad + gain_part
+        table = table + nn(one_hot, input_grad.astype(bf16))
+    vocabulary = embedding_ref.shape[0]
+    out_ref[:vocabulary] = table.astype(bf16)
+    nothing, is_encoder = jnp.zeros_like(gain_grad), section_ref[0] == 0
+    rows = [jnp.where(is_encoder, gain_grad, nothing), gain_refs[0][...], gain_refs[1][...]]
+    rows += [jnp.where(is_encoder, nothing, gain_grad), gain_refs[2][...], gain_refs[3][...]]
+    rows.append(jnp.zeros((out_ref.shape[0] - vocabulary - 6, out_ref.shape[1]), f32))
+    out_ref[vocabulary:] = jnp.concatenate(rows, 0).astype(bf16)
+
+
+def assemble_kernel(section_ref, plane_ref, *refs):
+    pieces, (table_ref, gains_ref, rows_ref) = refs[:PLANE], refs[PLANE:]
+    count = pieces[0].shape[0]
+    for k, piece in enumerate(pieces):
+        rows_ref[pl.ds(pl.multiple_of((plane_ref[0] ^ k) * count, 8), count)] = piece[...].astype(f32)
+    vocabulary = table_ref.shape[0]
+    table_ref[...] = rows_ref[:vocabulary]
+    gains = rows_ref[vocabulary : vocabulary + 8]
+    gains_ref[0] = jnp.where(section_ref[0] == 0, gains[:3], gains[3:6])
 
 
 def in_grad_kernel(*refs):
@@ -421,30 +449,17 @@
     def gather_plane(block, axis=0):
         return in_plane(spread(block), axis)
 
-    def scatter_line(partial):
-        if lines > 8:
-            return lax.psum_scatter(partial, "line", scatter_dimension=0).astype(f32)
-        z = lax.axis_index("line")
-        total = at(partial, z).astype(f32)
-        for step in range(1, lines):
-            for distance in (step, -step):
-                route = [(a, a + distance) for a in range(lines) if 0 <= a + distance < lines]
-                sent = at(partial, jnp.clip(z + distance, 0, lines - 1))
-                total = total + permute(sent, "line", route).astype(f32)
-        return total
-
-    def scatter_plane(parts):
+    def scattered(parts):
         j = lax.axis_index("plane")
-        total = at(parts, j).astype(f32)
-        for k in range(1, PLANE):
-            total = total + hop(at(parts, j ^ k), k).astype(f32)
-        return total
+        return [at(parts, j)] + [hop(at(parts, j ^ k), k) for k in range(1, PLANE)]
+
+    def total_of(terms):
+        return sum((term.astype(f32) for term in terms[1:]), terms[0].astype(f32))
 
     def spread(block):
         return [block] + [hop(block, k) for k in range(1, PLANE)]
 
-    def collected(partial):
-        parts = partial.reshape((PLANE, -1) + partial.shape[1:])
+    def collected(parts):
         return [parts[0]] + [hop(parts[k], k) for k in range(1, PLANE)]
 
     def per_device(
@@ -471,7 +486,7 @@
         tokens = rows * length
 
         def together(*values):
-            return lax.optimization_barrier(values)
+            return list(lax.optimization_barrier(values))
 
         def by_section(mine, other):
             return jnp.where(is_encoder, mine, other), jnp.where(is_encoder, other, mine)
@@ -483,7 +498,7 @@
         cross_cols = cross_first.shape[2]
         column, codes = together(
             jnp.concatenate([attention_in[0].T, attention_out[0], cross_first[0].T, cross_second[0].T], 0),
-            byte_codes[0].reshape(tokens),
+            byte_codes[0],
         )
         column = lax.all_gather(column, "line", axis=0)
         in_column = column[:, :in_cols].reshape(-1, width)
@@ -504,10 +519,9 @@
         )
         widen_e, widen_d = by_section(at(widen_parts, section), swap(at(widen_parts, 1 - section)))
 
-        one_hot = (
-            codes[:, None] == lax.broadcasted_iota(jnp.int32, (tokens, vocabulary), 1)
-        ).astype(bf16)
-        inputs = nn(one_hot, embedding)
+        columns = lax.broadcasted_iota(jnp.int32, (tokens, vocabulary), 1)
+        inputs = nn((codes.reshape(tokens, 1) == columns).astype(bf16), embedding)
+        codes_plane = spread(codes.reshape(1, tokens))
         own_segments = jnp.where(is_encoder, encoder_segments, target_segments)
         earlier = lax.broadcasted_iota(jnp.int32, (length, length), 1) <= lax.broadcasted_iota(
             jnp.int32, (length, length), 0
@@ -525,7 +539,8 @@
         gain_self = own_gains[:1].astype(f32)
 
         normed_plane = spread(rms_norm(inputs, gain_self).astype(bf16))
-        moved, *normed_plane = together(moved, *normed_plane)
+        moved, *planes = together(moved, *normed_plane, *codes_plane)
+        normed_plane, codes_plane = planes[:PLANE], planes[PLANE:]
         pack_e, pack_d = lax.optimization_barrier(
             (
                 jnp.concatenate([widen_e, moved[:padded_narrow]], 0),
@@ -538,13 +553,13 @@
         projected_parts = [
             nt(in_column, block).astype(bf16).reshape(lines, in_cols, tokens) for block in normed_plane
         ]
-        projected = ordered(
-            projected_parts[0],
-            [(j ^ k, hop(projected_parts[k], k)) for k in range(1, PLANE)],
-            j,
-            1,
-        ).reshape(3 * inner, tokens)
-        out_w = gather_plane(column[:, in_cols : in_cols + cross_cols], 1).reshape(-1, width)
+        hopped = together(*[hop(projected_parts[k], k) for k in range(1, PLANE)], column)
+        column = hopped[-1]
+        projected = in_plane([projected_parts[0], *hopped[:-1]], 1).reshape(3 * inner, tokens)
+        out_pieces = together(*spread(column[:, in_cols : in_cols + cross_cols]), column)
+        column = out_pieces[-1]
+        out_w = in_plane(out_pieces[:-1], 1).reshape(inner, width)
+        cross_pieces = spread(column[:, in_cols + cross_cols :])
         row_f32, row_bf16 = ((length, width), f32), ((length, width), bf16)
         context, first_kept, first_sent = call(
             self_forward_kernel,
@@ -565,102 +580,52 @@
             gains_e,
             gains_d,
         )
+        normed_first, *cross_pieces = together(normed_first, *cross_pieces)
         stream_e = spread(normed_first)
-        cross_rows, *stream_e = together(column[:, in_cols + cross_cols :], *stream_e)
-        cross_pieces = spread(cross_rows)
         group = PLANE * length
         group_bf16 = ((group, width), bf16)
-        steps = lines // 2
         pack_shape = (lines, padded_widen + padded_narrow, width)
-        pack_specs = feed_specs(lines, padded_widen, width)
-        joined_scratch = pltpu.VMEM((group, width), bf16)
-        sum_scratch = pltpu.VMEM((group, width), f32)
-
-        def unit(*middle):
-            block = (1,) + middle + (padded_widen, group)
-            return (
-                (steps,) + block[1:],
-                bf16,
-                pl.BlockSpec(block, lambda step: (step,) + (0,) * (len(block) - 1)),
-            )
+        halves_of = pack_specs(lines, padded_widen, width)
+        units = lines * padded_narrow
+        unit_bf16, pair_bf16, trio_bf16 = (((n * units, group), bf16) for n in (1, 2, 3))
+        blocks_bf16 = (row_bf16,) * PLANE
 
         def with_packs(first, *packs):
-            specs = {first + 3 * i + k: pack_specs[k] for i in range(len(packs)) for k in range(3)}
-            return [pack for pack in packs for _ in range(3)], specs
-
-        def feed_forward(stream, pack, *priors):
-            packs, specs = with_packs(4, pack)
-            return call(
-                functools.partial(feed_forward_kernel, len(priors)),
-                (unit(1), unit(1), unit(1), group_bf16),
-                *stream,
-                *packs,
-                *priors,
-                scratch=(joined_scratch, sum_scratch),
-                steps=steps,
-                specs=specs,
-            )
-
-        def feed_back(output_grad, packs, saved, ties):
-            packs, specs = with_packs(4, *packs)
-            specs.update({10 + i: unit(1)[2] for i in range(4)})
-            return call(
-                feed_back_kernel,
-                (unit(2), unit(2), group_bf16),
-                *output_grad,
-                *packs,
-                *saved,
-                scratch=(joined_scratch, sum_scratch),
-                steps=steps,
-                specs=specs,
-                time_us=8,
-                ties=ties,
-            )
-
-        def feed_both(stream, output_grad, pack, *priors, ties=()):
-            packs, specs = with_packs(8, pack)
-            return call(
-                functools.partial(feed_both_kernel, len(priors)),
-                (unit(1), unit(2), group_bf16, group_bf16),
-                *stream,
-                *output_grad,
-                *packs,
-                *priors,
-                scratch=(joined_scratch, joined_scratch, sum_scratch, sum_scratch),
-                steps=steps,
-                specs=specs,
-                time_us=8,
-                ties=ties,
-            )
-
-        def feed_grads(stream, output_grad, grads, hidden):
-            specs = {8 + i: unit(2)[2] for i in range(2)}
-            specs.update({10 + i: unit(1)[2] for i in range(2)})
-            own, other = call(
-                feed_grads_kernel,
-                ((pack_shape, bf16), (pack_shape, bf16)),
-                *stream,
-                *output_grad,
-                *grads,
-                *hidden,
-                scratch=(joined_scratch, joined_scratch),
-                steps=steps,
-                specs=specs,
-                time_us=9,
-            )
-            return (own.astype(f32) + swap(other).astype(f32)).astype(bf16)
+            specs = {first + 2 * i + k: halves_of[k] for i in range(len(packs)) for k in range(2)}
+            return dict(specs=specs), [pack for pack in packs for _ in range(2)]
+
+        def feed_grads(own, other, *ties):
+            (pack,) = call(feed_grads_kernel, ((pack_shape, bf16),), *own, *other, time_us=0.3, ties=ties)
+            return pack
 
         own_e, *stream_e = together(own_e, *stream_e)
         other_e = swap(own_e)
-        value_own, slope_own, hidden_own, part_own = feed_forward(stream_e, own_e)
-        value_other, slope_other, hidden_other, part_e = feed_forward(stream_e, other_e, part_own)
-
-        part_e, *cross_pieces = together(part_e, *cross_pieces)
+        cotangent_d, *stream_e = together(cotangent_d, *stream_e)
+        options, packs = with_packs(4, own_e)
+        value_own, slope_own, hidden_own, part_own, x_e = call(
+            feed_forward_own_kernel,
+            (unit_bf16, unit_bf16, unit_bf16, group_bf16, group_bf16),
+            *stream_e,
+            *packs,
+            **options,
+        )
+        output_grad_d = spread(cotangent_d)
+        x_e, *cross_pieces = together(x_e, *cross_pieces)
         cross_w = in_plane(cross_pieces, 1).reshape(devices, 2, cross_cols, width).swapaxes(0, 1)
-        cross_w = cross_w.reshape(-1, width)
+        cross_w = cross_w.reshape(2 * inner, width)
         cross_e, cross_d = by_section(cross_w, swap(cross_w))
-        cotangent_d, cross_w = together(cotangent_d, cross_w)
-        output_grad_d = spread(cotangent_d)
+        options, packs = with_packs(2, other_e)
+        value_other, slope_other, hidden_other, *part_e = call(
+            feed_forward_other_kernel,
+            (unit_bf16, unit_bf16, unit_bf16, *blocks_bf16),
+            x_e,
+            part_own,
+            *packs,
+            **options,
+        )
+        *part_e, output_grad_d[1], output_grad_d[2], output_grad_d[3] = together(
+            *part_e, *output_grad_d[1:]
+        )
 
         second_e, normed_final, cross_queries, states, cross_context, second_d, normed_last = call(
             middle_kernel,
@@ -685,18 +650,39 @@
         )
 
         stream_d = spread(normed_last)
-        own_d, in_rows, *stream_d = together(own_d, column[:, :in_cols], *stream_d)
-        in_pieces = [in_rows, hop(in_rows, 1), hop(in_rows, 2)]
+        own_d, *stream_d = together(own_d, *stream_d)
         other_d = swap(own_d)
-        hidden_own_d, grads_own_d, part_d, back_d = feed_both(stream_d, output_grad_d, own_d)
-        hidden_other_d, grads_other_d, part_d, back_d = feed_both(
-            stream_d, output_grad_d, other_d, part_d, back_d, ties=in_pieces[1:]
-        )
+        options, packs = with_packs(8, own_d)
+        factors_d, part_own, back_own, x_d, joined_grad_d = call(
+            feed_both_own_kernel,
+            (trio_bf16, group_bf16, group_bf16, group_bf16, group_bf16),
+            *stream_d,
+            *output_grad_d,
+            *packs,
+            **options,
+        )
+        options, packs = with_packs(4, other_d)
+        factors_other_d, *blocks = call(
+            feed_both_other_kernel,
+            (trio_bf16, *blocks_bf16, *blocks_bf16),
+            x_d,
+            joined_grad_d,
+            part_own,
+            back_own,
+            *packs,
+            **options,
+        )
+        feed_sum_d = feed_grads(
+            (x_d, joined_grad_d, factors_d),
+            (swap(x_d), swap(joined_grad_d), swap(factors_other_d)),
+        )
+        feed_sum_d, *blocks = together(feed_sum_d, *blocks)
+        back_d, part_d = collected(blocks[:PLANE]), blocks[PLANE:]
         gain_shape = ((1, width), f32)
         stream_two_d, cross_branch, cross_grads, stream_two_e, sent_e, gain_two_d, gain_two_e = call(
             middle_back_kernel,
             (row_f32, row_bf16, ((3 * inner, length), bf16), row_f32, row_bf16, gain_shape, gain_shape),
-            *collected(back_d),
+            *back_d,
             second_d,
             second_e,
             cotangent_d,
@@ -710,17 +696,6 @@
             cross_allowed,
         )
 
-        output_grad_e = spread(sent_e)
-        feed_sum_d = feed_grads(
-            stream_d, output_grad_d, (grads_own_d, grads_other_d), (hidden_own_d, hidden_other_d)
-        )
-        grads_own_e, grads_other_e, back_e = feed_back(
-            output_grad_e,
-            (own_e, other_e),
-            (value_own, slope_own, value_other, slope_other),
-            (feed_sum_d,),
-        )
-
         stream_one_d, gain_one_d = call(
             first_back_d_kernel,
             (row_f32, gain_shape),
@@ -730,13 +705,7 @@
             gains_d,
             stream_two_d,
         )
-        feed_sum_e = feed_grads(
-            stream_e, output_grad_e, (grads_own_e, grads_other_e), (hidden_own, hidden_other)
-        )
-        summed_d = lax.psum_scatter(feed_sum_d, "line", scatter_dimension=0)
-        feed_sum_e, summed_d = together(feed_sum_e, summed_d)
-        summed_e = lax.psum_scatter(feed_sum_e, "line", scatter_dimension=0)
-
+        output_grad_e = together(*spread(sent_e))
         cross_kept, cross_sent = call(
             cross_grads_kernel,
             (((2 * inner, width), bf16), ((2 * inner, width), bf16)),
@@ -746,23 +715,51 @@
             normed_cross,
             cross_context,
             cross_branch,
-            ties=(back_e,),
-        )
+        )
+        cross_grad = (cross_kept.astype(f32) + swap(cross_sent).astype(f32)).astype(bf16)
+        options, packs = with_packs(4, own_e, other_e)
+        grads_own, grads_other, joined_grad_e, *back_e = call(
+            feed_back_kernel,
+            (pair_bf16, pair_bf16, group_bf16, *blocks_bf16),
+            *output_grad_e,
+            *packs,
+            value_own,
+            slope_own,
+            value_other,
+            slope_other,
+            ties=(stream_one_d, cross_kept),
+            time_us=0.3,
+            **options,
+        )
+        def by_plane(*products):
+            parts = [m.astype(bf16).reshape(lines, PLANE, -1, width).swapaxes(0, 1) for m in products]
+            return jnp.concatenate(parts, 2)
+
+        cross_terms = scattered(by_plane(cross_grad[:inner], cross_grad[inner:]))
+        feed_sum_e = feed_grads(
+            (x_e, joined_grad_e, grads_own, hidden_own),
+            (swap(x_e), swap(joined_grad_e), swap(grads_other), swap(hidden_other)),
+        )
+        feed_sum_e, *blocks = together(feed_sum_e, *back_e, *cross_terms)
+        back_e, cross_terms = blocks[:PLANE], blocks[PLANE:]
+        back_e = collected(back_e)
+
+        summed_d = lax.psum_scatter(feed_sum_d, "line", scatter_dimension=0)
+        feed_sum_e, summed_d = together(feed_sum_e, summed_d)
+        summed_e = lax.psum_scatter(feed_sum_e, "line", scatter_dimension=0)
 
         stream_kept, stream_sent, gain_one_e = call(
             first_back_e_kernel,
             (row_f32, row_f32, gain_shape),
-            *collected(back_e),
+            *back_e,
             section_scalar,
             first_e,
             gains_e,
             stream_two_e,
             stream_one_d,
-        )
-        in_rows, part_d, stream_kept = together(in_rows, part_d, stream_kept)
-        in_pieces.append(hop(in_rows, 3))
-        in_w = in_plane(in_pieces, 1).reshape(-1, width)
-        stream_got, cross_sent = together(swap(stream_sent), cross_sent)
+            ties=(feed_sum_e,),
+        )
+        stream_got = swap(stream_sent)
         stream_one, branch_grad, projected_grad = call(
             self_back_kernel,
             (((tokens, width), f32), ((tokens, width), bf16), ((3 * inner, tokens), bf16)),
@@ -772,75 +769,63 @@
             out_w,
             projected,
             allowed,
-            ties=(feed_sum_e,),
-        )
-        def scatter_parts(*products):
-            parts = [m.astype(bf16).reshape(lines, PLANE, -1, width).swapaxes(0, 1) for m in products]
-            return scatter_plane(jnp.concatenate(parts, 2)).astype(bf16)
-
-        cross_grad = (cross_kept.astype(f32) + swap(cross_sent).astype(f32)).astype(bf16)
-        cross_part = scatter_parts(cross_grad[:inner], cross_grad[inner:])
-        second_out_d = second_d + sum(
-            part.astype(f32) for part in collected(part_d)
-        )
-        out_part = scatter_parts(nn(context, branch_grad))
+        )
         parts = projected_grad.reshape(lines, PLANE, in_cols, tokens)
         grad_parts = [at(parts, j, 1)] + [hop(at(parts, j ^ k, 1), k) for k in range(1, PLANE)]
+        branch_grad, *grad_parts = together(
+            branch_grad, *[part.reshape(lines * in_cols, tokens) for part in grad_parts]
+        )
+        out_part = total_of(scattered(by_plane(nn(context, branch_grad)))).astype(bf16)
+        cross_part = total_of(cross_terms).astype(bf16)
         (in_part,) = call(
             in_grad_kernel,
             (((lines * in_cols, width), bf16),),
-            *[part.reshape(lines * in_cols, tokens) for part in grad_parts],
+            *grad_parts,
             *normed_plane,
-            ties=(cross_part, out_part),
-        )
-        rest_sum = scatter_line(
-            jnp.concatenate([in_part.reshape(lines, in_cols, width), cross_part, out_part], 1)
-        )
-        table_grad, gain_zero = call(
+        )
+        padded = -(-(vocabulary + 6) // 64) * 64
+        (small,) = call(
             table_kernel,
-            (((vocabulary, width), bf16), gain_shape),
-            projected_grad,
-            in_w,
-            inputs,
+            (((padded, width), bf16),),
+            *grad_parts,
+            *codes_plane,
+            gain_one_e,
+            gain_two_e,
+            gain_one_d,
+            gain_two_d,
+            section_scalar,
+            in_column,
+            embedding,
             gain_self,
             stream_one,
-            one_hot,
-            ties=(in_part,),
-        )
-
-        zero_row = jnp.zeros_like(gain_zero)
-        gain_rows = jnp.concatenate(
-            [
-                jnp.where(is_encoder, gain_zero, zero_row),
-                gain_one_e,
-                gain_two_e,
-                jnp.where(is_encoder, zero_row, gain_zero),
-                gain_one_d,
-                gain_two_d,
-            ],
-            0,
-        ).astype(bf16)
-        padded = -(-(vocabulary + 6) // 64) * 64
-        padding = jnp.zeros((padded - vocabulary - 6, width), bf16)
-        small = jnp.concatenate([table_grad, gain_rows, padding], 0).reshape(2, padded // 2, width)
-        chip_sum = at(small, section).astype(f32) + swap(at(small, 1 - section)).astype(f32)
-        plane_sum = rounded(scatter_plane(chip_sum.astype(bf16).reshape(PLANE, -1, width)))
+            specs={4 + k: whole((1, tokens)) for k in range(PLANE)},
+        )
+        plane_sum = rounded(total_of(scattered(small.reshape(PLANE, -1, width))))
         plane_sum, summed_e = together(plane_sum, summed_e)
-        rest_sum, summed_e = together(rest_sum, summed_e)
-        half_sum = gather_plane(sum_line(plane_sum)).reshape(padded // 2, width)
-        small_sum = in_order(half_sum, swap(half_sum)).astype(f32)
-        embedding_grad = small_sum[:vocabulary]
-        gains_grad = at(small_sum[vocabulary : vocabulary + 6].reshape(2, 3, width), section)[None]
-
-        back = permute(
-            jnp.concatenate([summed_e[padded_widen:], summed_d[padded_widen:]], 0),
-            AXES,
-            [(b, a) for a, b in narrow_route],
-        )
-        halves_e = jnp.concatenate([summed_e[:padded_widen], back[:padded_narrow]], 0)
-        halves_d = jnp.concatenate([summed_d[:padded_widen], back[padded_narrow:]], 0)
-        half_kept, half_sent = by_section(halves_e, halves_d)
-        both = in_order(half_kept[None], swap(half_sent)[None])
+        chip_sum = rounded(plane_sum.astype(f32) + swap(plane_sum).astype(f32))
+        rest_pack = jnp.concatenate([in_part.reshape(lines, in_cols, width), cross_part, out_part], 1)
+        rest_pack, line_sum = together(rest_pack, sum_line(chip_sum))
+        rest_sum = lax.psum_scatter(rest_pack, "line", scatter_dimension=0).astype(f32)
+        pieces = together(*spread(line_sum), *part_d)
+        pieces[PLANE:] = collected(pieces[PLANE:])
+        second_out_d = second_d + sum(part.astype(f32) for part in pieces[PLANE:])
+        embedding_grad, gains_grad = call(
+            assemble_kernel,
+            (((vocabulary, width), f32), ((1, 3, width), f32)),
+            section_scalar,
+            j.astype(jnp.int32).reshape(1),
+            *pieces[:PLANE],
+            scratch=(pltpu.VMEM((padded, width), f32),),
+        )
+
+        def returned(summed, receiver):
+            narrow = permute(summed[padded_widen:], AXES, [(b, a) for a, b in narrow_route])
+            half = jnp.concatenate([summed[:padded_widen], narrow], 0)
+            return half, permute(half, "section", [(1 - receiver, receiver)])
+
+        half_d, got_d = returned(summed_d, 1)
+        half_e, got_e = returned(summed_e, 0)
+        both = jnp.where(is_encoder, jnp.stack([half_e, got_e]), jnp.stack([got_d, half_d]))
         both = both.reshape(2, 3, padded_narrow, width)[:, :, :narrow_half]
         widen_t = both[:, :2].reshape(2 * widen_half, width)
         narrow_grad = both[:, 2].reshape(2 * narrow_half, width).astype(f32)

time: 615 us -> 575 us (0.935)
  waiting for transfers between devices: 257 us -> 229 us
  other arithmetic: 49.2 us -> 33.3 us
    ppermute x79, waiting for transfers between devices: 229 us -> 211 us  [permute(): return lax.ppermute(block, axes, route).reshape(shape)]
    convert_element_type x7 -> x3, other arithmetic: 18.8 us -> 3.59 us  [the longest x1 2.35 us: per_device(): cross_part = total_of(cross_terms).astype(bf16)]
    all_gather x1, waiting for transfers between devices: 14.7 us -> 0.01 us  [per_device(): own_e = lax.all_gather(pack_e, 'line', axis=0)]
    unnamed x127 -> x152, local copies, waits for them, and re-layouts: 16 us -> 24.1 us
    pallas_call x17 -> x18, Pallas kernels: 130 us -> 132 us  [call(): pl.pallas_call(lambda *refs: kernel(*refs[:first], *refs[after:]), grid=(...]
  transfers between devices with their start and end apart: 84 -> 85, of which waited for: 46 -> 39; matrix products, arithmetic and copies ran while one was open for 13% -> 10% of each run, Pallas kernels for 18% -> 22%
where the time goes in v3:
time: 575 us; the launch traced here: 564 us
  waiting for transfers between devices  229 us (40%)
  Pallas kernels  132 us (23%)
  starting transfers between devices  107 us (19%)
  local copies, waits for them, and re-layouts  42.3 us (7%)
  other arithmetic  33.3 us (6%)
  between operations  15.5 us (3%)
    ppermute x79, waiting for transfers between devices, permute(): return lax.ppermute(block, axes, route).reshape(shape)  211 us
    pallas_call x18, Pallas kernels, call(): pl.pallas_call(lambda *refs: kernel(*refs[:first], *refs[after:]), grid=(...  132 us
    ppermute x79, starting transfers between devices, permute(): return lax.ppermute(block, axes, route).reshape(shape)  106 us
    unnamed x152, local copies, waits for them, and re-layouts  24.1 us
    all_gather x1, waiting for transfers between devices, per_device(): own_d = lax.all_gather(pack_d, 'line', axis=0)  12.2 us
  transfers between devices with their start and end apart: 85, of which 39 were waited for; matrix products, arithmetic and copies ran while one was open for 10% of the time, Pallas kernels for 22%

profile of v3, /device:TPU:0, one launch (start us, length us, event | category | flops | bytes accessed | tf_op | source)
XLA Modules:
  0.0 563.9 jit_solution(18414342640352008409)
XLA Ops:
  21.0 13.9 %collective-permute-done.7.refs_5_ = s32[1,256]{1,0:T(1,128)S(1)} collective-permute-done((s32[1,256]{1,0:T(1,128)S(1)}, s32[1,256]{1,0:T(1,128)S(1)}, u32[]{:S(2)}, u32[]{:S(2)}) %collective-permute-start.7) | collective-permute-done | bytes 1056 | tf_op jit(solution)/shard_map/ppermute | solution.py:38
  41.0 14.5 %collective-permute-done.9.refs_7_ = s32[1,256]{1,0:T(1,128)S(1)} collective-permute-done((s32[1,256]{1,0:T(1,128)S(1)}, s32[1,256]{1,0:T(1,128)S(1)}, u32[]{:S(2)}, u32[]{:S(2)}) %collective-permute-start.9) | collective-permute-done | bytes 1056 | tf_op jit(solution)/shard_map/ppermute | solution.py:38
  59.4 17.4 %collective-permute-start = (bf16[131,1472]{1,0:T(8,128)(2,1)}, bf16[131,1472]{1,0:T(8,128)(2,1)}, u32[]{:S(2)}, u32[]{:S(2)}) collective-permute-start(bf16[131,1472]{1,0:T(8,128)(2,1)} %pad_maximum_fusion.7), channel_id=1, source_target_pairs={{0,16},{16,0},{1,17},{17,1},{2,18},{18,2},{3,19},{19,3},{4,20},{20... | collective-permute-start | bytes 1157000 | tf_op jit(solution)/shard_map/ppermute | solution.py:38
  94.9 6.4 %collective-permute-done.13 = bf16[4,24,1472]{2,1,0:T(8,128)(2,1)S(1)} collective-permute-done((bf16[4,24,1472]{2,1,0:T(8,128)(2,1)S(1)}, bf16[4,24,1472]{2,1,0:T(8,128)(2,1)S(1)}, u32[]{:S(2)}, u32[]{:S(2)}) %collective-permute-start.13) | collective-permute-done | bytes 282656 | tf_op jit(solution)/shard_map/ppermute | solution.py:38
  101.3 5.8 %collective-permute-done.14 = bf16[4,24,1472]{2,1,0:T(8,128)(2,1)S(1)} collective-permute-done((bf16[4,24,1472]{2,1,0:T(8,128)(2,1)S(1)}, bf16[4,24,1472]{2,1,0:T(8,128)(2,1)S(1)}, u32[]{:S(2)}, u32[]{:S(2)}) %collective-permute-start.14) | collective-permute-done | bytes 282656 | tf_op jit(solution)/shard_map/ppermute | solution.py:38
  108.4 5.9 %shard_map.187 = (bf16[384,256]{1,0:T(8,128)(2,1)}, f32[128,1472]{1,0:T(8,128)}, f32[128,1472]{1,0:T(8,128)}) custom-call(s32[1]{0:T(128)} %bitcast.32.refs_0_.refs_4_.refs_12_, bf16[1152,256]{1,0:T(8,128)(2,1)} %bitcast.357, f32[2,128,128]{2,1,0:T(8,128)} %and_convert_fusion.refs_2_.refs_5_, f32[256,1472]{1,0:T(8,128)} %copy-done.2, bf16[384,1472]{1,0:T(8,128)(2,1)} %bitcast.347), custom_call_target="tpu_custom_call" | custom-call | flops 240000000 | bytes 750000 | tf_op jit(solution)/shard_map/pallas_call | solution.py:79
  123.5 7.0 %collective-permute-done.17 = bf16[4,48,1472]{2,1,0:T(8,128)(2,1)S(1)} collective-permute-done((bf16[4,48,1472]{2,1,0:T(8,128)(2,1)S(1)}, bf16[4,48,1472]{2,1,0:T(8,128)(2,1)S(1)}, u32[]{:S(2)}, u32[]{:S(2)}) %collective-permute-start.17) | collective-permute-done | bytes 565280 | tf_op jit(solution)/shard_map/ppermute | solution.py:38
  130.5 12.6 %collective-permute-done.18 = bf16[4,48,1472]{2,1,0:T(8,128)(2,1)S(1)} collective-permute-done((bf16[4,48,1472]{2,1,0:T(8,128)(2,1)S(1)}, bf16[4,48,1472]{2,1,0:T(8,128)(2,1)S(1)}, u32[]{:S(2)}, u32[]{:S(2)}) %collective-permute-start.18) | collective-permute-done | bytes 565280 | tf_op jit(solution)/shard_map/ppermute | solution.py:38
  148.4 7.0 %collective-permute-done.20 = bf16[16,8,1472]{2,1,0:T(8,128)(2,1)S(1)} collective-permute-done((bf16[16,8,1472]{2,1,0:T(8,128)(2,1)}, bf16[16,8,1472]{2,1,0:T(8,128)(2,1)S(1)}, u32[]{:S(2)}, u32[]{:S(2)}) %collective-permute-start.20) | collective-permute-done | bytes 376864 | tf_op jit(solution)/shard_map/ppermute | solution.py:38
  155.4 6.3 %collective-permute-done.21 = bf16[16,8,1472]{2,1,0:T(8,128)(2,1)} collective-permute-done((bf16[16,8,1472]{2,1,0:T(8,128)(2,1)}, bf16[16,8,1472]{2,1,0:T(8,128)(2,1)}, u32[]{:S(2)}, u32[]{:S(2)}) %collective-permute-start.21) | collective-permute-done | bytes 376864 | tf_op jit(solution)/shard_map/ppermute | solution.py:38
  163.3 7.6 %shard_map.189 = (bf16[448,512]{1,0:T(8,128)(2,1)}, bf16[448,512]{1,0:T(8,128)(2,1)}, bf16[448,512]{1,0:T(8,128)(2,1)}, bf16[512,1472]{1,0:T(8,128)(2,1)}, bf16[512,1472]{1,0:T(8,128)(2,1)}) custom-call(bf16[128,1472]{1,0:T(8,128)(2,1)} %get-tuple-element.195.refs_0_, bf16[128,1472]{1,0:T(8,128)(2,1)} %bitcast.417, bf16[128,1472]{1,0:T(8,128)(2,1)} %bitcast.57.refs_2_, ...), custom_call_target="tpu_custom_call" | custom-call | flops 240000000 | bytes 750000 | tf_op jit(solution)/shard_map/pallas_call | solution.py:79
  179.5 7.1 %shard_map.190 = (bf16[448,512]{1,0:T(8,128)(2,1)}, bf16[448,512]{1,0:T(8,128)(2,1)}, bf16[448,512]{1,0:T(8,128)(2,1)}, bf16[128,1472]{1,0:T(8,128)(2,1)}, bf16[...) custom-call(bf16[512,1472]{1,0:T(8,128)(2,1)} %get-tuple-element.205.refs_0_, ...), custom_call_target="tpu_custom_call" | custom-call | flops 240000000 | bytes 750000 | tf_op jit(solution)/shard_map/pallas_call | solution.py:79
  205.1 7.9 %collective-permute-done.28 = bf16[16,8,1472]{2,1,0:T(8,128)(2,1)S(1)} collective-permute-done((bf16[16,8,1472]{2,1,0:T(8,128)(2,1)}, bf16[16,8,1472]{2,1,0:T(8,128)(2,1)S(1)}, u32[]{:S(2)}, u32[]{:S(2)}) %collective-permute-start.28) | collective-permute-done | bytes 376864 | tf_op jit(solution)/shard_map/ppermute | solution.py:38
  213.8 8.7 %shard_map.191 = (f32[128,1472]{1,0:T(8,128)}, bf16[128,1472]{1,0:T(8,128)(2,1)}, bf16[384,128]{1,0:T(8,128)(2,1)}, bf16[768,128]{1,0:T(8,128)(2,1)}, bf16[384,1...) custom-call(bf16[128,1472]{1,0:T(8,128)(2,1)} %get-tuple-element.212.refs_0_, ...), custom_call_target="tpu_custom_call" | custom-call | flops 240000000 | bytes 750000 | tf_op jit(solution)/shard_map/pallas_call | solution.py:79
  226.0 12.2 %all-gather.11.cloned.1.call-done = bf16[1344,1472]{1,0:T(8,128)(2,1)} async-done(((bf16[336,1472]{1,0:T(8,128)(2,1)}), bf16[1344,1472]{1,0:T(8,128)(2,1)}) %all-gather.11.cloned.1.call-update) | async-done | bytes 3956752 | tf_op jit(solution)/shard_map/all_gather | solution.py:551
  241.0 9.9 %shard_map.192 = (bf16[1344,512]{1,0:T(8,128)(2,1)}, bf16[512,1472]{1,0:T(8,128)(2,1)}, bf16[512,1472]{1,0:T(8,128)(2,1)}, bf16[512,1472]{1,0:T(8,128)(2,1)}, bf16[512,1472]{1,0:T(8,128)(2,1)}) custom-call(bf16[128,1472]{1,0:T(8,128)(2,1)} %get-tuple-element.227.refs_0_, bf16[128,1472]{1,0:T(8,128)(2,1)} %bitcast.420, bf16[128,1472]{1,0:T(8,128)(2,1)} %bitcast.423, ...), custom_call_target="tpu_custom_call" | custom-call | flops 240000000 | bytes 750000 | tf_op jit(solution)/shard_map/pallas_call | solution.py:79
  253.5 10.7 %shard_map.193 = (bf16[1344,512]{1,0:T(8,128)(2,1)}, bf16[128,1472]{1,0:T(8,128)(2,1)}, bf16[128,1472]{1,0:T(8,128)(2,1)}, bf16[128,1472]{1,0:T(8,128)(2,1)}, bf...) custom-call(bf16[512,1472]{1,0:T(8,128)(2,1)} %get-tuple-element.235, ...), custom_call_target="tpu_custom_call" | custom-call | flops 240000000 | bytes 750000 | tf_op jit(solution)/shard_map/pallas_call | solution.py:79
  268.7 10.1 %shard_map.194 = bf16[4,336,1472]{2,1,0:T(8,128)(2,1)} custom-call(bf16[512,1472]{1,0:T(8,128)(2,1)} %get-tuple-element.235.refs_0_, bf16[512,1472]{1,0:T(8,128)(2,1)} %get-tuple-element.236.refs_1_, bf16[1344,512]{1,0:T(8,128)(2,1)} %get-tuple-element.237.refs_2_, bf16[512,1472]{1,0:T(8,128)(2,1)} %bitcast.378, bf16[512,1472]{1,0:T(8,128)(2,1)} %bitcast.379, ...), custom_call_target="tpu_custom_call" | custom-call | flops 240000000 | bytes 750000 | tf_op jit(solution)/shard_map/pallas_call | solution.py:79
  283.3 9.4 %collective-permute-done.40 = bf16[16,8,1472]{2,1,0:T(8,128)(2,1)S(1)} collective-permute-done((bf16[16,8,1472]{2,1,0:T(8,128)(2,1)S(1)}, bf16[16,8,1472]{2,1,0:T(8,128)(2,1)S(1)}, u32[]{:S(2)}, u32[]{:S(2)}) %collective-permute-start.40) | collective-permute-done | bytes 376864 | tf_op jit(solution)/shard_map/ppermute | solution.py:38
  292.7 7.8 %collective-permute-done.38 = bf16[16,8,1472]{2,1,0:T(8,128)(2,1)S(1)} collective-permute-done((bf16[16,8,1472]{2,1,0:T(8,128)(2,1)S(1)}, bf16[16,8,1472]{2,1,0:T(8,128)(2,1)S(1)}, u32[]{:S(2)}, u32[]{:S(2)}) %collective-permute-start.38) | collective-permute-done | bytes 376864 | tf_op jit(solution)/shard_map/ppermute | solution.py:38
  301.5 9.2 %shard_map.195 = (f32[128,1472]{1,0:T(8,128)}, bf16[128,1472]{1,0:T(8,128)(2,1)}, bf16[1152,128]{1,0:T(8,128)(2,1)}, f32[128,1472]{1,0:T(8,128)}, bf16[128,1472]...) custom-call(bf16[128,1472]{1,0:T(8,128)(2,1)} %get-tuple-element.249.refs_0_, bf16[128,1472]{1,0:T(8,128)(2,1)} %bitcast.422, ...), custom_call_target="tpu_custom_call" | custom-call | flops 240000000 | bytes 750000 | tf_op jit(solution)/shard_map/pallas_call | solution.py:79
  327.8 9.0 %collective-permute-done.42 = bf16[16,8,1472]{2,1,0:T(8,128)(2,1)S(1)} collective-permute-done((bf16[16,8,1472]{2,1,0:T(8,128)(2,1)}, bf16[16,8,1472]{2,1,0:T(8,128)(2,1)S(1)}, u32[]{:S(2)}, u32[]{:S(2)}) %collective-permute-start.42) | collective-permute-done | bytes 376864 | tf_op jit(solution)/shard_map/ppermute | solution.py:38
  337.7 11.3 %shard_map.198 = (bf16[896,512]{1,0:T(8,128)(2,1)}, bf16[896,512]{1,0:T(8,128)(2,1)}, bf16[512,1472]{1,0:T(8,128)(2,1)}, bf16[128,1472]{1,0:T(8,128)(2,1)}, bf16...) custom-call(bf16[128,1472]{1,0:T(8,128)(2,1)} %get-tuple-element.256.refs_0_, ...), custom_call_target="tpu_custom_call" | custom-call | flops 240000000 | bytes 750000 | tf_op jit(solution)/shard_map/pallas_call | solution.py:79
  355.1 10.2 %shard_map.199.refs_9_ = bf16[4,336,1472]{2,1,0:T(8,128)(2,1)} custom-call(bf16[512,1472]{1,0:T(8,128)(2,1)} %get-tuple-element.205.refs_0_, bf16[512,1472]{1,0:T(8,128)(2,1)} %get-tuple-element.271.refs_1_, bf16[896,512]{1,0:T(8,128)(2,1)} %get-tuple-element.272.refs_2_, bf16[448,512]{1,0:T(8,128)(2,1)} %get-tuple-element.273.refs_3_, ...), custom_call_target="tpu_custom_call" | custom-call | flops 240000000 | bytes 750000 | tf_op jit(solution)/shard_map/pallas_call | solution.py:79
  368.0 12.4 %collective-permute-done.50 = bf16[4,48,1472]{2,1,0:T(8,128)(2,1)} collective-permute-done((bf16[4,48,1472]{2,1,0:T(8,128)(2,1)}, bf16[4,48,1472]{2,1,0:T(8,128)(2,1)}, u32[]{:S(2)}, u32[]{:S(2)}) %collective-permute-start.50) | collective-permute-done | bytes 565280 | tf_op jit(solution)/shard_map/ppermute | solution.py:38
  384.9 8.6 %collective-permute-done.52 = bf16[16,8,1472]{2,1,0:T(8,128)(2,1)S(1)} collective-permute-done((bf16[16,8,1472]{2,1,0:T(8,128)(2,1)S(1)}, bf16[16,8,1472]{2,1,0:T(8,128)(2,1)S(1)}, u32[]{:S(2)}, u32[]{:S(2)}) %collective-permute-start.52) | collective-permute-done | bytes 376864 | tf_op jit(solution)/shard_map/ppermute | solution.py:38
  393.4 7.4 %collective-permute-done.53 = bf16[16,8,1472]{2,1,0:T(8,128)(2,1)S(1)} collective-permute-done((bf16[16,8,1472]{2,1,0:T(8,128)(2,1)S(1)}, bf16[16,8,1472]{2,1,0:T(8,128)(2,1)S(1)}, u32[]{:S(2)}, u32[]{:S(2)}) %collective-permute-start.53) | collective-permute-done | bytes 376864 | tf_op jit(solution)/shard_map/ppermute | solution.py:38
  409.3 8.7 %shard_map.201 = (f32[256,1472]{1,0:T(8,128)}, bf16[256,1472]{1,0:T(8,128)(2,1)}, bf16[1152,256]{1,0:T(8,128)(2,1)}) custom-call(s32[1]{0:T(128)} %bitcast.32.refs_0_.refs_4_.refs_12_, f32[128,1472]{1,0:T(8,128)} %get-tuple-element.289.refs_1_, f32[128,1472]{1,0:T(8,128)} %bitcast.395, bf16[384,1472]{1,0:T(8,128)(2,1)} %bitcast.348, ...), custom_call_target="tpu_custom_call" | custom-call | flops 240000000 | bytes 750000 | tf_op jit(solution)/shard_map/pallas_call | solution.py:79
  430.4 9.7 %shard_map.203 = bf16[448,1472]{1,0:T(8,128)(2,1)} custom-call(bf16[288,256]{1,0:T(8,128)(2,1)} %bitcast.387, bf16[288,256]{1,0:T(8,128)(2,1)} %bitcast.399, bf16[288,256]{1,0:T(8,128)(2,1)} %bitcast.401, bf16[288,256]{1,0:T(8,128)(2,1)} %bitcast.403, s32[1,256]{1,0:T(1,128)} %bitcast.448, s32[1,256]{1,0:T(1,128)} %copy-done.65, s32[1,256]{1,0:T(1,128)} %copy-done.66, ...), custom_call_target="tpu_custom_call" | custom-call | flops 240000000 | bytes 750000 | tf_op jit(solution)/shard_map/pallas_call | solution.py:79
  451.9 7.7 %collective-permute-start.78 = (bf16[42,8,1472]{2,1,0:T(8,128)(2,1)}, bf16[42,8,1472]{2,1,0:T(8,128)(2,1)}, u32[]{:S(2)}, u32[]{:S(2)}) collective-permute-start(bf16[42,8,1472]{2,1,0:T(8,128)(2,1)} %get-tuple-element.378), channel_id=1, source_target_pairs={{0,16},{1,17},{2,18},{3,19},{4,20},{5,21},{6,22},{7,23},{8,24},{9,... | collective-permute-start | bytes 2967560 | tf_op jit(solution)/shard_map/ppermute | solution.py:38
  479.6 7.1 %collective-permute-done.60 = bf16[4,24,1472]{2,1,0:T(8,128)(2,1)S(1)} collective-permute-done((bf16[4,24,1472]{2,1,0:T(8,128)(2,1)S(1)}, bf16[4,24,1472]{2,1,0:T(8,128)(2,1)S(1)}, u32[]{:S(2)}, u32[]{:S(2)}) %collective-permute-start.60) | collective-permute-done | bytes 282656 | tf_op jit(solution)/shard_map/ppermute | solution.py:38
  494.1 13.4 %collective-permute-done.67 = bf16[14,8,1472]{2,1,0:T(8,128)(2,1)S(1)} collective-permute-done((bf16[14,8,1472]{2,1,0:T(8,128)(2,1)S(1)}, bf16[14,8,1472]{2,1,0:T(8,128)(2,1)S(1)}, u32[]{:S(2)}, u32[]{:S(2)}) %collective-permute-start.67) | collective-permute-done | bytes 329760 | tf_op jit(solution)/shard_map/ppermute | solution.py:38
  (398 shorter events, 245.5 us)
Async XLA Ops:
  7.2 70.4 %all-gather.9.cloned.1.call-start = ((), (), s32[]{:S(2)}) async-start(), calls=%async_computation.7 | async-start | bytes 2211840 | tf_op jit(solution)/shard_map/all_gather | solution.py:503
  13.9 41.6 %collective-permute-start.4 = (bf16[32,8,1472]{2,1,0:T(8,128)(2,1)}, bf16[32,8,1472]{2,1,0:T(8,128)(2,1)S(1)}, u32[]{:S(2)}, u32[]{:S(2)}) collective-permute-start(bf16[32,8,1472]{2,1,0:T(8,128)(2,1)} %fusion.45), channel_id=1, source_target_pairs={{0,1},{1,0},{2,3},{3,2},{4,5},{5,4},{6,7},{7,6},{8,9},{9,8},{10,11... | collective-permute-start | bytes 2261000 | tf_op jit(solution)/shard_map/ppermute | solution.py:38
  16.4 39.2 %collective-permute-start.5 = (bf16[32,8,1472]{2,1,0:T(8,128)(2,1)}, bf16[32,8,1472]{2,1,0:T(8,128)(2,1)}, u32[]{:S(2)}, u32[]{:S(2)}) collective-permute-start(bf16[32,8,1472]{2,1,0:T(8,128)(2,1)} %fusion.45), channel_id=1, source_target_pairs={{0,2},{1,3},{2,0},{3,1},{4,6},{5,7},{6,4},{7,5},{8,10},{9,11},{10,... | collective-permute-start | bytes 2261000 | tf_op jit(solution)/shard_map/ppermute | solution.py:38
  18.5 19.1 %collective-permute-start.8 = (s32[1,256]{1,0:T(1,128)S(1)}, s32[1,256]{1,0:T(1,128)S(1)}, u32[]{:S(2)}, u32[]{:S(2)}) collective-permute-start(s32[1,256]{1,0:T(1,128)S(1)} %bitcast.451), channel_id=1, source_target_pairs={{0,2},{1,3},{2,0},{3,1},{4,6},{5,7},{6,4},{7,5},{8,10},{9,11},{10,... | collective-permute-start | bytes 3080 | tf_op jit(solution)/shard_map/ppermute | solution.py:38
  18.5 144.8 %all-gather.7.cloned.1.call-start = ((), (), s32[]{:S(2)}) async-start(), calls=%async_computation.6 | async-start | bytes 5160960 | tf_op jit(solution)/shard_map/all_gather | solution.py:550
  19.7 18.8 %collective-permute-start.1 = (bf16[28,8,1472]{2,1,0:T(8,128)(2,1)S(1)}, bf16[28,8,1472]{2,1,0:T(8,128)(2,1)S(1)}, u32[]{:S(2)}, u32[]{:S(2)}) collective-permute-start(bf16[28,8,1472]{2,1,0:T(8,128)(2,1)S(1)} %dynamic-slice_bitcast_fusion), channel_id=1, source_target_pairs={{0,16},{16,0},{1,17},{17,1},{2,18},{18,2},{3,19},{19,3},{4,20},{20... | collective-permute-start | bytes 1978376 | tf_op jit(solution)/shard_map/ppermute | solution.py:38
  34.9 20.7 %collective-permute-start.6 = (bf16[32,8,1472]{2,1,0:T(8,128)(2,1)}, bf16[32,8,1472]{2,1,0:T(8,128)(2,1)}, u32[]{:S(2)}, u32[]{:S(2)}) collective-permute-start(bf16[32,8,1472]{2,1,0:T(8,128)(2,1)} %fusion.45), channel_id=1, source_target_pairs={{0,3},{1,2},{2,1},{3,0},{4,7},{5,6},{6,5},{7,4},{8,11},{9,10},{10,... | collective-permute-start | bytes 2261000 | tf_op jit(solution)/shard_map/ppermute | solution.py:38
  57.2 181.0 %all-gather.11.cloned.1.call-start = ((), (), s32[]{:S(2)}) async-start(), calls=%async_computation.8 | async-start | bytes 5160960 | tf_op jit(solution)/shard_map/all_gather | solution.py:551
  59.4 58.9 %collective-permute-start = (bf16[131,1472]{1,0:T(8,128)(2,1)}, bf16[131,1472]{1,0:T(8,128)(2,1)}, u32[]{:S(2)}, u32[]{:S(2)}) collective-permute-start(bf16[131,1472]{1,0:T(8,128)(2,1)} %pad_maximum_fusion.7), channel_id=1, source_target_pairs={{0,16},{16,0},{1,17},{17,1},{2,18},{18,2},{3,19},{19,3},{4,20},{20... | collective-permute-start | bytes 1157000 | tf_op jit(solution)/shard_map/ppermute | solution.py:38
  115.0 28.1 %collective-permute-start.18 = (bf16[4,48,1472]{2,1,0:T(8,128)(2,1)S(1)}, bf16[4,48,1472]{2,1,0:T(8,128)(2,1)S(1)}, u32[]{:S(2)}, u32[]{:S(2)}) collective-permute-start(bf16[4,48,1472]{2,1,0:T(8,128)(2,1)S(1)} %slice.78), channel_id=1, source_target_pairs={{0,2},{1,3},{2,0},{3,1},{4,6},{5,7},{6,4},{7,5},{8,10},{9,11},{10,... | collective-permute-start | bytes 1695752 | tf_op jit(solution)/shard_map/ppermute | solution.py:38
  116.1 27.0 %collective-permute-start.19 = (bf16[4,48,1472]{2,1,0:T(8,128)(2,1)S(1)}, bf16[4,48,1472]{2,1,0:T(8,128)(2,1)}, u32[]{:S(2)}, u32[]{:S(2)}) collective-permute-start(bf16[4,48,1472]{2,1,0:T(8,128)(2,1)S(1)} %slice.78), channel_id=1, source_target_pairs={{0,3},{1,2},{2,1},{3,0},{4,7},{5,6},{6,5},{7,4},{8,11},{9,10},{10,... | collective-permute-start | bytes 1695752 | tf_op jit(solution)/shard_map/ppermute | solution.py:38
  118.1 262.3 %reduce-scatter.4.cloned.1.call-start = ((), (), s32[]{:S(2)}) async-start(), calls=%async_computation.3 | async-start | bytes 5160960 | tf_op jit(solution)/shard_map/reduce_scatter | solution.py:747
  145.0 18.3 %collective-permute-start.22 = (bf16[16,8,1472]{2,1,0:T(8,128)(2,1)}, bf16[16,8,1472]{2,1,0:T(8,128)(2,1)}, u32[]{:S(2)}, u32[]{:S(2)}) collective-permute-start(bf16[16,8,1472]{2,1,0:T(8,128)(2,1)} %bitcast.412), channel_id=1, source_target_pairs={{0,3},{1,2},{2,1},{3,0},{4,7},{5,6},{6,5},{7,4},{8,11},{9,10},{10,... | collective-permute-start | bytes 1130504 | tf_op jit(solution)/shard_map/ppermute | solution.py:38
  172.6 23.7 %collective-permute-start.30 = (bf16[96,8,1472]{2,1,0:T(8,128)(2,1)S(1)}, bf16[96,8,1472]{2,1,0:T(8,128)(2,1)}, u32[]{:S(2)}, u32[]{:S(2)}) collective-permute-start(bf16[96,8,1472]{2,1,0:T(8,128)(2,1)S(1)} %bitcast.350), channel_id=1, source_target_pairs={{0,16},{16,0},{1,17},{17,1},{2,18},{18,2},{3,19},{19,3},{4,20},{20... | collective-permute-start | bytes 6782984 | tf_op jit(solution)/shard_map/ppermute | solution.py:38
  173.5 18.5 %collective-permute-start.25 = (bf16[16,8,1472]{2,1,0:T(8,128)(2,1)S(1)}, bf16[16,8,1472]{2,1,0:T(8,128)(2,1)S(1)}, u32[]{:S(2)}, u32[]{:S(2)}) collective-permute-start(bf16[16,8,1472]{2,1,0:T(8,128)(2,1)S(1)} %bitcast.366), channel_id=1, source_target_pairs={{0,2},{1,3},{2,0},{3,1},{4,6},{5,7},{6,4},{7,5},{8,10},{9,11},{10,... | collective-permute-start | bytes 1130504 | tf_op jit(solution)/shard_map/ppermute | solution.py:38
  194.6 18.4 %collective-permute-start.28 = (bf16[16,8,1472]{2,1,0:T(8,128)(2,1)}, bf16[16,8,1472]{2,1,0:T(8,128)(2,1)S(1)}, u32[]{:S(2)}, u32[]{:S(2)}) collective-permute-start(bf16[16,8,1472]{2,1,0:T(8,128)(2,1)} %bitcast.465), channel_id=1, source_target_pairs={{0,2},{1,3},{2,0},{3,1},{4,6},{5,7},{6,4},{7,5},{8,10},{9,11},{10,... | collective-permute-start | bytes 1130504 | tf_op jit(solution)/shard_map/ppermute | solution.py:38
  278.9 188.9 %reduce-scatter.6.cloned.1.call-start = ((), (), s32[]{:S(2)}) async-start(), calls=%async_computation.4 | async-start | bytes 5160960 | tf_op jit(solution)/shard_map/reduce_scatter | solution.py:749
  281.7 18.8 %collective-permute-start.38 = (bf16[16,8,1472]{2,1,0:T(8,128)(2,1)S(1)}, bf16[16,8,1472]{2,1,0:T(8,128)(2,1)S(1)}, u32[]{:S(2)}, u32[]{:S(2)}) collective-permute-start(bf16[16,8,1472]{2,1,0:T(8,128)(2,1)S(1)} %bitcast.462), channel_id=1, source_target_pairs={{0,1},{1,0},{2,3},{3,2},{4,5},{5,4},{6,7},{7,6},{8,9},{9,8},{10,11... | collective-permute-start | bytes 1130504 | tf_op jit(solution)/shard_map/ppermute | solution.py:38
  315.7 33.8 %collective-permute-start.48 = (bf16[96,8,1472]{2,1,0:T(8,128)(2,1)}, bf16[96,8,1472]{2,1,0:T(8,128)(2,1)S(1)}, u32[]{:S(2)}, u32[]{:S(2)}) collective-permute-start(bf16[96,8,1472]{2,1,0:T(8,128)(2,1)} %bitcast.453), channel_id=1, source_target_pairs={{0,16},{16,0},{1,17},{17,1},{2,18},{18,2},{3,19},{19,3},{4,20},{20... | collective-permute-start | bytes 6782984 | tf_op jit(solution)/shard_map/ppermute | solution.py:38
  317.1 19.7 %collective-permute-start.42 = (bf16[16,8,1472]{2,1,0:T(8,128)(2,1)}, bf16[16,8,1472]{2,1,0:T(8,128)(2,1)S(1)}, u32[]{:S(2)}, u32[]{:S(2)}) collective-permute-start(bf16[16,8,1472]{2,1,0:T(8,128)(2,1)} %bitcast.430), channel_id=1, source_target_pairs={{0,2},{1,3},{2,0},{3,1},{4,6},{5,7},{6,4},{7,5},{8,10},{9,11},{10,... | collective-permute-start | bytes 1130504 | tf_op jit(solution)/shard_map/ppermute | solution.py:38
  317.8 19.0 %collective-permute-start.43 = (bf16[16,8,1472]{2,1,0:T(8,128)(2,1)}, bf16[16,8,1472]{2,1,0:T(8,128)(2,1)S(1)}, u32[]{:S(2)}, u32[]{:S(2)}) collective-permute-start(bf16[16,8,1472]{2,1,0:T(8,128)(2,1)} %bitcast.431), channel_id=1, source_target_pairs={{0,3},{1,2},{2,1},{3,0},{4,7},{5,6},{6,5},{7,4},{8,11},{9,10},{10,... | collective-permute-start | bytes 1130504 | tf_op jit(solution)/shard_map/ppermute | solution.py:38
  319.2 33.2 %collective-permute-start.44 = (bf16[64,8,1472]{2,1,0:T(8,128)(2,1)S(1)}, bf16[64,8,1472]{2,1,0:T(8,128)(2,1)S(1)}, u32[]{:S(2)}, u32[]{:S(2)}) collective-permute-start(bf16[64,8,1472]{2,1,0:T(8,128)(2,1)S(1)} %bitcast.353), channel_id=1, source_target_pairs={{0,16},{16,0},{1,17},{17,1},{2,18},{18,2},{3,19},{19,3},{4,20},{20... | collective-permute-start | bytes 4521992 | tf_op jit(solution)/shard_map/ppermute | solution.py:38
  327.8 25.9 %collective-permute-start.47 = (bf16[56,8,512]{2,1,0:T(8,128)(2,1)}, bf16[56,8,512]{2,1,0:T(8,128)(2,1)}, u32[]{:S(2)}, u32[]{:S(2)}) collective-permute-start(bf16[56,8,512]{2,1,0:T(8,128)(2,1)} %bitcast.111), channel_id=1, source_target_pairs={{0,16},{16,0},{1,17},{17,1},{2,18},{18,2},{3,19},{19,3},{4,20},{20... | collective-permute-start | bytes 1376264 | tf_op jit(solution)/shard_map/ppermute | solution.py:38
  352.4 28.0 %collective-permute-start.50 = (bf16[4,48,1472]{2,1,0:T(8,128)(2,1)}, bf16[4,48,1472]{2,1,0:T(8,128)(2,1)}, u32[]{:S(2)}, u32[]{:S(2)}) collective-permute-start(bf16[4,48,1472]{2,1,0:T(8,128)(2,1)} %get-tuple-element.365), channel_id=1, source_target_pairs={{0,2},{1,3},{2,0},{3,1},{4,6},{5,7},{6,4},{7,5},{8,10},{9,11},{10,... | collective-permute-start | bytes 1695752 | tf_op jit(solution)/shard_map/ppermute | solution.py:38
  353.7 26.7 %collective-permute-start.51 = (bf16[4,48,1472]{2,1,0:T(8,128)(2,1)}, bf16[4,48,1472]{2,1,0:T(8,128)(2,1)}, u32[]{:S(2)}, u32[]{:S(2)}) collective-permute-start(bf16[4,48,1472]{2,1,0:T(8,128)(2,1)} %get-tuple-element.362), channel_id=1, source_target_pairs={{0,3},{1,2},{2,1},{3,0},{4,7},{5,6},{6,5},{7,4},{8,11},{9,10},{10,... | collective-permute-start | bytes 1695752 | tf_op jit(solution)/shard_map/ppermute | solution.py:38
  380.4 172.0 %reduce-scatter.8.cloned.1.call-start = ((), (), s32[]{:S(2)}) async-start(), calls=%async_computation.5 | async-start | bytes 2211840 | tf_op jit(solution)/shard_map/reduce_scatter | solution.py:808
  382.6 18.2 %collective-permute-start.53 = (bf16[16,8,1472]{2,1,0:T(8,128)(2,1)S(1)}, bf16[16,8,1472]{2,1,0:T(8,128)(2,1)S(1)}, u32[]{:S(2)}, u32[]{:S(2)}) collective-permute-start(bf16[16,8,1472]{2,1,0:T(8,128)(2,1)S(1)} %bitcast.459), channel_id=1, source_target_pairs={{0,2},{1,3},{2,0},{3,1},{4,6},{5,7},{6,4},{7,5},{8,10},{9,11},{10,... | collective-permute-start | bytes 1130504 | tf_op jit(solution)/shard_map/ppermute | solution.py:38
  423.4 27.1 %collective-permute-start.77 = (bf16[14,8,1472]{2,1,0:T(8,128)(2,1)S(1)}, bf16[14,8,1472]{2,1,0:T(8,128)(2,1)S(1)}, u32[]{:S(2)}, u32[]{:S(2)}) collective-permute-start(bf16[14,8,1472]{2,1,0:T(8,128)(2,1)S(1)} %slice_bitcast_fusion.1), channel_id=1, source_target_pairs={{0,0},{16,1},{1,2},{17,3},{2,4},{18,5},{3,6},{19,7},{8,8},{24,9},{... | collective-permute-start | bytes 989192 | tf_op jit(solution)/shard_map/ppermute | solution.py:38
  441.4 18.2 %collective-permute-start.62 = (bf16[14,8,1472]{2,1,0:T(8,128)(2,1)S(1)}, bf16[14,8,1472]{2,1,0:T(8,128)(2,1)S(1)}, u32[]{:S(2)}, u32[]{:S(2)}) collective-permute-start(bf16[14,8,1472]{2,1,0:T(8,128)(2,1)S(1)} %get-tuple-element.372), channel_id=1, source_target_pairs={{0,1},{1,0},{2,3},{3,2},{4,5},{5,4},{6,7},{7,6},{8,9},{9,8},{10,11... | collective-permute-start | bytes 989192 | tf_op jit(solution)/shard_map/ppermute | solution.py:38
  442.9 18.0 %collective-permute-start.63 = (bf16[14,8,1472]{2,1,0:T(8,128)(2,1)S(1)}, bf16[14,8,1472]{2,1,0:T(8,128)(2,1)S(1)}, u32[]{:S(2)}, u32[]{:S(2)}) collective-permute-start(bf16[14,8,1472]{2,1,0:T(8,128)(2,1)S(1)} %get-tuple-element.374), channel_id=1, source_target_pairs={{0,2},{1,3},{2,0},{3,1},{4,6},{5,7},{6,4},{7,5},{8,10},{9,11},{10,... | collective-permute-start | bytes 989192 | tf_op jit(solution)/shard_map/ppermute | solution.py:38
  451.9 77.8 %collective-permute-start.78 = (bf16[42,8,1472]{2,1,0:T(8,128)(2,1)}, bf16[42,8,1472]{2,1,0:T(8,128)(2,1)}, u32[]{:S(2)}, u32[]{:S(2)}) collective-permute-start(bf16[42,8,1472]{2,1,0:T(8,128)(2,1)} %get-tuple-element.378), channel_id=1, source_target_pairs={{0,16},{1,17},{2,18},{3,19},{4,20},{5,21},{6,22},{7,23},{8,24},{9,... | collective-permute-start | bytes 2967560 | tf_op jit(solution)/shard_map/ppermute | solution.py:38
  509.6 20.1 %collective-permute-start.76 = (bf16[42,8,1472]{2,1,0:T(8,128)(2,1)S(1)}, bf16[42,8,1472]{2,1,0:T(8,128)(2,1)S(1)}, u32[]{:S(2)}, u32[]{:S(2)}) collective-permute-start(bf16[42,8,1472]{2,1,0:T(8,128)(2,1)S(1)} %get-tuple-element.381), channel_id=1, source_target_pairs={{16,0},{17,1},{18,2},{19,3},{20,4},{21,5},{22,6},{23,7},{24,8},{25... | collective-permute-start | bytes 2967560 | tf_op jit(solution)/shard_map/ppermute | solution.py:38
  (128 other events, 1204.4 us)
Sparse Core Ops, SparseCore 0:
  18.6 46.0 all-gather.8
  66.8 91.4 all-gather.6
  159.9 78.2 all-gather.10
  279.0 80.2 reduce-scatter.3
  380.5 87.2 reduce-scatter.5
  507.9 37.7 reduce-scatter.7

commit v4 on v3

--- a/solution.py
+++ b/solution.py
@@ -559,7 +559,6 @@
         out_pieces = together(*spread(column[:, in_cols : in_cols + cross_cols]), column)
         column = out_pieces[-1]
         out_w = in_plane(out_pieces[:-1], 1).reshape(inner, width)
-        cross_pieces = spread(column[:, in_cols + cross_cols :])
         row_f32, row_bf16 = ((length, width), f32), ((length, width), bf16)
         context, first_kept, first_sent = call(
             self_forward_kernel,
@@ -580,8 +579,9 @@
             gains_e,
             gains_d,
         )
-        normed_first, *cross_pieces = together(normed_first, *cross_pieces)
         stream_e = spread(normed_first)
+        column, *stream_e = together(column, *stream_e)
+        cross_pieces = spread(column[:, in_cols + cross_cols :])
         group = PLANE * length
         group_bf16 = ((group, width), bf16)
         pack_shape = (lines, padded_widen + padded_narrow, width)
@@ -676,7 +676,6 @@
             (x_d, joined_grad_d, factors_d),
             (swap(x_d), swap(joined_grad_d), swap(factors_other_d)),
         )
-        feed_sum_d, *blocks = together(feed_sum_d, *blocks)
         back_d, part_d = collected(blocks[:PLANE]), blocks[PLANE:]
         gain_shape = ((1, width), f32)
         stream_two_d, cross_branch, cross_grads, stream_two_e, sent_e, gain_two_d, gain_two_e = call(
@@ -694,6 +693,7 @@
             cross_queries,
             states,
             cross_allowed,
+            ties=(feed_sum_d,),
         )
 
         stream_one_d, gain_one_d = call(
@@ -740,8 +740,6 @@
             (x_e, joined_grad_e, grads_own, hidden_own),
             (swap(x_e), swap(joined_grad_e), swap(grads_other), swap(hidden_other)),
         )
-        feed_sum_e, *blocks = together(feed_sum_e, *back_e, *cross_terms)
-        back_e, cross_terms = blocks[:PLANE], blocks[PLANE:]
         back_e = collected(back_e)
 
         summed_d = lax.psum_scatter(feed_sum_d, "line", scatter_dimension=0)
@@ -770,6 +768,7 @@
             projected,
             allowed,
         )
+        projected_grad, *cross_terms = together(projected_grad, *cross_terms)
         parts = projected_grad.reshape(lines, PLANE, in_cols, tokens)
         grad_parts = [at(parts, j, 1)] + [hop(at(parts, j ^ k, 1), k) for k in range(1, PLANE)]
         branch_grad, *grad_parts = together(
@@ -801,13 +800,16 @@
             specs={4 + k: whole((1, tokens)) for k in range(PLANE)},
         )
         plane_sum = rounded(total_of(scattered(small.reshape(PLANE, -1, width))))
-        plane_sum, summed_e = together(plane_sum, summed_e)
-        chip_sum = rounded(plane_sum.astype(f32) + swap(plane_sum).astype(f32))
+        plane_sum, summed_e, *part_d = together(plane_sum, summed_e, *part_d)
+        part_d = collected(part_d)
+        halves = plane_sum.reshape(2, padded // 8, width)
+        chip_sum = rounded(at(halves, section).astype(f32) + swap(at(halves, 1 - section)).astype(f32))
         rest_pack = jnp.concatenate([in_part.reshape(lines, in_cols, width), cross_part, out_part], 1)
-        rest_pack, line_sum = together(rest_pack, sum_line(chip_sum))
+        rest_pack, line_sum, summed_d, summed_e = together(
+            rest_pack, sum_line(chip_sum), summed_d, summed_e
+        )
         rest_sum = lax.psum_scatter(rest_pack, "line", scatter_dimension=0).astype(f32)
-        pieces = together(*spread(line_sum), *part_d)
-        pieces[PLANE:] = collected(pieces[PLANE:])
+        pieces = together(*spread(in_order(line_sum, swap(line_sum))), *part_d)
         second_out_d = second_d + sum(part.astype(f32) for part in pieces[PLANE:])
         embedding_grad, gains_grad = call(
             assemble_kernel,
@@ -818,14 +820,15 @@
             scratch=(pltpu.VMEM((padded, width), f32),),
         )
 
-        def returned(summed, receiver):
-            narrow = permute(summed[padded_widen:], AXES, [(b, a) for a, b in narrow_route])
-            half = jnp.concatenate([summed[:padded_widen], narrow], 0)
-            return half, permute(half, "section", [(1 - receiver, receiver)])
-
-        half_d, got_d = returned(summed_d, 1)
-        half_e, got_e = returned(summed_e, 0)
-        both = jnp.where(is_encoder, jnp.stack([half_e, got_e]), jnp.stack([got_d, half_d]))
+        narrow = permute(
+            jnp.concatenate([summed_e[padded_widen:], summed_d[padded_widen:]], 0),
+            AXES,
+            [(b, a) for a, b in narrow_route],
+        )
+        half_e = jnp.concatenate([summed_e[:padded_widen], narrow[:padded_narrow]], 0)
+        half_d = jnp.concatenate([summed_d[:padded_widen], narrow[padded_narrow:]], 0)
+        half_kept, half_sent = by_section(half_e, half_d)
+        both = in_order(half_kept[None], swap(half_sent)[None])
         both = both.reshape(2, 3, padded_narrow, width)[:, :, :narrow_half]
         widen_t = both[:, :2].reshape(2 * widen_half, width)
         narrow_grad = both[:, 2].reshape(2 * narrow_half, width).astype(f32)

time: 575 us -> 569 us (0.990)
  waiting for transfers between devices: 229 us -> 221 us
    ppermute x79 -> x78, waiting for transfers between devices: 211 us -> 194 us  [permute(): return lax.ppermute(block, axes, route).reshape(shape)]
    all_gather x1, waiting for transfers between devices: 0.01 us -> 11.9 us  [per_device(): own_e = lax.all_gather(pack_e, 'line', axis=0)]
    ppermute x79 -> x78, starting transfers between devices: 106 us -> 111 us  [permute(): return lax.ppermute(block, axes, route).reshape(shape)]
    unnamed x152 -> x160, local copies, waits for them, and re-layouts: 24.1 us -> 24.5 us
  transfers between devices with their start and end apart: 85 -> 84, of which waited for: 39 -> 40; matrix products, arithmetic and copies ran while one was open for 10% -> 10% of each run, Pallas kernels for 22% -> 22%
where the time goes in v4:
time: 569 us; the launch traced here: 562 us
  waiting for transfers between devices  221 us (39%)
  Pallas kernels  131 us (23%)
  starting transfers between devices  112 us (20%)
  local copies, waits for them, and re-layouts  44.2 us (8%)
  other arithmetic  31.9 us (6%)
  between operations  15.5 us (3%)
    ppermute x78, waiting for transfers between devices, permute(): return lax.ppermute(block, axes, route).reshape(shape)  194 us
    pallas_call x18, Pallas kernels, call(): pl.pallas_call(lambda *refs: kernel(*refs[:first], *refs[after:]), grid=(...  131 us
    ppermute x78, starting transfers between devices, permute(): return lax.ppermute(block, axes, route).reshape(shape)  111 us
    unnamed x160, local copies, waits for them, and re-layouts  24.5 us
    all_gather x1, waiting for transfers between devices, per_device(): own_d = lax.all_gather(pack_d, 'line', axis=0)  13.9 us
    all_gather x1, waiting for transfers between devices, per_device(): own_e = lax.all_gather(pack_e, 'line', axis=0)  11.9 us
  transfers between devices with their start and end apart: 84, of which 40 were waited for; matrix products, arithmetic and copies ran while one was open for 10% of the time, Pallas kernels for 22%

profile of v4, /device:TPU:0, one launch (start us, length us, event | category | flops | bytes accessed | tf_op | source)
XLA Modules:
  0.0 561.6 jit_solution(10917492919593784383)
XLA Ops:
  19.9 14.9 %collective-permute-done.7.refs_5_ = s32[1,256]{1,0:T(1,128)S(1)} collective-permute-done((s32[1,256]{1,0:T(1,128)S(1)}, s32[1,256]{1,0:T(1,128)S(1)}, u32[]{:S(2)}, u32[]{:S(2)}) %collective-permute-start.7) | collective-permute-done | bytes 1056 | tf_op jit(solution)/shard_map/ppermute | solution.py:38
  41.0 14.5 %collective-permute-done.9.refs_7_ = s32[1,256]{1,0:T(1,128)S(1)} collective-permute-done((s32[1,256]{1,0:T(1,128)S(1)}, s32[1,256]{1,0:T(1,128)S(1)}, u32[]{:S(2)}, u32[]{:S(2)}) %collective-permute-start.9) | collective-permute-done | bytes 1056 | tf_op jit(solution)/shard_map/ppermute | solution.py:38
  59.4 17.4 %collective-permute-start = (bf16[131,1472]{1,0:T(8,128)(2,1)}, bf16[131,1472]{1,0:T(8,128)(2,1)}, u32[]{:S(2)}, u32[]{:S(2)}) collective-permute-start(bf16[131,1472]{1,0:T(8,128)(2,1)} %pad_maximum_fusion.6), channel_id=1, source_target_pairs={{0,16},{16,0},{1,17},{17,1},{2,18},{18,2},{3,19},{19,3},{4,20},{20... | collective-permute-start | bytes 1157000 | tf_op jit(solution)/shard_map/ppermute | solution.py:38
  94.8 6.4 %collective-permute-done.13 = bf16[4,24,1472]{2,1,0:T(8,128)(2,1)S(1)} collective-permute-done((bf16[4,24,1472]{2,1,0:T(8,128)(2,1)S(1)}, bf16[4,24,1472]{2,1,0:T(8,128)(2,1)S(1)}, u32[]{:S(2)}, u32[]{:S(2)}) %collective-permute-start.13) | collective-permute-done | bytes 282656 | tf_op jit(solution)/shard_map/ppermute | solution.py:38
  108.3 5.9 %shard_map.187 = (bf16[384,256]{1,0:T(8,128)(2,1)}, f32[128,1472]{1,0:T(8,128)}, f32[128,1472]{1,0:T(8,128)}) custom-call(s32[1]{0:T(128)} %bitcast.37.refs_0_.refs_4_.refs_12_, bf16[1152,256]{1,0:T(8,128)(2,1)} %bitcast.370, f32[2,128,128]{2,1,0:T(8,128)} %and_convert_fusion.refs_2_.refs_5_, f32[256,1472]{1,0:T(8,128)} %copy-done.2, bf16[384,1472]{1,0:T(8,128)(2,1)} %bitcast.361), custom_call_target="tpu_custom_call" | custom-call | flops 240000000 | bytes 750000 | tf_op jit(solution)/shard_map/pallas_call | solution.py:79
  124.0 8.7 %collective-permute-done.17 = bf16[16,8,1472]{2,1,0:T(8,128)(2,1)S(1)} collective-permute-done((bf16[16,8,1472]{2,1,0:T(8,128)(2,1)}, bf16[16,8,1472]{2,1,0:T(8,128)(2,1)S(1)}, u32[]{:S(2)}, u32[]{:S(2)}) %collective-permute-start.17) | collective-permute-done | bytes 376864 | tf_op jit(solution)/shard_map/ppermute | solution.py:38
  132.6 7.9 %collective-permute-done.18 = bf16[16,8,1472]{2,1,0:T(8,128)(2,1)S(1)} collective-permute-done((bf16[16,8,1472]{2,1,0:T(8,128)(2,1)}, bf16[16,8,1472]{2,1,0:T(8,128)(2,1)S(1)}, u32[]{:S(2)}, u32[]{:S(2)}) %collective-permute-start.18) | collective-permute-done | bytes 376864 | tf_op jit(solution)/shard_map/ppermute | solution.py:38
  146.5 11.9 %all-gather.7.cloned.1.call-done = bf16[1344,1472]{1,0:T(8,128)(2,1)} async-done(((bf16[336,1472]{1,0:T(8,128)(2,1)}), bf16[1344,1472]{1,0:T(8,128)(2,1)}) %all-gather.7.cloned.1.call-update) | async-done | bytes 3956752 | tf_op jit(solution)/shard_map/all_gather | solution.py:550
  158.3 7.3 %shard_map.189 = (bf16[448,512]{1,0:T(8,128)(2,1)}, bf16[448,512]{1,0:T(8,128)(2,1)}, bf16[448,512]{1,0:T(8,128)(2,1)}, bf16[512,1472]{1,0:T(8,128)(2,1)}, bf16[512,1472]{1,0:T(8,128)(2,1)}) custom-call(bf16[128,1472]{1,0:T(8,128)(2,1)} %get-tuple-element.191.refs_0_, bf16[128,1472]{1,0:T(8,128)(2,1)} %bitcast.429, bf16[128,1472]{1,0:T(8,128)(2,1)} %bitcast.430, ...), custom_call_target="tpu_custom_call" | custom-call | flops 240000000 | bytes 750000 | tf_op jit(solution)/shard_map/pallas_call | solution.py:79
  176.7 7.1 %shard_map.190 = (bf16[448,512]{1,0:T(8,128)(2,1)}, bf16[448,512]{1,0:T(8,128)(2,1)}, bf16[448,512]{1,0:T(8,128)(2,1)}, bf16[128,1472]{1,0:T(8,128)(2,1)}, bf16[...) custom-call(bf16[512,1472]{1,0:T(8,128)(2,1)} %get-tuple-element.198.refs_0_, ...), custom_call_target="tpu_custom_call" | custom-call | flops 240000000 | bytes 750000 | tf_op jit(solution)/shard_map/pallas_call | solution.py:79
  183.8 7.0 %collective-permute-done.25 = bf16[16,8,1472]{2,1,0:T(8,128)(2,1)S(1)} collective-permute-done((bf16[16,8,1472]{2,1,0:T(8,128)(2,1)S(1)}, bf16[16,8,1472]{2,1,0:T(8,128)(2,1)S(1)}, u32[]{:S(2)}, u32[]{:S(2)}) %collective-permute-start.25) | collective-permute-done | bytes 376864 | tf_op jit(solution)/shard_map/ppermute | solution.py:38
  203.1 8.1 %collective-permute-done.28 = bf16[16,8,1472]{2,1,0:T(8,128)(2,1)S(1)} collective-permute-done((bf16[16,8,1472]{2,1,0:T(8,128)(2,1)}, bf16[16,8,1472]{2,1,0:T(8,128)(2,1)S(1)}, u32[]{:S(2)}, u32[]{:S(2)}) %collective-permute-start.28) | collective-permute-done | bytes 376864 | tf_op jit(solution)/shard_map/ppermute | solution.py:38
  212.1 8.7 %shard_map.191 = (f32[128,1472]{1,0:T(8,128)}, bf16[128,1472]{1,0:T(8,128)(2,1)}, bf16[384,128]{1,0:T(8,128)(2,1)}, bf16[768,128]{1,0:T(8,128)(2,1)}, bf16[384,1...) custom-call(bf16[128,1472]{1,0:T(8,128)(2,1)} %get-tuple-element.205.refs_0_, ...), custom_call_target="tpu_custom_call" | custom-call | flops 240000000 | bytes 750000 | tf_op jit(solution)/shard_map/pallas_call | solution.py:79
  224.3 13.9 %all-gather.11.cloned.1.call-done = bf16[1344,1472]{1,0:T(8,128)(2,1)} async-done(((bf16[336,1472]{1,0:T(8,128)(2,1)}), bf16[1344,1472]{1,0:T(8,128)(2,1)}) %all-gather.11.cloned.1.call-update) | async-done | bytes 3956752 | tf_op jit(solution)/shard_map/all_gather | solution.py:551
  240.0 9.9 %shard_map.192 = (bf16[1344,512]{1,0:T(8,128)(2,1)}, bf16[512,1472]{1,0:T(8,128)(2,1)}, bf16[512,1472]{1,0:T(8,128)(2,1)}, bf16[512,1472]{1,0:T(8,128)(2,1)}, bf16[512,1472]{1,0:T(8,128)(2,1)}) custom-call(bf16[128,1472]{1,0:T(8,128)(2,1)} %get-tuple-element.220.refs_0_, bf16[128,1472]{1,0:T(8,128)(2,1)} %bitcast.440, bf16[128,1472]{1,0:T(8,128)(2,1)} %bitcast.444, ...), custom_call_target="tpu_custom_call" | custom-call | flops 240000000 | bytes 750000 | tf_op jit(solution)/shard_map/pallas_call | solution.py:79
  252.4 10.8 %shard_map.193 = (bf16[1344,512]{1,0:T(8,128)(2,1)}, bf16[128,1472]{1,0:T(8,128)(2,1)}, bf16[128,1472]{1,0:T(8,128)(2,1)}, bf16[128,1472]{1,0:T(8,128)(2,1)}, bf...) custom-call(bf16[512,1472]{1,0:T(8,128)(2,1)} %get-tuple-element.228, ...), custom_call_target="tpu_custom_call" | custom-call | flops 240000000 | bytes 750000 | tf_op jit(solution)/shard_map/pallas_call | solution.py:79
  267.7 10.1 %shard_map.194.refs_15_ = bf16[4,336,1472]{2,1,0:T(8,128)(2,1)} custom-call(bf16[512,1472]{1,0:T(8,128)(2,1)} %get-tuple-element.228.refs_0_, bf16[512,1472]{1,0:T(8,128)(2,1)} %get-tuple-element.229.refs_1_, bf16[1344,512]{1,0:T(8,128)(2,1)} %get-tuple-element.238.refs_2_, bf16[512,1472]{1,0:T(8,128)(2,1)} %bitcast.393, bf16[512,1472]{1,0:T(8,128)(2,1)} %bitcast.394, ...), custom_call_target="tpu_custom_call" | custom-call | flops 240000000 | bytes 750000 | tf_op jit(solution)/shard_map/pallas_call | solution.py:79
  282.3 8.5 %collective-permute-done.35 = bf16[16,8,1472]{2,1,0:T(8,128)(2,1)S(1)} collective-permute-done((bf16[16,8,1472]{2,1,0:T(8,128)(2,1)S(1)}, bf16[16,8,1472]{2,1,0:T(8,128)(2,1)S(1)}, u32[]{:S(2)}, u32[]{:S(2)}) %collective-permute-start.35) | collective-permute-done | bytes 376864 | tf_op jit(solution)/shard_map/ppermute | solution.py:38
  290.8 7.1 %collective-permute-done.36 = bf16[16,8,1472]{2,1,0:T(8,128)(2,1)S(1)} collective-permute-done((bf16[16,8,1472]{2,1,0:T(8,128)(2,1)S(1)}, bf16[16,8,1472]{2,1,0:T(8,128)(2,1)S(1)}, u32[]{:S(2)}, u32[]{:S(2)}) %collective-permute-start.36) | collective-permute-done | bytes 376864 | tf_op jit(solution)/shard_map/ppermute | solution.py:38
  300.3 9.3 %shard_map.195 = (f32[128,1472]{1,0:T(8,128)}, bf16[128,1472]{1,0:T(8,128)(2,1)}, bf16[1152,128]{1,0:T(8,128)(2,1)}, f32[128,1472]{1,0:T(8,128)}, bf16[128,1472]...) custom-call(bf16[128,1472]{1,0:T(8,128)(2,1)} %get-tuple-element.232.refs_0_, bf16[128,1472]{1,0:T(8,128)(2,1)} %bitcast.439, ...), custom_call_target="tpu_custom_call" | custom-call | flops 240000000 | bytes 750000 | tf_op jit(solution)/shard_map/pallas_call | solution.py:79
  321.9 7.0 %collective-permute-done.42 = bf16[16,8,1472]{2,1,0:T(8,128)(2,1)S(1)} collective-permute-done((bf16[16,8,1472]{2,1,0:T(8,128)(2,1)}, bf16[16,8,1472]{2,1,0:T(8,128)(2,1)S(1)}, u32[]{:S(2)}, u32[]{:S(2)}) %collective-permute-start.42) | collective-permute-done | bytes 376864 | tf_op jit(solution)/shard_map/ppermute | solution.py:38
  329.9 11.1 %shard_map.198 = (bf16[896,512]{1,0:T(8,128)(2,1)}, bf16[896,512]{1,0:T(8,128)(2,1)}, bf16[512,1472]{1,0:T(8,128)(2,1)}, bf16[128,1472]{1,0:T(8,128)(2,1)}, bf16...) custom-call(bf16[128,1472]{1,0:T(8,128)(2,1)} %get-tuple-element.241.refs_0_, ...), custom_call_target="tpu_custom_call" | custom-call | flops 240000000 | bytes 750000 | tf_op jit(solution)/shard_map/pallas_call | solution.py:79
  348.1 10.1 %shard_map.199.refs_9_ = bf16[4,336,1472]{2,1,0:T(8,128)(2,1)} custom-call(bf16[512,1472]{1,0:T(8,128)(2,1)} %get-tuple-element.198.refs_0_, bf16[512,1472]{1,0:T(8,128)(2,1)} %get-tuple-element.261.refs_1_, bf16[896,512]{1,0:T(8,128)(2,1)} %get-tuple-element.262.refs_2_, bf16[448,512]{1,0:T(8,128)(2,1)} %get-tuple-element.263.refs_3_, ...), custom_call_target="tpu_custom_call" | custom-call | flops 240000000 | bytes 750000 | tf_op jit(solution)/shard_map/pallas_call | solution.py:79
  364.1 6.8 %collective-permute-done.44 = bf16[16,8,1472]{2,1,0:T(8,128)(2,1)S(1)} collective-permute-done((bf16[16,8,1472]{2,1,0:T(8,128)(2,1)}, bf16[16,8,1472]{2,1,0:T(8,128)(2,1)S(1)}, u32[]{:S(2)}, u32[]{:S(2)}) %collective-permute-start.44) | collective-permute-done | bytes 376864 | tf_op jit(solution)/shard_map/ppermute | solution.py:38
  370.9 8.9 %collective-permute-done.45 = bf16[16,8,1472]{2,1,0:T(8,128)(2,1)S(1)} collective-permute-done((bf16[16,8,1472]{2,1,0:T(8,128)(2,1)S(1)}, bf16[16,8,1472]{2,1,0:T(8,128)(2,1)S(1)}, u32[]{:S(2)}, u32[]{:S(2)}) %collective-permute-start.45) | collective-permute-done | bytes 376864 | tf_op jit(solution)/shard_map/ppermute | solution.py:38
  390.1 8.7 %shard_map.201 = (f32[256,1472]{1,0:T(8,128)}, bf16[256,1472]{1,0:T(8,128)(2,1)}, bf16[1152,256]{1,0:T(8,128)(2,1)}) custom-call(s32[1]{0:T(128)} %bitcast.37.refs_0_.refs_4_.refs_12_, f32[128,1472]{1,0:T(8,128)} %get-tuple-element.267.refs_1_, f32[128,1472]{1,0:T(8,128)} %bitcast.409, bf16[384,1472]{1,0:T(8,128)(2,1)} %bitcast.362, ...), custom_call_target="tpu_custom_call" | custom-call | flops 240000000 | bytes 750000 | tf_op jit(solution)/shard_map/pallas_call | solution.py:79
  402.1 12.3 %collective-permute-done.55 = bf16[4,48,1472]{2,1,0:T(8,128)(2,1)S(1)} collective-permute-done((bf16[4,48,1472]{2,1,0:T(8,128)(2,1)S(1)}, bf16[4,48,1472]{2,1,0:T(8,128)(2,1)S(1)}, u32[]{:S(2)}, u32[]{:S(2)}) %collective-permute-start.55) | collective-permute-done | bytes 565280 | tf_op jit(solution)/shard_map/ppermute | solution.py:38
  427.0 9.7 %shard_map.203 = bf16[448,1472]{1,0:T(8,128)(2,1)} custom-call(bf16[288,256]{1,0:T(8,128)(2,1)} %bitcast.400, bf16[288,256]{1,0:T(8,128)(2,1)} %bitcast.414, bf16[288,256]{1,0:T(8,128)(2,1)} %bitcast.416, bf16[288,256]{1,0:T(8,128)(2,1)} %bitcast.418, s32[1,256]{1,0:T(1,128)} %bitcast.462, s32[1,256]{1,0:T(1,128)} %copy-done.69, s32[1,256]{1,0:T(1,128)} %copy-done.70, ...), custom_call_target="tpu_custom_call" | custom-call | flops 240000000 | bytes 750000 | tf_op jit(solution)/shard_map/pallas_call | solution.py:79
  444.7 6.4 %collective-permute-done.64 = bf16[14,8,1472]{2,1,0:T(8,128)(2,1)S(1)} collective-permute-done((bf16[14,8,1472]{2,1,0:T(8,128)(2,1)}, bf16[14,8,1472]{2,1,0:T(8,128)(2,1)S(1)}, u32[]{:S(2)}, u32[]{:S(2)}) %collective-permute-start.64) | collective-permute-done | bytes 329760 | tf_op jit(solution)/shard_map/ppermute | solution.py:38
  490.9 6.7 %collective-permute-start.76 = (bf16[28,8,1472]{2,1,0:T(8,128)(2,1)}, bf16[28,8,1472]{2,1,0:T(8,128)(2,1)}, u32[]{:S(2)}, u32[]{:S(2)}) collective-permute-start(bf16[28,8,1472]{2,1,0:T(8,128)(2,1)} %maximum_bitcast_fusion.1), channel_id=1, source_target_pairs={{0,0},{16,1},{1,2},{17,3},{2,4},{18,5},{3,6},{19,7},{8,8},{24,9},{... | collective-permute-start | bytes 1978376 | tf_op jit(solution)/shard_map/ppermute | solution.py:38
  502.3 8.2 %collective-permute-start.71 = (bf16[14,8,1472]{2,1,0:T(8,128)(2,1)}, bf16[14,8,1472]{2,1,0:T(8,128)(2,1)}, u32[]{:S(2)}, u32[]{:S(2)}) collective-permute-start(bf16[14,8,1472]{2,1,0:T(8,128)(2,1)} %get-tuple-element.390), channel_id=1, source_target_pairs={{0,3},{1,2},{2,1},{3,0},{4,7},{5,6},{6,5},{7,4},{8,11},{9,10},{10,... | collective-permute-start | bytes 989192 | tf_op jit(solution)/shard_map/ppermute | solution.py:38
  511.7 15.4 %collective-permute-done.69 = bf16[14,8,1472]{2,1,0:T(8,128)(2,1)S(1)} collective-permute-done((bf16[14,8,1472]{2,1,0:T(8,128)(2,1)}, bf16[14,8,1472]{2,1,0:T(8,128)(2,1)S(1)}, u32[]{:S(2)}, u32[]{:S(2)}) %collective-permute-start.69) | collective-permute-done | bytes 329760 | tf_op jit(solution)/shard_map/ppermute | solution.py:38
  (408 shorter events, 239.5 us)
Async XLA Ops:
  7.2 70.3 %all-gather.9.cloned.1.call-start = ((), (), s32[]{:S(2)}) async-start(), calls=%async_computation.7 | async-start | bytes 2211840 | tf_op jit(solution)/shard_map/all_gather | solution.py:503
  13.9 41.6 %collective-permute-start.4 = (bf16[32,8,1472]{2,1,0:T(8,128)(2,1)}, bf16[32,8,1472]{2,1,0:T(8,128)(2,1)S(1)}, u32[]{:S(2)}, u32[]{:S(2)}) collective-permute-start(bf16[32,8,1472]{2,1,0:T(8,128)(2,1)} %fusion.49), channel_id=1, source_target_pairs={{0,1},{1,0},{2,3},{3,2},{4,5},{5,4},{6,7},{7,6},{8,9},{9,8},{10,11... | collective-permute-start | bytes 2261000 | tf_op jit(solution)/shard_map/ppermute | solution.py:38
  16.4 39.2 %collective-permute-start.5 = (bf16[32,8,1472]{2,1,0:T(8,128)(2,1)}, bf16[32,8,1472]{2,1,0:T(8,128)(2,1)}, u32[]{:S(2)}, u32[]{:S(2)}) collective-permute-start(bf16[32,8,1472]{2,1,0:T(8,128)(2,1)} %fusion.49), channel_id=1, source_target_pairs={{0,2},{1,3},{2,0},{3,1},{4,6},{5,7},{6,4},{7,5},{8,10},{9,11},{10,... | collective-permute-start | bytes 2261000 | tf_op jit(solution)/shard_map/ppermute | solution.py:38
  18.4 19.1 %collective-permute-start.8 = (s32[1,256]{1,0:T(1,128)S(1)}, s32[1,256]{1,0:T(1,128)S(1)}, u32[]{:S(2)}, u32[]{:S(2)}) collective-permute-start(s32[1,256]{1,0:T(1,128)S(1)} %bitcast.465), channel_id=1, source_target_pairs={{0,2},{1,3},{2,0},{3,1},{4,6},{5,7},{6,4},{7,5},{8,10},{9,11},{10,... | collective-permute-start | bytes 3080 | tf_op jit(solution)/shard_map/ppermute | solution.py:38
  18.5 139.9 %all-gather.7.cloned.1.call-start = ((), (), s32[]{:S(2)}) async-start(), calls=%async_computation.6 | async-start | bytes 5160960 | tf_op jit(solution)/shard_map/all_gather | solution.py:550
  19.7 18.8 %collective-permute-start.1 = (bf16[28,8,1472]{2,1,0:T(8,128)(2,1)S(1)}, bf16[28,8,1472]{2,1,0:T(8,128)(2,1)S(1)}, u32[]{:S(2)}, u32[]{:S(2)}) collective-permute-start(bf16[28,8,1472]{2,1,0:T(8,128)(2,1)S(1)} %dynamic-slice_bitcast_fusion), channel_id=1, source_target_pairs={{0,16},{16,0},{1,17},{17,1},{2,18},{18,2},{3,19},{19,3},{4,20},{20... | collective-permute-start | bytes 1978376 | tf_op jit(solution)/shard_map/ppermute | solution.py:38
  34.9 20.7 %collective-permute-start.6 = (bf16[32,8,1472]{2,1,0:T(8,128)(2,1)}, bf16[32,8,1472]{2,1,0:T(8,128)(2,1)}, u32[]{:S(2)}, u32[]{:S(2)}) collective-permute-start(bf16[32,8,1472]{2,1,0:T(8,128)(2,1)} %fusion.49), channel_id=1, source_target_pairs={{0,3},{1,2},{2,1},{3,0},{4,7},{5,6},{6,5},{7,4},{8,11},{9,10},{10,... | collective-permute-start | bytes 2261000 | tf_op jit(solution)/shard_map/ppermute | solution.py:38
  57.2 181.0 %all-gather.11.cloned.1.call-start = ((), (), s32[]{:S(2)}) async-start(), calls=%async_computation.8 | async-start | bytes 5160960 | tf_op jit(solution)/shard_map/all_gather | solution.py:551
  59.4 54.9 %collective-permute-start = (bf16[131,1472]{1,0:T(8,128)(2,1)}, bf16[131,1472]{1,0:T(8,128)(2,1)}, u32[]{:S(2)}, u32[]{:S(2)}) collective-permute-start(bf16[131,1472]{1,0:T(8,128)(2,1)} %pad_maximum_fusion.6), channel_id=1, source_target_pairs={{0,16},{16,0},{1,17},{17,1},{2,18},{18,2},{3,19},{19,3},{4,20},{20... | collective-permute-start | bytes 1157000 | tf_op jit(solution)/shard_map/ppermute | solution.py:38
  121.1 19.5 %collective-permute-start.18 = (bf16[16,8,1472]{2,1,0:T(8,128)(2,1)}, bf16[16,8,1472]{2,1,0:T(8,128)(2,1)S(1)}, u32[]{:S(2)}, u32[]{:S(2)}) collective-permute-start(bf16[16,8,1472]{2,1,0:T(8,128)(2,1)} %bitcast.427), channel_id=1, source_target_pairs={{0,2},{1,3},{2,0},{3,1},{4,6},{5,7},{6,4},{7,5},{8,10},{9,11},{10,... | collective-permute-start | bytes 1130504 | tf_op jit(solution)/shard_map/ppermute | solution.py:38
  122.2 18.4 %collective-permute-start.19 = (bf16[16,8,1472]{2,1,0:T(8,128)(2,1)}, bf16[16,8,1472]{2,1,0:T(8,128)(2,1)S(1)}, u32[]{:S(2)}, u32[]{:S(2)}) collective-permute-start(bf16[16,8,1472]{2,1,0:T(8,128)(2,1)} %bitcast.428), channel_id=1, source_target_pairs={{0,3},{1,2},{2,1},{3,0},{4,7},{5,6},{6,5},{7,4},{8,11},{9,10},{10,... | collective-permute-start | bytes 1130504 | tf_op jit(solution)/shard_map/ppermute | solution.py:38
  140.6 25.0 %collective-permute-start.20 = (bf16[4,48,1472]{2,1,0:T(8,128)(2,1)S(1)}, bf16[4,48,1472]{2,1,0:T(8,128)(2,1)S(1)}, u32[]{:S(2)}, u32[]{:S(2)}) collective-permute-start(bf16[4,48,1472]{2,1,0:T(8,128)(2,1)S(1)} %slice.90), channel_id=1, source_target_pairs={{0,1},{1,0},{2,3},{3,2},{4,5},{5,4},{6,7},{7,6},{8,9},{9,8},{10,11... | collective-permute-start | bytes 1695752 | tf_op jit(solution)/shard_map/ppermute | solution.py:38
  142.1 24.8 %collective-permute-start.21 = (bf16[4,48,1472]{2,1,0:T(8,128)(2,1)S(1)}, bf16[4,48,1472]{2,1,0:T(8,128)(2,1)S(1)}, u32[]{:S(2)}, u32[]{:S(2)}) collective-permute-start(bf16[4,48,1472]{2,1,0:T(8,128)(2,1)S(1)} %slice.90), channel_id=1, source_target_pairs={{0,2},{1,3},{2,0},{3,1},{4,6},{5,7},{6,4},{7,5},{8,10},{9,11},{10,... | collective-permute-start | bytes 1695752 | tf_op jit(solution)/shard_map/ppermute | solution.py:38
  142.5 26.2 %collective-permute-start.22 = (bf16[4,48,1472]{2,1,0:T(8,128)(2,1)S(1)}, bf16[4,48,1472]{2,1,0:T(8,128)(2,1)}, u32[]{:S(2)}, u32[]{:S(2)}) collective-permute-start(bf16[4,48,1472]{2,1,0:T(8,128)(2,1)S(1)} %slice.90), channel_id=1, source_target_pairs={{0,3},{1,2},{2,1},{3,0},{4,7},{5,6},{6,5},{7,4},{8,11},{9,10},{10,... | collective-permute-start | bytes 1695752 | tf_op jit(solution)/shard_map/ppermute | solution.py:38
  144.2 214.0 %reduce-scatter.4.cloned.1.call-start = ((), (), s32[]{:S(2)}) async-start(), calls=%async_computation.3 | async-start | bytes 5160960 | tf_op jit(solution)/shard_map/reduce_scatter | solution.py:745
  170.3 24.0 %collective-permute-start.30 = (bf16[96,8,1472]{2,1,0:T(8,128)(2,1)S(1)}, bf16[96,8,1472]{2,1,0:T(8,128)(2,1)}, u32[]{:S(2)}, u32[]{:S(2)}) collective-permute-start(bf16[96,8,1472]{2,1,0:T(8,128)(2,1)S(1)} %bitcast.364), channel_id=1, source_target_pairs={{0,16},{16,0},{1,17},{17,1},{2,18},{18,2},{3,19},{19,3},{4,20},{20... | collective-permute-start | bytes 6782984 | tf_op jit(solution)/shard_map/ppermute | solution.py:38
  171.2 19.6 %collective-permute-start.25 = (bf16[16,8,1472]{2,1,0:T(8,128)(2,1)S(1)}, bf16[16,8,1472]{2,1,0:T(8,128)(2,1)S(1)}, u32[]{:S(2)}, u32[]{:S(2)}) collective-permute-start(bf16[16,8,1472]{2,1,0:T(8,128)(2,1)S(1)} %bitcast.378), channel_id=1, source_target_pairs={{0,2},{1,3},{2,0},{3,1},{4,6},{5,7},{6,4},{7,5},{8,10},{9,11},{10,... | collective-permute-start | bytes 1130504 | tf_op jit(solution)/shard_map/ppermute | solution.py:38
  192.1 19.1 %collective-permute-start.28 = (bf16[16,8,1472]{2,1,0:T(8,128)(2,1)}, bf16[16,8,1472]{2,1,0:T(8,128)(2,1)S(1)}, u32[]{:S(2)}, u32[]{:S(2)}) collective-permute-start(bf16[16,8,1472]{2,1,0:T(8,128)(2,1)} %bitcast.483), channel_id=1, source_target_pairs={{0,2},{1,3},{2,0},{3,1},{4,6},{5,7},{6,4},{7,5},{8,10},{9,11},{10,... | collective-permute-start | bytes 1130504 | tf_op jit(solution)/shard_map/ppermute | solution.py:38
  277.9 179.5 %reduce-scatter.6.cloned.1.call-start = ((), (), s32[]{:S(2)}) async-start(), calls=%async_computation.4 | async-start | bytes 5160960 | tf_op jit(solution)/shard_map/reduce_scatter | solution.py:747
  281.0 18.5 %collective-permute-start.37 = (bf16[16,8,1472]{2,1,0:T(8,128)(2,1)S(1)}, bf16[16,8,1472]{2,1,0:T(8,128)(2,1)S(1)}, u32[]{:S(2)}, u32[]{:S(2)}) collective-permute-start(bf16[16,8,1472]{2,1,0:T(8,128)(2,1)S(1)} %bitcast.479), channel_id=1, source_target_pairs={{0,3},{1,2},{2,1},{3,0},{4,7},{5,6},{6,5},{7,4},{8,11},{9,10},{10,... | collective-permute-start | bytes 1130504 | tf_op jit(solution)/shard_map/ppermute | solution.py:38
  310.5 18.5 %collective-permute-start.42 = (bf16[16,8,1472]{2,1,0:T(8,128)(2,1)}, bf16[16,8,1472]{2,1,0:T(8,128)(2,1)S(1)}, u32[]{:S(2)}, u32[]{:S(2)}) collective-permute-start(bf16[16,8,1472]{2,1,0:T(8,128)(2,1)} %bitcast.448), channel_id=1, source_target_pairs={{0,2},{1,3},{2,0},{3,1},{4,6},{5,7},{6,4},{7,5},{8,10},{9,11},{10,... | collective-permute-start | bytes 1130504 | tf_op jit(solution)/shard_map/ppermute | solution.py:38
  313.2 28.5 %collective-permute-start.47 = (bf16[64,8,1472]{2,1,0:T(8,128)(2,1)S(1)}, bf16[64,8,1472]{2,1,0:T(8,128)(2,1)S(1)}, u32[]{:S(2)}, u32[]{:S(2)}) collective-permute-start(bf16[64,8,1472]{2,1,0:T(8,128)(2,1)S(1)} %bitcast.367), channel_id=1, source_target_pairs={{0,16},{16,0},{1,17},{17,1},{2,18},{18,2},{3,19},{19,3},{4,20},{20... | collective-permute-start | bytes 4521992 | tf_op jit(solution)/shard_map/ppermute | solution.py:38
  358.3 191.8 %reduce-scatter.8.cloned.1.call-start = ((), (), s32[]{:S(2)}) async-start(), calls=%async_computation.5 | async-start | bytes 2211840 | tf_op jit(solution)/shard_map/reduce_scatter | solution.py:811
  360.3 19.5 %collective-permute-start.45 = (bf16[16,8,1472]{2,1,0:T(8,128)(2,1)S(1)}, bf16[16,8,1472]{2,1,0:T(8,128)(2,1)S(1)}, u32[]{:S(2)}, u32[]{:S(2)}) collective-permute-start(bf16[16,8,1472]{2,1,0:T(8,128)(2,1)S(1)} %bitcast.477), channel_id=1, source_target_pairs={{0,2},{1,3},{2,0},{3,1},{4,6},{5,7},{6,4},{7,5},{8,10},{9,11},{10,... | collective-permute-start | bytes 1130504 | tf_op jit(solution)/shard_map/ppermute | solution.py:38
  360.8 19.0 %collective-permute-start.46 = (bf16[16,8,1472]{2,1,0:T(8,128)(2,1)S(1)}, bf16[16,8,1472]{2,1,0:T(8,128)(2,1)S(1)}, u32[]{:S(2)}, u32[]{:S(2)}) collective-permute-start(bf16[16,8,1472]{2,1,0:T(8,128)(2,1)S(1)} %bitcast.476), channel_id=1, source_target_pairs={{0,3},{1,2},{2,1},{3,0},{4,7},{5,6},{6,5},{7,4},{8,11},{9,10},{10,... | collective-permute-start | bytes 1130504 | tf_op jit(solution)/shard_map/ppermute | solution.py:38
  387.5 26.9 %collective-permute-start.55 = (bf16[4,48,1472]{2,1,0:T(8,128)(2,1)S(1)}, bf16[4,48,1472]{2,1,0:T(8,128)(2,1)S(1)}, u32[]{:S(2)}, u32[]{:S(2)}) collective-permute-start(bf16[4,48,1472]{2,1,0:T(8,128)(2,1)S(1)} %get-tuple-element.348), channel_id=1, source_target_pairs={{0,3},{1,2},{2,1},{3,0},{4,7},{5,6},{6,5},{7,4},{8,11},{9,10},{10,... | collective-permute-start | bytes 1695752 | tf_op jit(solution)/shard_map/ppermute | solution.py:38
  483.1 19.2 %collective-permute-start.73 = (bf16[16,8,1472]{2,1,0:T(8,128)(2,1)}, bf16[16,8,1472]{2,1,0:T(8,128)(2,1)}, u32[]{:S(2)}, u32[]{:S(2)}) collective-permute-start(bf16[16,8,1472]{2,1,0:T(8,128)(2,1)} %bitcast.474), channel_id=1, source_target_pairs={{0,2},{1,3},{2,0},{3,1},{4,6},{5,7},{6,4},{7,5},{8,10},{9,11},{10,... | collective-permute-start | bytes 1130504 | tf_op jit(solution)/shard_map/ppermute | solution.py:38
  483.8 27.8 %collective-permute-start.74 = (bf16[16,8,1472]{2,1,0:T(8,128)(2,1)}, bf16[16,8,1472]{2,1,0:T(8,128)(2,1)}, u32[]{:S(2)}, u32[]{:S(2)}) collective-permute-start(bf16[16,8,1472]{2,1,0:T(8,128)(2,1)} %bitcast.473), channel_id=1, source_target_pairs={{0,3},{1,2},{2,1},{3,0},{4,7},{5,6},{6,5},{7,4},{8,11},{9,10},{10,... | collective-permute-start | bytes 1130504 | tf_op jit(solution)/shard_map/ppermute | solution.py:38
  490.9 48.4 %collective-permute-start.76 = (bf16[28,8,1472]{2,1,0:T(8,128)(2,1)}, bf16[28,8,1472]{2,1,0:T(8,128)(2,1)}, u32[]{:S(2)}, u32[]{:S(2)}) collective-permute-start(bf16[28,8,1472]{2,1,0:T(8,128)(2,1)} %maximum_bitcast_fusion.1), channel_id=1, source_target_pairs={{0,0},{16,1},{1,2},{17,3},{2,4},{18,5},{3,6},{19,7},{8,8},{24,9},{... | collective-permute-start | bytes 1978376 | tf_op jit(solution)/shard_map/ppermute | solution.py:38
  498.6 28.4 %collective-permute-start.69 = (bf16[14,8,1472]{2,1,0:T(8,128)(2,1)}, bf16[14,8,1472]{2,1,0:T(8,128)(2,1)S(1)}, u32[]{:S(2)}, u32[]{:S(2)}) collective-permute-start(bf16[14,8,1472]{2,1,0:T(8,128)(2,1)} %get-tuple-element.390), channel_id=1, source_target_pairs={{0,1},{1,0},{2,3},{3,2},{4,5},{5,4},{6,7},{7,6},{8,9},{9,8},{10,11... | collective-permute-start | bytes 989192 | tf_op jit(solution)/shard_map/ppermute | solution.py:38
  498.6 28.4 %collective-permute-start.70 = (bf16[14,8,1472]{2,1,0:T(8,128)(2,1)}, bf16[14,8,1472]{2,1,0:T(8,128)(2,1)}, u32[]{:S(2)}, u32[]{:S(2)}) collective-permute-start(bf16[14,8,1472]{2,1,0:T(8,128)(2,1)} %get-tuple-element.390), channel_id=1, source_target_pairs={{0,2},{1,3},{2,0},{3,1},{4,6},{5,7},{6,4},{7,5},{8,10},{9,11},{10,... | collective-permute-start | bytes 989192 | tf_op jit(solution)/shard_map/ppermute | solution.py:38
  502.3 24.7 %collective-permute-start.71 = (bf16[14,8,1472]{2,1,0:T(8,128)(2,1)}, bf16[14,8,1472]{2,1,0:T(8,128)(2,1)}, u32[]{:S(2)}, u32[]{:S(2)}) collective-permute-start(bf16[14,8,1472]{2,1,0:T(8,128)(2,1)} %get-tuple-element.390), channel_id=1, source_target_pairs={{0,3},{1,2},{2,1},{3,0},{4,7},{5,6},{6,5},{7,4},{8,11},{9,10},{10,... | collective-permute-start | bytes 989192 | tf_op jit(solution)/shard_map/ppermute | solution.py:38
  (130 other events, 1172.5 us)
Sparse Core Ops, SparseCore 0:
  18.6 46.0 all-gather.8
  66.8 91.4 all-gather.6
  159.9 78.2 all-gather.10
  278.0 79.4 reduce-scatter.3
  359.7 77.7 reduce-scatter.5
  511.8 38.2 reduce-scatter.7

commit v5 on v4

--- a/solution.py
+++ b/solution.py
@@ -66,7 +66,7 @@
     return pl.BlockSpec(shape, lambda step: (0,) * len(shape))
 
 
-def call(kernel, outputs, *args, scratch=(), specs=None, time_us=0.3, ties=(), vmem=56):
+def call(kernel, outputs, *args, scratch=(), specs=None, time_us=1, ties=(), vmem=56):
     specs = specs or {}
     in_specs = [
         specs.get(i)
@@ -521,7 +521,6 @@
 
         columns = lax.broadcasted_iota(jnp.int32, (tokens, vocabulary), 1)
         inputs = nn((codes.reshape(tokens, 1) == columns).astype(bf16), embedding)
-        codes_plane = spread(codes.reshape(1, tokens))
         own_segments = jnp.where(is_encoder, encoder_segments, target_segments)
         earlier = lax.broadcasted_iota(jnp.int32, (length, length), 1) <= lax.broadcasted_iota(
             jnp.int32, (length, length), 0
@@ -539,8 +538,7 @@
         gain_self = own_gains[:1].astype(f32)
 
         normed_plane = spread(rms_norm(inputs, gain_self).astype(bf16))
-        moved, *planes = together(moved, *normed_plane, *codes_plane)
-        normed_plane, codes_plane = planes[:PLANE], planes[PLANE:]
+        moved, *normed_plane = together(moved, *normed_plane)
         pack_e, pack_d = lax.optimization_barrier(
             (
                 jnp.concatenate([widen_e, moved[:padded_narrow]], 0),
@@ -553,7 +551,11 @@
         projected_parts = [
             nt(in_column, block).astype(bf16).reshape(lines, in_cols, tokens) for block in normed_plane
         ]
-        hopped = together(*[hop(projected_parts[k], k) for k in range(1, PLANE)], column)
+        codes_row, *projected_parts = together(codes.reshape(1, tokens), *projected_parts)
+        hopped = together(
+            *spread(codes_row), *[hop(projected_parts[k], k) for k in range(1, PLANE)], column
+        )
+        codes_plane, hopped = hopped[:PLANE], hopped[PLANE:]
         column = hopped[-1]
         projected = in_plane([projected_parts[0], *hopped[:-1]], 1).reshape(3 * inner, tokens)
         out_pieces = together(*spread(column[:, in_cols : in_cols + cross_cols]), column)
@@ -595,7 +597,7 @@
             return dict(specs=specs), [pack for pack in packs for _ in range(2)]
 
         def feed_grads(own, other, *ties):
-            (pack,) = call(feed_grads_kernel, ((pack_shape, bf16),), *own, *other, time_us=0.3, ties=ties)
+            (pack,) = call(feed_grads_kernel, ((pack_shape, bf16),), *own, *other, time_us=1, ties=ties)
             return pack
 
         own_e, *stream_e = together(own_e, *stream_e)
@@ -728,7 +730,7 @@
             value_other,
             slope_other,
             ties=(stream_one_d, cross_kept),
-            time_us=0.3,
+            time_us=1,
             **options,
         )
         def by_plane(*products):

time: 569 us -> 565 us (level)
  starting transfers between devices: 112 us -> 91.3 us
  waiting for transfers between devices: 221 us -> 233 us
    ppermute x78, waiting for transfers between devices: 194 us -> 222 us  [permute(): return lax.ppermute(block, axes, route).reshape(shape)]
    ppermute x78, starting transfers between devices: 111 us -> 90.5 us  [permute(): return lax.ppermute(block, axes, route).reshape(shape)]
    all_gather x1, waiting for transfers between devices: 11.9 us -> 4.24 us  [per_device(): own_e = lax.all_gather(pack_e, 'line', axis=0)]
    all_gather x1, waiting for transfers between devices: 13.9 us -> 6.82 us  [per_device(): own_d = lax.all_gather(pack_d, 'line', axis=0)]
    unnamed x160 -> x156, local copies, waits for them, and re-layouts: 24.5 us -> 24.5 us
  transfers between devices with their start and end apart: 84 -> 84, of which waited for: 40 -> 39; matrix products, arithmetic and copies ran while one was open for 10% -> 11% of each run, Pallas kernels for 22% -> 22%
where the time goes in v5:
time: 565 us; the launch traced here: 557 us
  waiting for transfers between devices  233 us (41%)
  Pallas kernels  131 us (23%)
  starting transfers between devices  91.3 us (16%)
  local copies, waits for them, and re-layouts  45.3 us (8%)
  other arithmetic  34.5 us (6%)
  between operations  15.5 us (3%)
  matrix products  6.55 us (1%)
    ppermute x78, waiting for transfers between devices, permute(): return lax.ppermute(block, axes, route).reshape(shape)  222 us
    pallas_call x18, Pallas kernels, call(): pl.pallas_call(lambda *refs: kernel(*refs[:first], *refs[after:]), grid=(...  131 us
    ppermute x78, starting transfers between devices, permute(): return lax.ppermute(block, axes, route).reshape(shape)  90.5 us
    unnamed x156, local copies, waits for them, and re-layouts  24.5 us
  transfers between devices with their start and end apart: 84, of which 39 were waited for; matrix products, arithmetic and copies ran while one was open for 11% of the time, Pallas kernels for 22%

profile of v5, /device:TPU:0, one launch (start us, length us, event | category | flops | bytes accessed | tf_op | source)
XLA Modules:
  0.0 557.1 jit_solution(10140955031811045673)
XLA Ops:
  23.1 6.7 %collective-permute-start.3 = (bf16[28,8,1472]{2,1,0:T(8,128)(2,1)}, bf16[28,8,1472]{2,1,0:T(8,128)(2,1)}, u32[]{:S(2)}, u32[]{:S(2)}) collective-permute-start(bf16[28,8,1472]{2,1,0:T(8,128)(2,1)} %maximum_bitcast_fusion), channel_id=1, source_target_pairs={{0,0},{1,16},{2,1},{3,17},{4,2},{5,18},{6,3},{7,19},{8,8},{9,24},{... | collective-permute-start | bytes 1978376 | tf_op jit(solution)/shard_map/ppermute | solution.py:38
  37.6 28.1 %collective-permute-done.5 = bf16[32,8,1472]{2,1,0:T(8,128)(2,1)} collective-permute-done((bf16[32,8,1472]{2,1,0:T(8,128)(2,1)}, bf16[32,8,1472]{2,1,0:T(8,128)(2,1)}, u32[]{:S(2)}, u32[]{:S(2)}) %collective-permute-start.5) | collective-permute-done | bytes 753696 | tf_op jit(solution)/shard_map/ppermute | solution.py:38
  95.4 6.3 %collective-permute-done.13 = bf16[4,24,1472]{2,1,0:T(8,128)(2,1)S(1)} collective-permute-done((bf16[4,24,1472]{2,1,0:T(8,128)(2,1)S(1)}, bf16[4,24,1472]{2,1,0:T(8,128)(2,1)S(1)}, u32[]{:S(2)}, u32[]{:S(2)}) %collective-permute-start.13) | collective-permute-done | bytes 282656 | tf_op jit(solution)/shard_map/ppermute | solution.py:38
  101.7 6.8 %collective-permute-done.14 = bf16[4,24,1472]{2,1,0:T(8,128)(2,1)S(1)} collective-permute-done((bf16[4,24,1472]{2,1,0:T(8,128)(2,1)S(1)}, bf16[4,24,1472]{2,1,0:T(8,128)(2,1)S(1)}, u32[]{:S(2)}, u32[]{:S(2)}) %collective-permute-start.14) | collective-permute-done | bytes 282656 | tf_op jit(solution)/shard_map/ppermute | solution.py:38
  126.0 8.2 %collective-permute-done.17 = bf16[16,8,1472]{2,1,0:T(8,128)(2,1)S(1)} collective-permute-done((bf16[16,8,1472]{2,1,0:T(8,128)(2,1)}, bf16[16,8,1472]{2,1,0:T(8,128)(2,1)S(1)}, u32[]{:S(2)}, u32[]{:S(2)}) %collective-permute-start.17) | collective-permute-done | bytes 376864 | tf_op jit(solution)/shard_map/ppermute | solution.py:38
  134.3 7.7 %collective-permute-done.18 = bf16[16,8,1472]{2,1,0:T(8,128)(2,1)S(1)} collective-permute-done((bf16[16,8,1472]{2,1,0:T(8,128)(2,1)}, bf16[16,8,1472]{2,1,0:T(8,128)(2,1)S(1)}, u32[]{:S(2)}, u32[]{:S(2)}) %collective-permute-start.18) | collective-permute-done | bytes 376864 | tf_op jit(solution)/shard_map/ppermute | solution.py:38
  153.0 7.3 %shard_map.189 = (bf16[448,512]{1,0:T(8,128)(2,1)}, bf16[448,512]{1,0:T(8,128)(2,1)}, bf16[448,512]{1,0:T(8,128)(2,1)}, bf16[512,1472]{1,0:T(8,128)(2,1)}, bf16[512,1472]{1,0:T(8,128)(2,1)}) custom-call(bf16[128,1472]{1,0:T(8,128)(2,1)} %get-tuple-element.201.refs_0_, bf16[128,1472]{1,0:T(8,128)(2,1)} %bitcast.427, bf16[128,1472]{1,0:T(8,128)(2,1)} %bitcast.428, ...), custom_call_target="tpu_custom_call" | custom-call | flops 800000000 | bytes 2500000 | tf_op jit(solution)/shard_map/pallas_call | solution.py:79
  160.2 9.4 %collective-permute-done.21 = bf16[4,48,1472]{2,1,0:T(8,128)(2,1)S(1)} collective-permute-done((bf16[4,48,1472]{2,1,0:T(8,128)(2,1)S(1)}, bf16[4,48,1472]{2,1,0:T(8,128)(2,1)S(1)}, u32[]{:S(2)}, u32[]{:S(2)}) %collective-permute-start.21) | collective-permute-done | bytes 565280 | tf_op jit(solution)/shard_map/ppermute | solution.py:38
  178.5 7.1 %shard_map.190 = (bf16[448,512]{1,0:T(8,128)(2,1)}, bf16[448,512]{1,0:T(8,128)(2,1)}, bf16[448,512]{1,0:T(8,128)(2,1)}, bf16[128,1472]{1,0:T(8,128)(2,1)}, bf16[...) custom-call(bf16[512,1472]{1,0:T(8,128)(2,1)} %get-tuple-element.208.refs_0_, ...), custom_call_target="tpu_custom_call" | custom-call | flops 800000000 | bytes 2500000 | tf_op jit(solution)/shard_map/pallas_call | solution.py:79
  185.5 6.8 %collective-permute-done.25 = bf16[16,8,1472]{2,1,0:T(8,128)(2,1)S(1)} collective-permute-done((bf16[16,8,1472]{2,1,0:T(8,128)(2,1)S(1)}, bf16[16,8,1472]{2,1,0:T(8,128)(2,1)S(1)}, u32[]{:S(2)}, u32[]{:S(2)}) %collective-permute-start.25) | collective-permute-done | bytes 376864 | tf_op jit(solution)/shard_map/ppermute | solution.py:38
  204.7 8.3 %collective-permute-done.28 = bf16[16,8,1472]{2,1,0:T(8,128)(2,1)S(1)} collective-permute-done((bf16[16,8,1472]{2,1,0:T(8,128)(2,1)}, bf16[16,8,1472]{2,1,0:T(8,128)(2,1)S(1)}, u32[]{:S(2)}, u32[]{:S(2)}) %collective-permute-start.28) | collective-permute-done | bytes 376864 | tf_op jit(solution)/shard_map/ppermute | solution.py:38
  213.9 8.6 %shard_map.191 = (f32[128,1472]{1,0:T(8,128)}, bf16[128,1472]{1,0:T(8,128)(2,1)}, bf16[384,128]{1,0:T(8,128)(2,1)}, bf16[768,128]{1,0:T(8,128)(2,1)}, bf16[384,1...) custom-call(bf16[128,1472]{1,0:T(8,128)(2,1)} %get-tuple-element.215.refs_0_, ...), custom_call_target="tpu_custom_call" | custom-call | flops 800000000 | bytes 2500000 | tf_op jit(solution)/shard_map/pallas_call | solution.py:79
  226.0 6.8 %all-gather.11.cloned.1.call-done = bf16[1344,1472]{1,0:T(8,128)(2,1)} async-done(((bf16[336,1472]{1,0:T(8,128)(2,1)}), bf16[1344,1472]{1,0:T(8,128)(2,1)}) %all-gather.11.cloned.1.call-update) | async-done | bytes 3956752 | tf_op jit(solution)/shard_map/all_gather | solution.py:549
  234.7 6.0 %collective-permute-done.32 = bf16[16,8,1472]{2,1,0:T(8,128)(2,1)S(1)} collective-permute-done((bf16[16,8,1472]{2,1,0:T(8,128)(2,1)}, bf16[16,8,1472]{2,1,0:T(8,128)(2,1)S(1)}, u32[]{:S(2)}, u32[]{:S(2)}) %collective-permute-start.32) | collective-permute-done | bytes 376864 | tf_op jit(solution)/shard_map/ppermute | solution.py:38
  241.7 9.9 %shard_map.192 = (bf16[1344,512]{1,0:T(8,128)(2,1)}, bf16[512,1472]{1,0:T(8,128)(2,1)}, bf16[512,1472]{1,0:T(8,128)(2,1)}, bf16[512,1472]{1,0:T(8,128)(2,1)}, bf16[512,1472]{1,0:T(8,128)(2,1)}) custom-call(bf16[128,1472]{1,0:T(8,128)(2,1)} %get-tuple-element.230.refs_0_, bf16[128,1472]{1,0:T(8,128)(2,1)} %bitcast.438, bf16[128,1472]{1,0:T(8,128)(2,1)} %bitcast.442, ...), custom_call_target="tpu_custom_call" | custom-call | flops 800000000 | bytes 2500000 | tf_op jit(solution)/shard_map/pallas_call | solution.py:79
  254.1 10.7 %shard_map.193 = (bf16[1344,512]{1,0:T(8,128)(2,1)}, bf16[128,1472]{1,0:T(8,128)(2,1)}, bf16[128,1472]{1,0:T(8,128)(2,1)}, bf16[128,1472]{1,0:T(8,128)(2,1)}, bf...) custom-call(bf16[512,1472]{1,0:T(8,128)(2,1)} %get-tuple-element.238, ...), custom_call_target="tpu_custom_call" | custom-call | flops 800000000 | bytes 2500000 | tf_op jit(solution)/shard_map/pallas_call | solution.py:79
  269.4 10.1 %shard_map.194.refs_15_ = bf16[4,336,1472]{2,1,0:T(8,128)(2,1)} custom-call(bf16[512,1472]{1,0:T(8,128)(2,1)} %get-tuple-element.238.refs_0_, bf16[512,1472]{1,0:T(8,128)(2,1)} %get-tuple-element.239.refs_1_, bf16[1344,512]{1,0:T(8,128)(2,1)} %get-tuple-element.248.refs_2_, bf16[512,1472]{1,0:T(8,128)(2,1)} %bitcast.393, bf16[512,1472]{1,0:T(8,128)(2,1)} %bitcast.394, ...), custom_call_target="tpu_custom_call" | custom-call | flops 800000000 | bytes 2500000 | tf_op jit(solution)/shard_map/pallas_call | solution.py:79
  284.0 8.5 %collective-permute-done.35 = bf16[16,8,1472]{2,1,0:T(8,128)(2,1)S(1)} collective-permute-done((bf16[16,8,1472]{2,1,0:T(8,128)(2,1)S(1)}, bf16[16,8,1472]{2,1,0:T(8,128)(2,1)S(1)}, u32[]{:S(2)}, u32[]{:S(2)}) %collective-permute-start.35) | collective-permute-done | bytes 376864 | tf_op jit(solution)/shard_map/ppermute | solution.py:38
  292.4 7.0 %collective-permute-done.36 = bf16[16,8,1472]{2,1,0:T(8,128)(2,1)S(1)} collective-permute-done((bf16[16,8,1472]{2,1,0:T(8,128)(2,1)S(1)}, bf16[16,8,1472]{2,1,0:T(8,128)(2,1)S(1)}, u32[]{:S(2)}, u32[]{:S(2)}) %collective-permute-start.36) | collective-permute-done | bytes 376864 | tf_op jit(solution)/shard_map/ppermute | solution.py:38
  302.0 9.3 %shard_map.195 = (f32[128,1472]{1,0:T(8,128)}, bf16[128,1472]{1,0:T(8,128)(2,1)}, bf16[1152,128]{1,0:T(8,128)(2,1)}, f32[128,1472]{1,0:T(8,128)}, bf16[128,1472]...) custom-call(bf16[128,1472]{1,0:T(8,128)(2,1)} %get-tuple-element.242.refs_0_, bf16[128,1472]{1,0:T(8,128)(2,1)} %bitcast.437, ...), custom_call_target="tpu_custom_call" | custom-call | flops 800000000 | bytes 2500000 | tf_op jit(solution)/shard_map/pallas_call | solution.py:79
  323.5 6.9 %collective-permute-done.42 = bf16[16,8,1472]{2,1,0:T(8,128)(2,1)S(1)} collective-permute-done((bf16[16,8,1472]{2,1,0:T(8,128)(2,1)}, bf16[16,8,1472]{2,1,0:T(8,128)(2,1)S(1)}, u32[]{:S(2)}, u32[]{:S(2)}) %collective-permute-start.42) | collective-permute-done | bytes 376864 | tf_op jit(solution)/shard_map/ppermute | solution.py:38
  331.3 11.1 %shard_map.198 = (bf16[896,512]{1,0:T(8,128)(2,1)}, bf16[896,512]{1,0:T(8,128)(2,1)}, bf16[512,1472]{1,0:T(8,128)(2,1)}, bf16[128,1472]{1,0:T(8,128)(2,1)}, bf16...) custom-call(bf16[128,1472]{1,0:T(8,128)(2,1)} %get-tuple-element.251.refs_0_, ...), custom_call_target="tpu_custom_call" | custom-call | flops 800000000 | bytes 2500000 | tf_op jit(solution)/shard_map/pallas_call | solution.py:79
  349.6 10.1 %shard_map.199.refs_9_ = bf16[4,336,1472]{2,1,0:T(8,128)(2,1)} custom-call(bf16[512,1472]{1,0:T(8,128)(2,1)} %get-tuple-element.208.refs_0_, bf16[512,1472]{1,0:T(8,128)(2,1)} %get-tuple-element.271.refs_1_, bf16[896,512]{1,0:T(8,128)(2,1)} %get-tuple-element.272.refs_2_, bf16[448,512]{1,0:T(8,128)(2,1)} %get-tuple-element.273.refs_3_, ...), custom_call_target="tpu_custom_call" | custom-call | flops 800000000 | bytes 2500000 | tf_op jit(solution)/shard_map/pallas_call | solution.py:79
  365.6 6.8 %collective-permute-done.44 = bf16[16,8,1472]{2,1,0:T(8,128)(2,1)S(1)} collective-permute-done((bf16[16,8,1472]{2,1,0:T(8,128)(2,1)}, bf16[16,8,1472]{2,1,0:T(8,128)(2,1)S(1)}, u32[]{:S(2)}, u32[]{:S(2)}) %collective-permute-start.44) | collective-permute-done | bytes 376864 | tf_op jit(solution)/shard_map/ppermute | solution.py:38
  372.3 9.1 %collective-permute-done.45 = bf16[16,8,1472]{2,1,0:T(8,128)(2,1)S(1)} collective-permute-done((bf16[16,8,1472]{2,1,0:T(8,128)(2,1)S(1)}, bf16[16,8,1472]{2,1,0:T(8,128)(2,1)S(1)}, u32[]{:S(2)}, u32[]{:S(2)}) %collective-permute-start.45) | collective-permute-done | bytes 376864 | tf_op jit(solution)/shard_map/ppermute | solution.py:38
  391.6 8.7 %shard_map.201 = (f32[256,1472]{1,0:T(8,128)}, bf16[256,1472]{1,0:T(8,128)(2,1)}, bf16[1152,256]{1,0:T(8,128)(2,1)}) custom-call(s32[1]{0:T(128)} %bitcast.38.refs_0_.refs_4_.refs_12_, f32[128,1472]{1,0:T(8,128)} %get-tuple-element.277.refs_1_, f32[128,1472]{1,0:T(8,128)} %bitcast.408, bf16[384,1472]{1,0:T(8,128)(2,1)} %bitcast.362, ...), custom_call_target="tpu_custom_call" | custom-call | flops 800000000 | bytes 2500000 | tf_op jit(solution)/shard_map/pallas_call | solution.py:79
  403.6 12.3 %collective-permute-done.54 = bf16[4,48,1472]{2,1,0:T(8,128)(2,1)S(1)} collective-permute-done((bf16[4,48,1472]{2,1,0:T(8,128)(2,1)S(1)}, bf16[4,48,1472]{2,1,0:T(8,128)(2,1)S(1)}, u32[]{:S(2)}, u32[]{:S(2)}) %collective-permute-start.54) | collective-permute-done | bytes 565280 | tf_op jit(solution)/shard_map/ppermute | solution.py:38
  428.7 9.7 %shard_map.203 = bf16[448,1472]{1,0:T(8,128)(2,1)} custom-call(bf16[288,256]{1,0:T(8,128)(2,1)} %bitcast.400, bf16[288,256]{1,0:T(8,128)(2,1)} %bitcast.412, bf16[288,256]{1,0:T(8,128)(2,1)} %bitcast.414, bf16[288,256]{1,0:T(8,128)(2,1)} %bitcast.416, s32[1,256]{1,0:T(1,128)} %bitcast.460, s32[1,256]{1,0:T(1,128)} %copy-done.66, s32[1,256]{1,0:T(1,128)} %copy-done.67, ...), custom_call_target="tpu_custom_call" | custom-call | flops 800000000 | bytes 2500000 | tf_op jit(solution)/shard_map/pallas_call | solution.py:79
  446.4 6.4 %collective-permute-done.64 = bf16[14,8,1472]{2,1,0:T(8,128)(2,1)S(1)} collective-permute-done((bf16[14,8,1472]{2,1,0:T(8,128)(2,1)}, bf16[14,8,1472]{2,1,0:T(8,128)(2,1)S(1)}, u32[]{:S(2)}, u32[]{:S(2)}) %collective-permute-start.64) | collective-permute-done | bytes 329760 | tf_op jit(solution)/shard_map/ppermute | solution.py:38
  487.1 6.7 %collective-permute-start.76 = (bf16[28,8,1472]{2,1,0:T(8,128)(2,1)}, bf16[28,8,1472]{2,1,0:T(8,128)(2,1)}, u32[]{:S(2)}, u32[]{:S(2)}) collective-permute-start(bf16[28,8,1472]{2,1,0:T(8,128)(2,1)} %maximum_bitcast_fusion.1), channel_id=1, source_target_pairs={{0,0},{16,1},{1,2},{17,3},{2,4},{18,5},{3,6},{19,7},{8,8},{24,9},{... | collective-permute-start | bytes 1978376 | tf_op jit(solution)/shard_map/ppermute | solution.py:38
  500.4 7.6 %collective-permute-start.71 = (bf16[14,8,1472]{2,1,0:T(8,128)(2,1)S(1)}, bf16[14,8,1472]{2,1,0:T(8,128)(2,1)}, u32[]{:S(2)}, u32[]{:S(2)}) collective-permute-start(bf16[14,8,1472]{2,1,0:T(8,128)(2,1)S(1)} %get-tuple-element.400), channel_id=1, source_target_pairs={{0,3},{1,2},{2,1},{3,0},{4,7},{5,6},{6,5},{7,4},{8,11},{9,10},{10,... | collective-permute-start | bytes 989192 | tf_op jit(solution)/shard_map/ppermute | solution.py:38
  509.2 15.1 %collective-permute-done.69 = bf16[14,8,1472]{2,1,0:T(8,128)(2,1)} collective-permute-done((bf16[14,8,1472]{2,1,0:T(8,128)(2,1)S(1)}, bf16[14,8,1472]{2,1,0:T(8,128)(2,1)}, u32[]{:S(2)}, u32[]{:S(2)}) %collective-permute-start.69) | collective-permute-done | bytes 329760 | tf_op jit(solution)/shard_map/ppermute | solution.py:38
  (404 shorter events, 251.4 us)
Async XLA Ops:
  7.2 62.9 %all-gather.9.cloned.1.call-start = ((), (), s32[]{:S(2)}) async-start(), calls=%async_computation.7 | async-start | bytes 2211840 | tf_op jit(solution)/shard_map/all_gather | solution.py:503
  12.8 24.8 %collective-permute-start.4 = (bf16[32,8,1472]{2,1,0:T(8,128)(2,1)}, bf16[32,8,1472]{2,1,0:T(8,128)(2,1)S(1)}, u32[]{:S(2)}, u32[]{:S(2)}) collective-permute-start(bf16[32,8,1472]{2,1,0:T(8,128)(2,1)} %fusion.49), channel_id=1, source_target_pairs={{0,1},{1,0},{2,3},{3,2},{4,5},{5,4},{6,7},{7,6},{8,9},{9,8},{10,11... | collective-permute-start | bytes 2261000 | tf_op jit(solution)/shard_map/ppermute | solution.py:38
  15.8 50.0 %collective-permute-start.5 = (bf16[32,8,1472]{2,1,0:T(8,128)(2,1)}, bf16[32,8,1472]{2,1,0:T(8,128)(2,1)}, u32[]{:S(2)}, u32[]{:S(2)}) collective-permute-start(bf16[32,8,1472]{2,1,0:T(8,128)(2,1)} %fusion.49), channel_id=1, source_target_pairs={{0,2},{1,3},{2,0},{3,1},{4,6},{5,7},{6,4},{7,5},{8,10},{9,11},{10,... | collective-permute-start | bytes 2261000 | tf_op jit(solution)/shard_map/ppermute | solution.py:38
  17.3 48.4 %collective-permute-start.6 = (bf16[32,8,1472]{2,1,0:T(8,128)(2,1)}, bf16[32,8,1472]{2,1,0:T(8,128)(2,1)}, u32[]{:S(2)}, u32[]{:S(2)}) collective-permute-start(bf16[32,8,1472]{2,1,0:T(8,128)(2,1)} %fusion.49), channel_id=1, source_target_pairs={{0,3},{1,2},{2,1},{3,0},{4,7},{5,6},{6,5},{7,4},{8,11},{9,10},{10,... | collective-permute-start | bytes 2261000 | tf_op jit(solution)/shard_map/ppermute | solution.py:38
  20.6 132.4 %all-gather.7.cloned.1.call-start = ((), (), s32[]{:S(2)}) async-start(), calls=%async_computation.6 | async-start | bytes 5160960 | tf_op jit(solution)/shard_map/all_gather | solution.py:548
  23.1 42.6 %collective-permute-start.3 = (bf16[28,8,1472]{2,1,0:T(8,128)(2,1)}, bf16[28,8,1472]{2,1,0:T(8,128)(2,1)}, u32[]{:S(2)}, u32[]{:S(2)}) collective-permute-start(bf16[28,8,1472]{2,1,0:T(8,128)(2,1)} %maximum_bitcast_fusion), channel_id=1, source_target_pairs={{0,0},{1,16},{2,1},{3,17},{4,2},{5,18},{6,3},{7,19},{8,8},{9,24},{... | collective-permute-start | bytes 1978376 | tf_op jit(solution)/shard_map/ppermute | solution.py:38
  68.4 164.4 %all-gather.11.cloned.1.call-start = ((), (), s32[]{:S(2)}) async-start(), calls=%async_computation.8 | async-start | bytes 5160960 | tf_op jit(solution)/shard_map/all_gather | solution.py:549
  84.0 31.8 %collective-permute-start = (bf16[131,1472]{1,0:T(8,128)(2,1)}, bf16[131,1472]{1,0:T(8,128)(2,1)S(1)}, u32[]{:S(2)}, u32[]{:S(2)}) collective-permute-start(bf16[131,1472]{1,0:T(8,128)(2,1)} %pad_maximum_fusion.6), channel_id=1, source_target_pairs={{0,16},{16,0},{1,17},{17,1},{2,18},{18,2},{3,19},{19,3},{4,20},{20... | collective-permute-start | bytes 1157000 | tf_op jit(solution)/shard_map/ppermute | solution.py:38
  122.4 19.5 %collective-permute-start.18 = (bf16[16,8,1472]{2,1,0:T(8,128)(2,1)}, bf16[16,8,1472]{2,1,0:T(8,128)(2,1)S(1)}, u32[]{:S(2)}, u32[]{:S(2)}) collective-permute-start(bf16[16,8,1472]{2,1,0:T(8,128)(2,1)} %bitcast.425), channel_id=1, source_target_pairs={{0,2},{1,3},{2,0},{3,1},{4,6},{5,7},{6,4},{7,5},{8,10},{9,11},{10,... | collective-permute-start | bytes 1130504 | tf_op jit(solution)/shard_map/ppermute | solution.py:38
  125.8 233.9 %reduce-scatter.4.cloned.1.call-start = ((), (), s32[]{:S(2)}) async-start(), calls=%async_computation.3 | async-start | bytes 5160960 | tf_op jit(solution)/shard_map/reduce_scatter | solution.py:747
  145.1 24.5 %collective-permute-start.21 = (bf16[4,48,1472]{2,1,0:T(8,128)(2,1)S(1)}, bf16[4,48,1472]{2,1,0:T(8,128)(2,1)S(1)}, u32[]{:S(2)}, u32[]{:S(2)}) collective-permute-start(bf16[4,48,1472]{2,1,0:T(8,128)(2,1)S(1)} %slice.90), channel_id=1, source_target_pairs={{0,2},{1,3},{2,0},{3,1},{4,6},{5,7},{6,4},{7,5},{8,10},{9,11},{10,... | collective-permute-start | bytes 1695752 | tf_op jit(solution)/shard_map/ppermute | solution.py:38
  145.4 26.0 %collective-permute-start.22 = (bf16[4,48,1472]{2,1,0:T(8,128)(2,1)S(1)}, bf16[4,48,1472]{2,1,0:T(8,128)(2,1)S(1)}, u32[]{:S(2)}, u32[]{:S(2)}) collective-permute-start(bf16[4,48,1472]{2,1,0:T(8,128)(2,1)S(1)} %slice.90), channel_id=1, source_target_pairs={{0,3},{1,2},{2,1},{3,0},{4,7},{5,6},{6,5},{7,4},{8,11},{9,10},{10,... | collective-permute-start | bytes 1695752 | tf_op jit(solution)/shard_map/ppermute | solution.py:38
  153.0 23.4 %collective-permute-start.23 = (bf16[4,336,1472]{2,1,0:T(8,128)(2,1)}, bf16[4,336,1472]{2,1,0:T(8,128)(2,1)S(1)}, u32[]{:S(2)}, u32[]{:S(2)}) collective-permute-start(bf16[4,336,1472]{2,1,0:T(8,128)(2,1)} %bitcast.348), channel_id=1, source_target_pairs={{0,16},{16,0},{1,17},{17,1},{2,18},{18,2},{3,19},{19,3},{4,20},{20... | collective-permute-start | bytes 11870216 | tf_op jit(solution)/shard_map/ppermute | solution.py:38
  172.0 23.9 %collective-permute-start.30 = (bf16[96,8,1472]{2,1,0:T(8,128)(2,1)S(1)}, bf16[96,8,1472]{2,1,0:T(8,128)(2,1)}, u32[]{:S(2)}, u32[]{:S(2)}) collective-permute-start(bf16[96,8,1472]{2,1,0:T(8,128)(2,1)S(1)} %bitcast.364), channel_id=1, source_target_pairs={{0,16},{16,0},{1,17},{17,1},{2,18},{18,2},{3,19},{19,3},{4,20},{20... | collective-permute-start | bytes 6782984 | tf_op jit(solution)/shard_map/ppermute | solution.py:38
  172.8 19.6 %collective-permute-start.25 = (bf16[16,8,1472]{2,1,0:T(8,128)(2,1)S(1)}, bf16[16,8,1472]{2,1,0:T(8,128)(2,1)S(1)}, u32[]{:S(2)}, u32[]{:S(2)}) collective-permute-start(bf16[16,8,1472]{2,1,0:T(8,128)(2,1)S(1)} %bitcast.378), channel_id=1, source_target_pairs={{0,2},{1,3},{2,0},{3,1},{4,6},{5,7},{6,4},{7,5},{8,10},{9,11},{10,... | collective-permute-start | bytes 1130504 | tf_op jit(solution)/shard_map/ppermute | solution.py:38
  193.8 19.1 %collective-permute-start.28 = (bf16[16,8,1472]{2,1,0:T(8,128)(2,1)}, bf16[16,8,1472]{2,1,0:T(8,128)(2,1)S(1)}, u32[]{:S(2)}, u32[]{:S(2)}) collective-permute-start(bf16[16,8,1472]{2,1,0:T(8,128)(2,1)} %bitcast.481), channel_id=1, source_target_pairs={{0,2},{1,3},{2,0},{3,1},{4,6},{5,7},{6,4},{7,5},{8,10},{9,11},{10,... | collective-permute-start | bytes 1130504 | tf_op jit(solution)/shard_map/ppermute | solution.py:38
  194.5 18.4 %collective-permute-start.29 = (bf16[16,8,1472]{2,1,0:T(8,128)(2,1)}, bf16[16,8,1472]{2,1,0:T(8,128)(2,1)S(1)}, u32[]{:S(2)}, u32[]{:S(2)}) collective-permute-start(bf16[16,8,1472]{2,1,0:T(8,128)(2,1)} %bitcast.480), channel_id=1, source_target_pairs={{0,3},{1,2},{2,1},{3,0},{4,7},{5,6},{6,5},{7,4},{8,11},{9,10},{10,... | collective-permute-start | bytes 1130504 | tf_op jit(solution)/shard_map/ppermute | solution.py:38
  279.5 179.3 %reduce-scatter.6.cloned.1.call-start = ((), (), s32[]{:S(2)}) async-start(), calls=%async_computation.4 | async-start | bytes 5160960 | tf_op jit(solution)/shard_map/reduce_scatter | solution.py:749
  282.5 18.7 %collective-permute-start.37 = (bf16[16,8,1472]{2,1,0:T(8,128)(2,1)S(1)}, bf16[16,8,1472]{2,1,0:T(8,128)(2,1)S(1)}, u32[]{:S(2)}, u32[]{:S(2)}) collective-permute-start(bf16[16,8,1472]{2,1,0:T(8,128)(2,1)S(1)} %bitcast.477), channel_id=1, source_target_pairs={{0,3},{1,2},{2,1},{3,0},{4,7},{5,6},{6,5},{7,4},{8,11},{9,10},{10,... | collective-permute-start | bytes 1130504 | tf_op jit(solution)/shard_map/ppermute | solution.py:38
  312.0 18.4 %collective-permute-start.42 = (bf16[16,8,1472]{2,1,0:T(8,128)(2,1)}, bf16[16,8,1472]{2,1,0:T(8,128)(2,1)S(1)}, u32[]{:S(2)}, u32[]{:S(2)}) collective-permute-start(bf16[16,8,1472]{2,1,0:T(8,128)(2,1)} %bitcast.446), channel_id=1, source_target_pairs={{0,2},{1,3},{2,0},{3,1},{4,6},{5,7},{6,4},{7,5},{8,10},{9,11},{10,... | collective-permute-start | bytes 1130504 | tf_op jit(solution)/shard_map/ppermute | solution.py:38
  314.7 28.3 %collective-permute-start.47 = (bf16[64,8,1472]{2,1,0:T(8,128)(2,1)S(1)}, bf16[64,8,1472]{2,1,0:T(8,128)(2,1)S(1)}, u32[]{:S(2)}, u32[]{:S(2)}) collective-permute-start(bf16[64,8,1472]{2,1,0:T(8,128)(2,1)S(1)} %bitcast.367), channel_id=1, source_target_pairs={{0,16},{16,0},{1,17},{17,1},{2,18},{18,2},{3,19},{19,3},{4,20},{20... | collective-permute-start | bytes 4521992 | tf_op jit(solution)/shard_map/ppermute | solution.py:38
  359.7 186.0 %reduce-scatter.8.cloned.1.call-start = ((), (), s32[]{:S(2)}) async-start(), calls=%async_computation.5 | async-start | bytes 2211840 | tf_op jit(solution)/shard_map/reduce_scatter | solution.py:813
  361.8 19.5 %collective-permute-start.45 = (bf16[16,8,1472]{2,1,0:T(8,128)(2,1)S(1)}, bf16[16,8,1472]{2,1,0:T(8,128)(2,1)S(1)}, u32[]{:S(2)}, u32[]{:S(2)}) collective-permute-start(bf16[16,8,1472]{2,1,0:T(8,128)(2,1)S(1)} %bitcast.475), channel_id=1, source_target_pairs={{0,2},{1,3},{2,0},{3,1},{4,6},{5,7},{6,4},{7,5},{8,10},{9,11},{10,... | collective-permute-start | bytes 1130504 | tf_op jit(solution)/shard_map/ppermute | solution.py:38
  362.1 19.2 %collective-permute-start.46 = (bf16[16,8,1472]{2,1,0:T(8,128)(2,1)S(1)}, bf16[16,8,1472]{2,1,0:T(8,128)(2,1)S(1)}, u32[]{:S(2)}, u32[]{:S(2)}) collective-permute-start(bf16[16,8,1472]{2,1,0:T(8,128)(2,1)S(1)} %bitcast.474), channel_id=1, source_target_pairs={{0,3},{1,2},{2,1},{3,0},{4,7},{5,6},{6,5},{7,4},{8,11},{9,10},{10,... | collective-permute-start | bytes 1130504 | tf_op jit(solution)/shard_map/ppermute | solution.py:38
  387.8 28.1 %collective-permute-start.54 = (bf16[4,48,1472]{2,1,0:T(8,128)(2,1)S(1)}, bf16[4,48,1472]{2,1,0:T(8,128)(2,1)S(1)}, u32[]{:S(2)}, u32[]{:S(2)}) collective-permute-start(bf16[4,48,1472]{2,1,0:T(8,128)(2,1)S(1)} %get-tuple-element.361), channel_id=1, source_target_pairs={{0,2},{1,3},{2,0},{3,1},{4,6},{5,7},{6,4},{7,5},{8,10},{9,11},{10,... | collective-permute-start | bytes 1695752 | tf_op jit(solution)/shard_map/ppermute | solution.py:38
  389.1 26.8 %collective-permute-start.55 = (bf16[4,48,1472]{2,1,0:T(8,128)(2,1)S(1)}, bf16[4,48,1472]{2,1,0:T(8,128)(2,1)S(1)}, u32[]{:S(2)}, u32[]{:S(2)}) collective-permute-start(bf16[4,48,1472]{2,1,0:T(8,128)(2,1)S(1)} %get-tuple-element.358), channel_id=1, source_target_pairs={{0,3},{1,2},{2,1},{3,0},{4,7},{5,6},{6,5},{7,4},{8,11},{9,10},{10,... | collective-permute-start | bytes 1695752 | tf_op jit(solution)/shard_map/ppermute | solution.py:38
  480.3 20.1 %collective-permute-start.73 = (bf16[16,8,1472]{2,1,0:T(8,128)(2,1)}, bf16[16,8,1472]{2,1,0:T(8,128)(2,1)}, u32[]{:S(2)}, u32[]{:S(2)}) collective-permute-start(bf16[16,8,1472]{2,1,0:T(8,128)(2,1)} %bitcast.472), channel_id=1, source_target_pairs={{0,2},{1,3},{2,0},{3,1},{4,6},{5,7},{6,4},{7,5},{8,10},{9,11},{10,... | collective-permute-start | bytes 1130504 | tf_op jit(solution)/shard_map/ppermute | solution.py:38
  481.0 28.2 %collective-permute-start.74 = (bf16[16,8,1472]{2,1,0:T(8,128)(2,1)}, bf16[16,8,1472]{2,1,0:T(8,128)(2,1)}, u32[]{:S(2)}, u32[]{:S(2)}) collective-permute-start(bf16[16,8,1472]{2,1,0:T(8,128)(2,1)} %bitcast.471), channel_id=1, source_target_pairs={{0,3},{1,2},{2,1},{3,0},{4,7},{5,6},{6,5},{7,4},{8,11},{9,10},{10,... | collective-permute-start | bytes 1130504 | tf_op jit(solution)/shard_map/ppermute | solution.py:38
  487.1 49.2 %collective-permute-start.76 = (bf16[28,8,1472]{2,1,0:T(8,128)(2,1)}, bf16[28,8,1472]{2,1,0:T(8,128)(2,1)}, u32[]{:S(2)}, u32[]{:S(2)}) collective-permute-start(bf16[28,8,1472]{2,1,0:T(8,128)(2,1)} %maximum_bitcast_fusion.1), channel_id=1, source_target_pairs={{0,0},{16,1},{1,2},{17,3},{2,4},{18,5},{3,6},{19,7},{8,8},{24,9},{... | collective-permute-start | bytes 1978376 | tf_op jit(solution)/shard_map/ppermute | solution.py:38
  494.7 29.6 %collective-permute-start.69 = (bf16[14,8,1472]{2,1,0:T(8,128)(2,1)S(1)}, bf16[14,8,1472]{2,1,0:T(8,128)(2,1)}, u32[]{:S(2)}, u32[]{:S(2)}) collective-permute-start(bf16[14,8,1472]{2,1,0:T(8,128)(2,1)S(1)} %get-tuple-element.400), channel_id=1, source_target_pairs={{0,1},{1,0},{2,3},{3,2},{4,5},{5,4},{6,7},{7,6},{8,9},{9,8},{10,11... | collective-permute-start | bytes 989192 | tf_op jit(solution)/shard_map/ppermute | solution.py:38
  494.7 29.6 %collective-permute-start.70 = (bf16[14,8,1472]{2,1,0:T(8,128)(2,1)S(1)}, bf16[14,8,1472]{2,1,0:T(8,128)(2,1)}, u32[]{:S(2)}, u32[]{:S(2)}) collective-permute-start(bf16[14,8,1472]{2,1,0:T(8,128)(2,1)S(1)} %get-tuple-element.400), channel_id=1, source_target_pairs={{0,2},{1,3},{2,0},{3,1},{4,6},{5,7},{6,4},{7,5},{8,10},{9,11},{10,... | collective-permute-start | bytes 989192 | tf_op jit(solution)/shard_map/ppermute | solution.py:38
  500.4 24.0 %collective-permute-start.71 = (bf16[14,8,1472]{2,1,0:T(8,128)(2,1)S(1)}, bf16[14,8,1472]{2,1,0:T(8,128)(2,1)}, u32[]{:S(2)}, u32[]{:S(2)}) collective-permute-start(bf16[14,8,1472]{2,1,0:T(8,128)(2,1)S(1)} %get-tuple-element.400), channel_id=1, source_target_pairs={{0,3},{1,2},{2,1},{3,0},{4,7},{5,6},{6,5},{7,4},{8,11},{9,10},{10,... | collective-permute-start | bytes 989192 | tf_op jit(solution)/shard_map/ppermute | solution.py:38
  (128 other events, 1101.6 us)
Sparse Core Ops, SparseCore 0:
  20.7 46.3 all-gather.8
  69.2 83.6 all-gather.6
  154.5 78.2 all-gather.10
  279.6 74.9 reduce-scatter.3
  359.8 74.7 reduce-scatter.5
  509.3 35.8 reduce-scatter.7

commit v6 on v5

--- a/solution.py
+++ b/solution.py
@@ -807,9 +807,8 @@
         halves = plane_sum.reshape(2, padded // 8, width)
         chip_sum = rounded(at(halves, section).astype(f32) + swap(at(halves, 1 - section)).astype(f32))
         rest_pack = jnp.concatenate([in_part.reshape(lines, in_cols, width), cross_part, out_part], 1)
-        rest_pack, line_sum, summed_d, summed_e = together(
-            rest_pack, sum_line(chip_sum), summed_d, summed_e
-        )
+        chip_sum, rest_pack = together(chip_sum, rest_pack)
+        line_sum, summed_d, summed_e = together(sum_line(chip_sum), summed_d, summed_e)
         rest_sum = lax.psum_scatter(rest_pack, "line", scatter_dimension=0).astype(f32)
         pieces = together(*spread(in_order(line_sum, swap(line_sum))), *part_d)
         second_out_d = second_d + sum(part.astype(f32) for part in pieces[PLANE:])

time: 565 us -> 559 us (0.989)
  waiting for transfers between devices: 233 us -> 227 us
    ppermute x78, waiting for transfers between devices: 222 us -> 216 us  [permute(): return lax.ppermute(block, axes, route).reshape(shape)]
    unnamed x156 -> x152, local copies, waits for them, and re-layouts: 24.5 us -> 23.2 us
  transfers between devices with their start and end apart: 84 -> 84, of which waited for: 39 -> 40; matrix products, arithmetic and copies ran while one was open for 11% -> 11% of each run, Pallas kernels for 22% -> 22%
where the time goes in v6:
time: 559 us; the launch traced here: 550 us
  waiting for transfers between devices  227 us (41%)
  Pallas kernels  131 us (23%)
  starting transfers between devices  90.3 us (16%)
  local copies, waits for them, and re-layouts  44.9 us (8%)
  other arithmetic  34 us (6%)
  between operations  15.6 us (3%)
  matrix products  6.57 us (1%)
    ppermute x78, waiting for transfers between devices, permute(): return lax.ppermute(block, axes, route).reshape(shape)  216 us
    pallas_call x18, Pallas kernels, call(): pl.pallas_call(lambda *refs: kernel(*refs[:first], *refs[after:]), grid=(...  131 us
    ppermute x78, starting transfers between devices, permute(): return lax.ppermute(block, axes, route).reshape(shape)  89.4 us
    unnamed x152, local copies, waits for them, and re-layouts  23.2 us
  transfers between devices with their start and end apart: 84, of which 40 were waited for; matrix products, arithmetic and copies ran while one was open for 11% of the time, Pallas kernels for 22%

profile of v6, /device:TPU:0, one launch (start us, length us, event | category | flops | bytes accessed | tf_op | source)
XLA Modules:
  0.0 549.9 jit_solution(14923303892029719814)
XLA Ops:
  23.1 6.8 %collective-permute-start.3 = (bf16[28,8,1472]{2,1,0:T(8,128)(2,1)}, bf16[28,8,1472]{2,1,0:T(8,128)(2,1)}, u32[]{:S(2)}, u32[]{:S(2)}) collective-permute-start(bf16[28,8,1472]{2,1,0:T(8,128)(2,1)} %maximum_bitcast_fusion), channel_id=1, source_target_pairs={{0,0},{1,16},{2,1},{3,17},{4,2},{5,18},{6,3},{7,19},{8,8},{9,24},{... | collective-permute-start | bytes 1978376 | tf_op jit(solution)/shard_map/ppermute | solution.py:38
  35.8 30.0 %collective-permute-done.5 = bf16[32,8,1472]{2,1,0:T(8,128)(2,1)} collective-permute-done((bf16[32,8,1472]{2,1,0:T(8,128)(2,1)}, bf16[32,8,1472]{2,1,0:T(8,128)(2,1)}, u32[]{:S(2)}, u32[]{:S(2)}) %collective-permute-start.5) | collective-permute-done | bytes 753696 | tf_op jit(solution)/shard_map/ppermute | solution.py:38
  95.9 6.3 %collective-permute-done.13 = bf16[4,24,1472]{2,1,0:T(8,128)(2,1)S(1)} collective-permute-done((bf16[4,24,1472]{2,1,0:T(8,128)(2,1)S(1)}, bf16[4,24,1472]{2,1,0:T(8,128)(2,1)S(1)}, u32[]{:S(2)}, u32[]{:S(2)}) %collective-permute-start.13) | collective-permute-done | bytes 282656 | tf_op jit(solution)/shard_map/ppermute | solution.py:38
  102.2 6.8 %collective-permute-done.14 = bf16[4,24,1472]{2,1,0:T(8,128)(2,1)S(1)} collective-permute-done((bf16[4,24,1472]{2,1,0:T(8,128)(2,1)S(1)}, bf16[4,24,1472]{2,1,0:T(8,128)(2,1)S(1)}, u32[]{:S(2)}, u32[]{:S(2)}) %collective-permute-start.14) | collective-permute-done | bytes 282656 | tf_op jit(solution)/shard_map/ppermute | solution.py:38
  126.5 8.2 %collective-permute-done.17 = bf16[16,8,1472]{2,1,0:T(8,128)(2,1)S(1)} collective-permute-done((bf16[16,8,1472]{2,1,0:T(8,128)(2,1)}, bf16[16,8,1472]{2,1,0:T(8,128)(2,1)S(1)}, u32[]{:S(2)}, u32[]{:S(2)}) %collective-permute-start.17) | collective-permute-done | bytes 376864 | tf_op jit(solution)/shard_map/ppermute | solution.py:38
  134.7 7.7 %collective-permute-done.18 = bf16[16,8,1472]{2,1,0:T(8,128)(2,1)S(1)} collective-permute-done((bf16[16,8,1472]{2,1,0:T(8,128)(2,1)}, bf16[16,8,1472]{2,1,0:T(8,128)(2,1)S(1)}, u32[]{:S(2)}, u32[]{:S(2)}) %collective-permute-start.18) | collective-permute-done | bytes 376864 | tf_op jit(solution)/shard_map/ppermute | solution.py:38
  153.7 7.3 %shard_map.189 = (bf16[448,512]{1,0:T(8,128)(2,1)}, bf16[448,512]{1,0:T(8,128)(2,1)}, bf16[448,512]{1,0:T(8,128)(2,1)}, bf16[512,1472]{1,0:T(8,128)(2,1)}, bf16[512,1472]{1,0:T(8,128)(2,1)}) custom-call(bf16[128,1472]{1,0:T(8,128)(2,1)} %get-tuple-element.202.refs_0_, bf16[128,1472]{1,0:T(8,128)(2,1)} %bitcast.409, bf16[128,1472]{1,0:T(8,128)(2,1)} %bitcast.410, ...), custom_call_target="tpu_custom_call" | custom-call | flops 800000000 | bytes 2500000 | tf_op jit(solution)/shard_map/pallas_call | solution.py:79
  161.0 9.1 %collective-permute-done.21 = bf16[4,48,1472]{2,1,0:T(8,128)(2,1)S(1)} collective-permute-done((bf16[4,48,1472]{2,1,0:T(8,128)(2,1)S(1)}, bf16[4,48,1472]{2,1,0:T(8,128)(2,1)S(1)}, u32[]{:S(2)}, u32[]{:S(2)}) %collective-permute-start.21) | collective-permute-done | bytes 565280 | tf_op jit(solution)/shard_map/ppermute | solution.py:38
  178.9 7.1 %shard_map.190 = (bf16[448,512]{1,0:T(8,128)(2,1)}, bf16[448,512]{1,0:T(8,128)(2,1)}, bf16[448,512]{1,0:T(8,128)(2,1)}, bf16[128,1472]{1,0:T(8,128)(2,1)}, bf16[...) custom-call(bf16[512,1472]{1,0:T(8,128)(2,1)} %get-tuple-element.209.refs_0_, ...), custom_call_target="tpu_custom_call" | custom-call | flops 800000000 | bytes 2500000 | tf_op jit(solution)/shard_map/pallas_call | solution.py:79
  186.0 6.9 %collective-permute-done.25 = bf16[16,8,1472]{2,1,0:T(8,128)(2,1)S(1)} collective-permute-done((bf16[16,8,1472]{2,1,0:T(8,128)(2,1)S(1)}, bf16[16,8,1472]{2,1,0:T(8,128)(2,1)S(1)}, u32[]{:S(2)}, u32[]{:S(2)}) %collective-permute-start.25) | collective-permute-done | bytes 376864 | tf_op jit(solution)/shard_map/ppermute | solution.py:38
  205.3 8.2 %collective-permute-done.28 = bf16[16,8,1472]{2,1,0:T(8,128)(2,1)S(1)} collective-permute-done((bf16[16,8,1472]{2,1,0:T(8,128)(2,1)}, bf16[16,8,1472]{2,1,0:T(8,128)(2,1)S(1)}, u32[]{:S(2)}, u32[]{:S(2)}) %collective-permute-start.28) | collective-permute-done | bytes 376864 | tf_op jit(solution)/shard_map/ppermute | solution.py:38
  214.3 8.6 %shard_map.191 = (f32[128,1472]{1,0:T(8,128)}, bf16[128,1472]{1,0:T(8,128)(2,1)}, bf16[384,128]{1,0:T(8,128)(2,1)}, bf16[768,128]{1,0:T(8,128)(2,1)}, bf16[384,1...) custom-call(bf16[128,1472]{1,0:T(8,128)(2,1)} %get-tuple-element.216.refs_0_, ...), custom_call_target="tpu_custom_call" | custom-call | flops 800000000 | bytes 2500000 | tf_op jit(solution)/shard_map/pallas_call | solution.py:79
  226.4 7.0 %all-gather.11.cloned.1.call-done = bf16[1344,1472]{1,0:T(8,128)(2,1)} async-done(((bf16[336,1472]{1,0:T(8,128)(2,1)}), bf16[1344,1472]{1,0:T(8,128)(2,1)}) %all-gather.11.cloned.1.call-update) | async-done | bytes 3956752 | tf_op jit(solution)/shard_map/all_gather | solution.py:549
  235.2 6.0 %collective-permute-done.32 = bf16[16,8,1472]{2,1,0:T(8,128)(2,1)S(1)} collective-permute-done((bf16[16,8,1472]{2,1,0:T(8,128)(2,1)}, bf16[16,8,1472]{2,1,0:T(8,128)(2,1)S(1)}, u32[]{:S(2)}, u32[]{:S(2)}) %collective-permute-start.32) | collective-permute-done | bytes 376864 | tf_op jit(solution)/shard_map/ppermute | solution.py:38
  242.2 9.9 %shard_map.192 = (bf16[1344,512]{1,0:T(8,128)(2,1)}, bf16[512,1472]{1,0:T(8,128)(2,1)}, bf16[512,1472]{1,0:T(8,128)(2,1)}, bf16[512,1472]{1,0:T(8,128)(2,1)}, bf16[512,1472]{1,0:T(8,128)(2,1)}) custom-call(bf16[128,1472]{1,0:T(8,128)(2,1)} %get-tuple-element.231.refs_0_, bf16[128,1472]{1,0:T(8,128)(2,1)} %bitcast.420, bf16[128,1472]{1,0:T(8,128)(2,1)} %bitcast.424, ...), custom_call_target="tpu_custom_call" | custom-call | flops 800000000 | bytes 2500000 | tf_op jit(solution)/shard_map/pallas_call | solution.py:79
  254.6 10.7 %shard_map.193 = (bf16[1344,512]{1,0:T(8,128)(2,1)}, bf16[128,1472]{1,0:T(8,128)(2,1)}, bf16[128,1472]{1,0:T(8,128)(2,1)}, bf16[128,1472]{1,0:T(8,128)(2,1)}, bf...) custom-call(bf16[512,1472]{1,0:T(8,128)(2,1)} %get-tuple-element.239, ...), custom_call_target="tpu_custom_call" | custom-call | flops 800000000 | bytes 2500000 | tf_op jit(solution)/shard_map/pallas_call | solution.py:79
  269.9 10.1 %shard_map.194.refs_15_ = bf16[4,336,1472]{2,1,0:T(8,128)(2,1)} custom-call(bf16[512,1472]{1,0:T(8,128)(2,1)} %get-tuple-element.239.refs_0_, bf16[512,1472]{1,0:T(8,128)(2,1)} %get-tuple-element.240.refs_1_, bf16[1344,512]{1,0:T(8,128)(2,1)} %get-tuple-element.249.refs_2_, bf16[512,1472]{1,0:T(8,128)(2,1)} %bitcast.372, bf16[512,1472]{1,0:T(8,128)(2,1)} %bitcast.373, ...), custom_call_target="tpu_custom_call" | custom-call | flops 800000000 | bytes 2500000 | tf_op jit(solution)/shard_map/pallas_call | solution.py:79
  284.4 8.5 %collective-permute-done.35 = bf16[16,8,1472]{2,1,0:T(8,128)(2,1)S(1)} collective-permute-done((bf16[16,8,1472]{2,1,0:T(8,128)(2,1)S(1)}, bf16[16,8,1472]{2,1,0:T(8,128)(2,1)S(1)}, u32[]{:S(2)}, u32[]{:S(2)}) %collective-permute-start.35) | collective-permute-done | bytes 376864 | tf_op jit(solution)/shard_map/ppermute | solution.py:38
  292.9 7.0 %collective-permute-done.36 = bf16[16,8,1472]{2,1,0:T(8,128)(2,1)S(1)} collective-permute-done((bf16[16,8,1472]{2,1,0:T(8,128)(2,1)S(1)}, bf16[16,8,1472]{2,1,0:T(8,128)(2,1)S(1)}, u32[]{:S(2)}, u32[]{:S(2)}) %collective-permute-start.36) | collective-permute-done | bytes 376864 | tf_op jit(solution)/shard_map/ppermute | solution.py:38
  302.5 9.2 %shard_map.195 = (f32[128,1472]{1,0:T(8,128)}, bf16[128,1472]{1,0:T(8,128)(2,1)}, bf16[1152,128]{1,0:T(8,128)(2,1)}, f32[128,1472]{1,0:T(8,128)}, bf16[128,1472]...) custom-call(bf16[128,1472]{1,0:T(8,128)(2,1)} %get-tuple-element.243.refs_0_, bf16[128,1472]{1,0:T(8,128)(2,1)} %bitcast.419, ...), custom_call_target="tpu_custom_call" | custom-call | flops 800000000 | bytes 2500000 | tf_op jit(solution)/shard_map/pallas_call | solution.py:79
  323.9 6.8 %collective-permute-done.42 = bf16[16,8,1472]{2,1,0:T(8,128)(2,1)S(1)} collective-permute-done((bf16[16,8,1472]{2,1,0:T(8,128)(2,1)}, bf16[16,8,1472]{2,1,0:T(8,128)(2,1)S(1)}, u32[]{:S(2)}, u32[]{:S(2)}) %collective-permute-start.42) | collective-permute-done | bytes 376864 | tf_op jit(solution)/shard_map/ppermute | solution.py:38
  331.7 11.2 %shard_map.198 = (bf16[896,512]{1,0:T(8,128)(2,1)}, bf16[896,512]{1,0:T(8,128)(2,1)}, bf16[512,1472]{1,0:T(8,128)(2,1)}, bf16[128,1472]{1,0:T(8,128)(2,1)}, bf16...) custom-call(bf16[128,1472]{1,0:T(8,128)(2,1)} %get-tuple-element.252.refs_0_, ...), custom_call_target="tpu_custom_call" | custom-call | flops 800000000 | bytes 2500000 | tf_op jit(solution)/shard_map/pallas_call | solution.py:79
  350.0 10.1 %shard_map.199.refs_9_ = bf16[4,336,1472]{2,1,0:T(8,128)(2,1)} custom-call(bf16[512,1472]{1,0:T(8,128)(2,1)} %get-tuple-element.209.refs_0_, bf16[512,1472]{1,0:T(8,128)(2,1)} %get-tuple-element.272.refs_1_, bf16[896,512]{1,0:T(8,128)(2,1)} %get-tuple-element.273.refs_2_, bf16[448,512]{1,0:T(8,128)(2,1)} %get-tuple-element.274.refs_3_, ...), custom_call_target="tpu_custom_call" | custom-call | flops 800000000 | bytes 2500000 | tf_op jit(solution)/shard_map/pallas_call | solution.py:79
  366.0 6.8 %collective-permute-done.44 = bf16[16,8,1472]{2,1,0:T(8,128)(2,1)S(1)} collective-permute-done((bf16[16,8,1472]{2,1,0:T(8,128)(2,1)}, bf16[16,8,1472]{2,1,0:T(8,128)(2,1)S(1)}, u32[]{:S(2)}, u32[]{:S(2)}) %collective-permute-start.44) | collective-permute-done | bytes 376864 | tf_op jit(solution)/shard_map/ppermute | solution.py:38
  372.8 9.0 %collective-permute-done.45 = bf16[16,8,1472]{2,1,0:T(8,128)(2,1)S(1)} collective-permute-done((bf16[16,8,1472]{2,1,0:T(8,128)(2,1)S(1)}, bf16[16,8,1472]{2,1,0:T(8,128)(2,1)S(1)}, u32[]{:S(2)}, u32[]{:S(2)}) %collective-permute-start.45) | collective-permute-done | bytes 376864 | tf_op jit(solution)/shard_map/ppermute | solution.py:38
  394.9 8.7 %shard_map.201 = (f32[256,1472]{1,0:T(8,128)}, bf16[256,1472]{1,0:T(8,128)(2,1)}, bf16[1152,256]{1,0:T(8,128)(2,1)}) custom-call(s32[1]{0:T(128)} %bitcast.38.refs_0_.refs_4_.refs_12_, f32[128,1472]{1,0:T(8,128)} %get-tuple-element.278.refs_1_, f32[128,1472]{1,0:T(8,128)} %bitcast.390, bf16[384,1472]{1,0:T(8,128)(2,1)} %bitcast.344, ...), custom_call_target="tpu_custom_call" | custom-call | flops 800000000 | bytes 2500000 | tf_op jit(solution)/shard_map/pallas_call | solution.py:79
  404.2 12.6 %collective-permute-done.54 = bf16[4,48,1472]{2,1,0:T(8,128)(2,1)} collective-permute-done((bf16[4,48,1472]{2,1,0:T(8,128)(2,1)}, bf16[4,48,1472]{2,1,0:T(8,128)(2,1)}, u32[]{:S(2)}, u32[]{:S(2)}) %collective-permute-start.54) | collective-permute-done | bytes 565280 | tf_op jit(solution)/shard_map/ppermute | solution.py:38
  434.2 9.8 %shard_map.202 = bf16[448,1472]{1,0:T(8,128)(2,1)} custom-call(bf16[288,256]{1,0:T(8,128)(2,1)} %bitcast.382, bf16[288,256]{1,0:T(8,128)(2,1)} %bitcast.394, bf16[288,256]{1,0:T(8,128)(2,1)} %bitcast.396, bf16[288,256]{1,0:T(8,128)(2,1)} %bitcast.398, s32[1,256]{1,0:T(1,128)} %bitcast.442, s32[1,256]{1,0:T(1,128)} %copy-done.61, s32[1,256]{1,0:T(1,128)} %copy-done.62, ...), custom_call_target="tpu_custom_call" | custom-call | flops 800000000 | bytes 2500000 | tf_op jit(solution)/shard_map/pallas_call | solution.py:79
  454.3 6.3 %collective-permute-done.60 = bf16[14,8,1472]{2,1,0:T(8,128)(2,1)S(1)} collective-permute-done((bf16[14,8,1472]{2,1,0:T(8,128)(2,1)S(1)}, bf16[14,8,1472]{2,1,0:T(8,128)(2,1)S(1)}, u32[]{:S(2)}, u32[]{:S(2)}) %collective-permute-start.60) | collective-permute-done | bytes 329760 | tf_op jit(solution)/shard_map/ppermute | solution.py:38
  463.4 6.8 %collective-permute-done.66 = bf16[7,8,1472]{2,1,0:T(8,128)(2,1)S(1)} collective-permute-done((bf16[7,8,1472]{2,1,0:T(8,128)(2,1)S(1)}, bf16[7,8,1472]{2,1,0:T(8,128)(2,1)S(1)}, u32[]{:S(2)}, u32[]{:S(2)}) %collective-permute-start.66) | collective-permute-done | bytes 164896 | tf_op jit(solution)/shard_map/ppermute | solution.py:38
  484.2 6.7 %collective-permute-start.76 = (bf16[28,8,1472]{2,1,0:T(8,128)(2,1)}, bf16[28,8,1472]{2,1,0:T(8,128)(2,1)}, u32[]{:S(2)}, u32[]{:S(2)}) collective-permute-start(bf16[28,8,1472]{2,1,0:T(8,128)(2,1)} %maximum_bitcast_fusion.1), channel_id=1, source_target_pairs={{0,0},{16,1},{1,2},{17,3},{2,4},{18,5},{3,6},{19,7},{8,8},{24,9},{... | collective-permute-start | bytes 1978376 | tf_op jit(solution)/shard_map/ppermute | solution.py:38
  496.5 18.5 %collective-permute-done.69 = bf16[14,8,1472]{2,1,0:T(8,128)(2,1)S(1)} collective-permute-done((bf16[14,8,1472]{2,1,0:T(8,128)(2,1)S(1)}, bf16[14,8,1472]{2,1,0:T(8,128)(2,1)S(1)}, u32[]{:S(2)}, u32[]{:S(2)}) %collective-permute-start.69) | collective-permute-done | bytes 329760 | tf_op jit(solution)/shard_map/ppermute | solution.py:38
  (400 shorter events, 239.7 us)
Async XLA Ops:
  7.2 62.9 %all-gather.9.cloned.1.call-start = ((), (), s32[]{:S(2)}) async-start(), calls=%async_computation.7 | async-start | bytes 2211840 | tf_op jit(solution)/shard_map/all_gather | solution.py:503
  12.8 22.9 %collective-permute-start.4 = (bf16[32,8,1472]{2,1,0:T(8,128)(2,1)}, bf16[32,8,1472]{2,1,0:T(8,128)(2,1)S(1)}, u32[]{:S(2)}, u32[]{:S(2)}) collective-permute-start(bf16[32,8,1472]{2,1,0:T(8,128)(2,1)} %fusion.44), channel_id=1, source_target_pairs={{0,1},{1,0},{2,3},{3,2},{4,5},{5,4},{6,7},{7,6},{8,9},{9,8},{10,11... | collective-permute-start | bytes 2261000 | tf_op jit(solution)/shard_map/ppermute | solution.py:38
  15.8 50.0 %collective-permute-start.5 = (bf16[32,8,1472]{2,1,0:T(8,128)(2,1)}, bf16[32,8,1472]{2,1,0:T(8,128)(2,1)}, u32[]{:S(2)}, u32[]{:S(2)}) collective-permute-start(bf16[32,8,1472]{2,1,0:T(8,128)(2,1)} %fusion.44), channel_id=1, source_target_pairs={{0,2},{1,3},{2,0},{3,1},{4,6},{5,7},{6,4},{7,5},{8,10},{9,11},{10,... | collective-permute-start | bytes 2261000 | tf_op jit(solution)/shard_map/ppermute | solution.py:38
  17.3 48.4 %collective-permute-start.6 = (bf16[32,8,1472]{2,1,0:T(8,128)(2,1)}, bf16[32,8,1472]{2,1,0:T(8,128)(2,1)}, u32[]{:S(2)}, u32[]{:S(2)}) collective-permute-start(bf16[32,8,1472]{2,1,0:T(8,128)(2,1)} %fusion.44), channel_id=1, source_target_pairs={{0,3},{1,2},{2,1},{3,0},{4,7},{5,6},{6,5},{7,4},{8,11},{9,10},{10,... | collective-permute-start | bytes 2261000 | tf_op jit(solution)/shard_map/ppermute | solution.py:38
  18.1 135.6 %all-gather.7.cloned.1.call-start = ((), (), s32[]{:S(2)}) async-start(), calls=%async_computation.6 | async-start | bytes 5160960 | tf_op jit(solution)/shard_map/all_gather | solution.py:548
  23.1 42.6 %collective-permute-start.3 = (bf16[28,8,1472]{2,1,0:T(8,128)(2,1)}, bf16[28,8,1472]{2,1,0:T(8,128)(2,1)}, u32[]{:S(2)}, u32[]{:S(2)}) collective-permute-start(bf16[28,8,1472]{2,1,0:T(8,128)(2,1)} %maximum_bitcast_fusion), channel_id=1, source_target_pairs={{0,0},{1,16},{2,1},{3,17},{4,2},{5,18},{6,3},{7,19},{8,8},{9,24},{... | collective-permute-start | bytes 1978376 | tf_op jit(solution)/shard_map/ppermute | solution.py:38
  68.4 165.1 %all-gather.11.cloned.1.call-start = ((), (), s32[]{:S(2)}) async-start(), calls=%async_computation.8 | async-start | bytes 5160960 | tf_op jit(solution)/shard_map/all_gather | solution.py:549
  84.5 31.8 %collective-permute-start = (bf16[131,1472]{1,0:T(8,128)(2,1)}, bf16[131,1472]{1,0:T(8,128)(2,1)S(1)}, u32[]{:S(2)}, u32[]{:S(2)}) collective-permute-start(bf16[131,1472]{1,0:T(8,128)(2,1)} %pad_maximum_fusion.6), channel_id=1, source_target_pairs={{0,16},{16,0},{1,17},{17,1},{2,18},{18,2},{3,19},{19,3},{4,20},{20... | collective-permute-start | bytes 1157000 | tf_op jit(solution)/shard_map/ppermute | solution.py:38
  122.9 19.5 %collective-permute-start.18 = (bf16[16,8,1472]{2,1,0:T(8,128)(2,1)}, bf16[16,8,1472]{2,1,0:T(8,128)(2,1)S(1)}, u32[]{:S(2)}, u32[]{:S(2)}) collective-permute-start(bf16[16,8,1472]{2,1,0:T(8,128)(2,1)} %bitcast.407), channel_id=1, source_target_pairs={{0,2},{1,3},{2,0},{3,1},{4,6},{5,7},{6,4},{7,5},{8,10},{9,11},{10,... | collective-permute-start | bytes 1130504 | tf_op jit(solution)/shard_map/ppermute | solution.py:38
  126.3 233.8 %reduce-scatter.4.cloned.1.call-start = ((), (), s32[]{:S(2)}) async-start(), calls=%async_computation.3 | async-start | bytes 5160960 | tf_op jit(solution)/shard_map/reduce_scatter | solution.py:747
  145.6 24.5 %collective-permute-start.21 = (bf16[4,48,1472]{2,1,0:T(8,128)(2,1)S(1)}, bf16[4,48,1472]{2,1,0:T(8,128)(2,1)S(1)}, u32[]{:S(2)}, u32[]{:S(2)}) collective-permute-start(bf16[4,48,1472]{2,1,0:T(8,128)(2,1)S(1)} %slice.90), channel_id=1, source_target_pairs={{0,2},{1,3},{2,0},{3,1},{4,6},{5,7},{6,4},{7,5},{8,10},{9,11},{10,... | collective-permute-start | bytes 1695752 | tf_op jit(solution)/shard_map/ppermute | solution.py:38
  146.0 26.0 %collective-permute-start.22 = (bf16[4,48,1472]{2,1,0:T(8,128)(2,1)S(1)}, bf16[4,48,1472]{2,1,0:T(8,128)(2,1)S(1)}, u32[]{:S(2)}, u32[]{:S(2)}) collective-permute-start(bf16[4,48,1472]{2,1,0:T(8,128)(2,1)S(1)} %slice.90), channel_id=1, source_target_pairs={{0,3},{1,2},{2,1},{3,0},{4,7},{5,6},{6,5},{7,4},{8,11},{9,10},{10,... | collective-permute-start | bytes 1695752 | tf_op jit(solution)/shard_map/ppermute | solution.py:38
  153.7 23.2 %collective-permute-start.23 = (bf16[4,336,1472]{2,1,0:T(8,128)(2,1)}, bf16[4,336,1472]{2,1,0:T(8,128)(2,1)S(1)}, u32[]{:S(2)}, u32[]{:S(2)}) collective-permute-start(bf16[4,336,1472]{2,1,0:T(8,128)(2,1)} %bitcast.330), channel_id=1, source_target_pairs={{0,16},{16,0},{1,17},{17,1},{2,18},{18,2},{3,19},{19,3},{4,20},{20... | collective-permute-start | bytes 11870216 | tf_op jit(solution)/shard_map/ppermute | solution.py:38
  172.5 24.0 %collective-permute-start.30 = (bf16[96,8,1472]{2,1,0:T(8,128)(2,1)S(1)}, bf16[96,8,1472]{2,1,0:T(8,128)(2,1)}, u32[]{:S(2)}, u32[]{:S(2)}) collective-permute-start(bf16[96,8,1472]{2,1,0:T(8,128)(2,1)S(1)} %bitcast.346), channel_id=1, source_target_pairs={{0,16},{16,0},{1,17},{17,1},{2,18},{18,2},{3,19},{19,3},{4,20},{20... | collective-permute-start | bytes 6782984 | tf_op jit(solution)/shard_map/ppermute | solution.py:38
  173.3 19.6 %collective-permute-start.25 = (bf16[16,8,1472]{2,1,0:T(8,128)(2,1)S(1)}, bf16[16,8,1472]{2,1,0:T(8,128)(2,1)S(1)}, u32[]{:S(2)}, u32[]{:S(2)}) collective-permute-start(bf16[16,8,1472]{2,1,0:T(8,128)(2,1)S(1)} %bitcast.360), channel_id=1, source_target_pairs={{0,2},{1,3},{2,0},{3,1},{4,6},{5,7},{6,4},{7,5},{8,10},{9,11},{10,... | collective-permute-start | bytes 1130504 | tf_op jit(solution)/shard_map/ppermute | solution.py:38
  194.3 19.1 %collective-permute-start.28 = (bf16[16,8,1472]{2,1,0:T(8,128)(2,1)}, bf16[16,8,1472]{2,1,0:T(8,128)(2,1)S(1)}, u32[]{:S(2)}, u32[]{:S(2)}) collective-permute-start(bf16[16,8,1472]{2,1,0:T(8,128)(2,1)} %bitcast.460), channel_id=1, source_target_pairs={{0,2},{1,3},{2,0},{3,1},{4,6},{5,7},{6,4},{7,5},{8,10},{9,11},{10,... | collective-permute-start | bytes 1130504 | tf_op jit(solution)/shard_map/ppermute | solution.py:38
  280.0 181.8 %reduce-scatter.6.cloned.1.call-start = ((), (), s32[]{:S(2)}) async-start(), calls=%async_computation.4 | async-start | bytes 5160960 | tf_op jit(solution)/shard_map/reduce_scatter | solution.py:749
  315.2 28.3 %collective-permute-start.47 = (bf16[64,8,1472]{2,1,0:T(8,128)(2,1)S(1)}, bf16[64,8,1472]{2,1,0:T(8,128)(2,1)S(1)}, u32[]{:S(2)}, u32[]{:S(2)}) collective-permute-start(bf16[64,8,1472]{2,1,0:T(8,128)(2,1)S(1)} %bitcast.349), channel_id=1, source_target_pairs={{0,16},{16,0},{1,17},{17,1},{2,18},{18,2},{3,19},{19,3},{4,20},{20... | collective-permute-start | bytes 4521992 | tf_op jit(solution)/shard_map/ppermute | solution.py:38
  360.1 178.2 %reduce-scatter.8.cloned.1.call-start = ((), (), s32[]{:S(2)}) async-start(), calls=%async_computation.5 | async-start | bytes 2211840 | tf_op jit(solution)/shard_map/reduce_scatter | solution.py:812
  362.3 19.5 %collective-permute-start.45 = (bf16[16,8,1472]{2,1,0:T(8,128)(2,1)S(1)}, bf16[16,8,1472]{2,1,0:T(8,128)(2,1)S(1)}, u32[]{:S(2)}, u32[]{:S(2)}) collective-permute-start(bf16[16,8,1472]{2,1,0:T(8,128)(2,1)S(1)} %bitcast.454), channel_id=1, source_target_pairs={{0,2},{1,3},{2,0},{3,1},{4,6},{5,7},{6,4},{7,5},{8,10},{9,11},{10,... | collective-permute-start | bytes 1130504 | tf_op jit(solution)/shard_map/ppermute | solution.py:38
  362.6 19.2 %collective-permute-start.46 = (bf16[16,8,1472]{2,1,0:T(8,128)(2,1)S(1)}, bf16[16,8,1472]{2,1,0:T(8,128)(2,1)S(1)}, u32[]{:S(2)}, u32[]{:S(2)}) collective-permute-start(bf16[16,8,1472]{2,1,0:T(8,128)(2,1)S(1)} %bitcast.453), channel_id=1, source_target_pairs={{0,3},{1,2},{2,1},{3,0},{4,7},{5,6},{6,5},{7,4},{8,11},{9,10},{10,... | collective-permute-start | bytes 1130504 | tf_op jit(solution)/shard_map/ppermute | solution.py:38
  388.4 28.4 %collective-permute-start.54 = (bf16[4,48,1472]{2,1,0:T(8,128)(2,1)}, bf16[4,48,1472]{2,1,0:T(8,128)(2,1)}, u32[]{:S(2)}, u32[]{:S(2)}) collective-permute-start(bf16[4,48,1472]{2,1,0:T(8,128)(2,1)} %get-tuple-element.363), channel_id=1, source_target_pairs={{0,2},{1,3},{2,0},{3,1},{4,6},{5,7},{6,4},{7,5},{8,10},{9,11},{10,... | collective-permute-start | bytes 1695752 | tf_op jit(solution)/shard_map/ppermute | solution.py:38
  389.7 27.1 %collective-permute-start.55 = (bf16[4,48,1472]{2,1,0:T(8,128)(2,1)}, bf16[4,48,1472]{2,1,0:T(8,128)(2,1)}, u32[]{:S(2)}, u32[]{:S(2)}) collective-permute-start(bf16[4,48,1472]{2,1,0:T(8,128)(2,1)} %get-tuple-element.360), channel_id=1, source_target_pairs={{0,3},{1,2},{2,1},{3,0},{4,7},{5,6},{6,5},{7,4},{8,11},{9,10},{10,... | collective-permute-start | bytes 1695752 | tf_op jit(solution)/shard_map/ppermute | solution.py:38
  430.6 20.6 %collective-permute-start.63 = (bf16[4,24,1472]{2,1,0:T(8,128)(2,1)S(1)}, bf16[4,24,1472]{2,1,0:T(8,128)(2,1)S(1)}, u32[]{:S(2)}, u32[]{:S(2)}) collective-permute-start(bf16[4,24,1472]{2,1,0:T(8,128)(2,1)S(1)} %get-tuple-element.375), channel_id=1, source_target_pairs={{0,1},{1,0},{2,3},{3,2},{4,5},{5,4},{6,7},{7,6},{8,9},{9,8},{10,11... | collective-permute-start | bytes 847880 | tf_op jit(solution)/shard_map/ppermute | solution.py:38
  431.4 21.6 %collective-permute-start.64 = (bf16[4,24,1472]{2,1,0:T(8,128)(2,1)S(1)}, bf16[4,24,1472]{2,1,0:T(8,128)(2,1)S(1)}, u32[]{:S(2)}, u32[]{:S(2)}) collective-permute-start(bf16[4,24,1472]{2,1,0:T(8,128)(2,1)S(1)} %get-tuple-element.377), channel_id=1, source_target_pairs={{0,2},{1,3},{2,0},{3,1},{4,6},{5,7},{6,4},{7,5},{8,10},{9,11},{10,... | collective-permute-start | bytes 847880 | tf_op jit(solution)/shard_map/ppermute | solution.py:38
  432.6 20.3 %collective-permute-start.65 = (bf16[4,24,1472]{2,1,0:T(8,128)(2,1)S(1)}, bf16[4,24,1472]{2,1,0:T(8,128)(2,1)S(1)}, u32[]{:S(2)}, u32[]{:S(2)}) collective-permute-start(bf16[4,24,1472]{2,1,0:T(8,128)(2,1)S(1)} %get-tuple-element.376), channel_id=1, source_target_pairs={{0,3},{1,2},{2,1},{3,0},{4,7},{5,6},{6,5},{7,4},{8,11},{9,10},{10,... | collective-permute-start | bytes 847880 | tf_op jit(solution)/shard_map/ppermute | solution.py:38
  473.1 18.7 %collective-permute-start.72 = (bf16[16,8,1472]{2,1,0:T(8,128)(2,1)}, bf16[16,8,1472]{2,1,0:T(8,128)(2,1)}, u32[]{:S(2)}, u32[]{:S(2)}) collective-permute-start(bf16[16,8,1472]{2,1,0:T(8,128)(2,1)} %bitcast.170), channel_id=1, source_target_pairs={{0,1},{1,0},{2,3},{3,2},{4,5},{5,4},{6,7},{7,6},{8,9},{9,8},{10,11... | collective-permute-start | bytes 1130504 | tf_op jit(solution)/shard_map/ppermute | solution.py:38
  474.8 21.6 %collective-permute-start.74 = (bf16[16,8,1472]{2,1,0:T(8,128)(2,1)}, bf16[16,8,1472]{2,1,0:T(8,128)(2,1)}, u32[]{:S(2)}, u32[]{:S(2)}) collective-permute-start(bf16[16,8,1472]{2,1,0:T(8,128)(2,1)} %bitcast.174), channel_id=1, source_target_pairs={{0,3},{1,2},{2,1},{3,0},{4,7},{5,6},{6,5},{7,4},{8,11},{9,10},{10,... | collective-permute-start | bytes 1130504 | tf_op jit(solution)/shard_map/ppermute | solution.py:38
  484.2 45.3 %collective-permute-start.76 = (bf16[28,8,1472]{2,1,0:T(8,128)(2,1)}, bf16[28,8,1472]{2,1,0:T(8,128)(2,1)}, u32[]{:S(2)}, u32[]{:S(2)}) collective-permute-start(bf16[28,8,1472]{2,1,0:T(8,128)(2,1)} %maximum_bitcast_fusion.1), channel_id=1, source_target_pairs={{0,0},{16,1},{1,2},{17,3},{2,4},{18,5},{3,6},{19,7},{8,8},{24,9},{... | collective-permute-start | bytes 1978376 | tf_op jit(solution)/shard_map/ppermute | solution.py:38
  491.8 23.2 %collective-permute-start.69 = (bf16[14,8,1472]{2,1,0:T(8,128)(2,1)S(1)}, bf16[14,8,1472]{2,1,0:T(8,128)(2,1)S(1)}, u32[]{:S(2)}, u32[]{:S(2)}) collective-permute-start(bf16[14,8,1472]{2,1,0:T(8,128)(2,1)S(1)} %get-tuple-element.402), channel_id=1, source_target_pairs={{0,1},{1,0},{2,3},{3,2},{4,5},{5,4},{6,7},{7,6},{8,9},{9,8},{10,11... | collective-permute-start | bytes 989192 | tf_op jit(solution)/shard_map/ppermute | solution.py:38
  491.8 23.2 %collective-permute-start.70 = (bf16[14,8,1472]{2,1,0:T(8,128)(2,1)S(1)}, bf16[14,8,1472]{2,1,0:T(8,128)(2,1)S(1)}, u32[]{:S(2)}, u32[]{:S(2)}) collective-permute-start(bf16[14,8,1472]{2,1,0:T(8,128)(2,1)S(1)} %get-tuple-element.402), channel_id=1, source_target_pairs={{0,2},{1,3},{2,0},{3,1},{4,6},{5,7},{6,4},{7,5},{8,10},{9,11},{10,... | collective-permute-start | bytes 989192 | tf_op jit(solution)/shard_map/ppermute | solution.py:38
  492.8 22.1 %collective-permute-start.71 = (bf16[14,8,1472]{2,1,0:T(8,128)(2,1)S(1)}, bf16[14,8,1472]{2,1,0:T(8,128)(2,1)S(1)}, u32[]{:S(2)}, u32[]{:S(2)}) collective-permute-start(bf16[14,8,1472]{2,1,0:T(8,128)(2,1)S(1)} %get-tuple-element.402), channel_id=1, source_target_pairs={{0,3},{1,2},{2,1},{3,0},{4,7},{5,6},{6,5},{7,4},{8,11},{9,10},{10,... | collective-permute-start | bytes 989192 | tf_op jit(solution)/shard_map/ppermute | solution.py:38
  (126 other events, 1041.1 us)
Sparse Core Ops, SparseCore 0:
  18.2 48.1 all-gather.8
  68.5 85.1 all-gather.6
  155.3 78.1 all-gather.10
  280.1 75.4 reduce-scatter.3
  360.2 75.3 reduce-scatter.5
  476.7 50.3 reduce-scatter.7
